TPU v7x, 32 devices: a whole 2x2x4 slice. The times are simulated.
32 devices in a mesh: rep: 4 (over z), shard: 8 (over y, x, core).
Axes of the slice: x: 2, y: 2, z: 4, core: 2. Of those that a mesh axis runs over, the one named last changes fastest.
Arguments:
- hidden: bfloat16 [32768, 1024], P(('rep', 'shard')), may hold values from -6 to 6
- segments: int32 [32768], P(('rep', 'shard')), may hold values from 0 to 63, never falling along the last dimension, each value on 1 to 1024 neighbouring positions
- pad_mask: int32 [32768], P(('rep', 'shard')), may hold values from 0 to 1, as said below
- encoder: bfloat16 [32, 1024, 1024], P(('rep', 'shard')), may hold values from -6 to 6
- src_len: int32 [32], P(('rep', 'shard')), may hold values from 256 to 1024
- grad_out: bfloat16 [32768, 1024], P(('rep', 'shard')), may hold values from -6 to 6
- ln_gain: bfloat16 [3, 1024], P(None, 'shard'), may hold values from 0.099609375 to 1.8984375
- self_qkv: bfloat16 [1024, 3072], P('shard'), may hold values from -0.1875 to 0.1875
- self_out: bfloat16 [1024, 1024], P('shard'), may hold values from -0.375 to 0.375
- self_vec: bfloat16 [4096], P('shard'), may hold values from -3 to 3
- cross_qkv: bfloat16 [1024, 3072], P('shard'), may hold values from -0.1875 to 0.1875
- cross_out: bfloat16 [1024, 1024], P('shard'), may hold values from -0.375 to 0.375
- cross_vec: bfloat16 [4096], P('shard'), may hold values from -3 to 3
- fc_in: bfloat16 [1024, 8192], P('shard'), may hold values from -0.1875 to 0.1875
- fc_out: bfloat16 [8192, 1024], P('shard'), may hold values from -0.09375 to 0.09375
- mlp_vec: bfloat16 [10240], P('shard'), may hold values from -3 to 3
Outputs:
- output: bfloat16 [32768, 1024], P(('rep', 'shard'))
- grad_hidden: bfloat16 [32768, 1024], P(('rep', 'shard'))
- grad_encoder: bfloat16 [32, 1024, 1024], P(('rep', 'shard'))
- grad_ln_gain: float32 [3, 1024], P(None, 'shard')
- grad_self_qkv: float32 [1024, 3072], P('shard')
- grad_self_out: float32 [1024, 1024], P('shard')
- grad_self_vec: float32 [4096], P('shard')
- grad_cross_qkv: float32 [1024, 3072], P('shard')
- grad_cross_out: float32 [1024, 1024], P('shard')
- grad_cross_vec: float32 [4096], P('shard')
- grad_fc_in: float32 [1024, 8192], P('shard')
- grad_fc_out: float32 [8192, 1024], P('shard')
- grad_mlp_vec: float32 [10240], P('shard')
Inputs may be any that keep to these rules, and one draw needn't show every extreme that they name: `pad_mask`: in each sequence of 1024 tokens the real tokens (1) come first and number 1024 - 1024 // 4 or more; the rest is padding (0).
All inputs are finite; a program needn't handle non-finite values.
Results may differ from a plain program's by a relative error of at most 0.02.
Values may be sent and summed in bfloat16 or wider, within the bound.
No kernel may reach another device: no remote copies, remote signals or barrier semaphores. Data moves between devices by JAX's collectives and lax.ppermute only.
A program may use at most 384 MiB of HBM per device.

v0:
```python
import math

import jax
import jax.numpy as jnp
from jax import lax
from jax.sharding import PartitionSpec as P

HEADS = 16
HEAD_DIM = 64


EPSILON = 1e-05
MASKED = -1e30


def smooth_unit(values):
    return jax.nn.gelu(values, approximate=True)


def layer_norm(values, gain, shift):
    center = jnp.mean(values, -1, keepdims=True)
    offset = values - center
    scale_inv = lax.rsqrt(jnp.mean(offset * offset, -1, keepdims=True) + EPSILON)
    normed = offset * scale_inv
    return (normed * gain + shift, normed, scale_inv)


def norm_back(grad, normed, scale_inv, gain):
    scaled = grad * gain
    centered = (
        scaled
        - jnp.mean(scaled, -1, keepdims=True)
        - normed * jnp.mean(scaled * normed, -1, keepdims=True)
    )
    return (scale_inv * centered, jnp.sum(grad * normed, 0), jnp.sum(grad, 0))


def outer_sum(left, right):
    return lax.dot_general(
        left, right, (((0,), (0,)), ((), ())), preferred_element_type=jnp.float32
    )


def times_transpose(grad, weight):
    return lax.dot_general(
        grad, weight, (((1,), (1,)), ((), ())), preferred_element_type=jnp.float32
    )


def split_heads(values):
    return values.reshape(values.shape[0], HEADS, HEAD_DIM)


def masked_scores(query_block, key_heads, allowed):
    scores = jnp.einsum("qhd,khd->hqk", query_block, key_heads, preferred_element_type=jnp.float32)
    return jnp.where(allowed[None], scores, MASKED)


def self_mask(seg_ids, pad_ids):
    col_ids = jnp.arange(seg_ids.shape[0], dtype=jnp.int32)

    def allowed(first_row, block_rows):
        row_ids = first_row + jnp.arange(block_rows, dtype=jnp.int32)
        seg_rows = lax.dynamic_slice_in_dim(seg_ids, first_row, block_rows)
        causal = col_ids[None, :] <= row_ids[:, None]
        same_doc = seg_rows[:, None] == seg_ids[None, :]
        real_key = (pad_ids[None, :] == 1) | (col_ids[None, :] == row_ids[:, None])
        return causal & same_doc & real_key

    return allowed


def cross_mask(length, key_count):
    col_ids = jnp.arange(key_count, dtype=jnp.int32)

    def allowed(first_row, block_rows):
        return jnp.broadcast_to(col_ids[None, :] < length, (block_rows, key_count))

    return allowed


def attend_forward(query_heads, key_heads, value_heads, allowed_fn):
    row_count = query_heads.shape[0]
    block_rows = min(512, row_count)
    block_count = row_count // block_rows
    query_blocks = query_heads.reshape(block_count, block_rows, HEADS, HEAD_DIM)
    firsts = jnp.arange(block_count, dtype=jnp.int32) * block_rows

    def one_block(element):
        query_block, first_row = element
        scores = masked_scores(query_block, key_heads, allowed_fn(first_row, block_rows))
        row_max = jnp.max(scores, -1, keepdims=True)
        exp_scores = jnp.exp(scores - row_max)
        row_total = jnp.sum(exp_scores, -1, keepdims=True)
        weights_p = (exp_scores / row_total).astype(jnp.bfloat16)
        mixed = jnp.einsum(
            "hqk,khd->qhd", weights_p, value_heads, preferred_element_type=jnp.float32
        )
        return (mixed.astype(jnp.bfloat16), (row_max + jnp.log(row_total))[..., 0])

    mixed_all, log_totals = lax.map(one_block, (query_blocks, firsts))
    return (mixed_all.reshape(row_count, HEADS * HEAD_DIM), log_totals)


def attend_backward(query_heads, key_heads, value_heads, grad_heads, log_totals, allowed_fn):
    row_count = query_heads.shape[0]
    block_rows = min(512, row_count)
    block_count = row_count // block_rows
    query_blocks = query_heads.reshape(block_count, block_rows, HEADS, HEAD_DIM)
    grad_blocks = grad_heads.reshape(block_count, block_rows, HEADS, HEAD_DIM)
    firsts = jnp.arange(block_count, dtype=jnp.int32) * block_rows

    def one_block(carry, element):
        grad_keys, grad_values = carry
        query_block, grad_block, log_block, first_row = element
        scores = masked_scores(query_block, key_heads, allowed_fn(first_row, block_rows))
        weights_p = jnp.exp(scores - log_block[..., None])
        grad_weights = jnp.einsum(
            "qhd,khd->hqk", grad_block, value_heads, preferred_element_type=jnp.float32
        )
        grad_scores = (
            weights_p * (grad_weights - jnp.sum(weights_p * grad_weights, -1, keepdims=True))
        ).astype(jnp.bfloat16)
        grad_query = jnp.einsum(
            "hqk,khd->qhd", grad_scores, key_heads, preferred_element_type=jnp.float32
        )
        grad_keys = grad_keys + jnp.einsum(
            "hqk,qhd->khd", grad_scores, query_block, preferred_element_type=jnp.float32
        )
        grad_values = grad_values + jnp.einsum(
            "hqk,qhd->khd",
            weights_p.astype(jnp.bfloat16),
            grad_block,
            preferred_element_type=jnp.float32,
        )
        return ((grad_keys, grad_values), grad_query)

    zeroes = jnp.zeros(key_heads.shape, jnp.float32)
    (grad_keys, grad_values), grad_query = lax.scan(
        one_block, (zeroes, zeroes), (query_blocks, grad_blocks, log_totals, firsts)
    )
    width = HEADS * HEAD_DIM
    return (
        grad_query.reshape(row_count, width),
        grad_keys.reshape(-1, width),
        grad_values.reshape(-1, width),
    )


def fetch(matrix_first, matrix_second, gain_row, vector):
    return (
        lax.all_gather(matrix_first, "shard", axis=0, tiled=True),
        lax.all_gather(matrix_second, "shard", axis=0, tiled=True),
        lax.all_gather(gain_row, "shard", axis=0, tiled=True),
        lax.all_gather(vector, "shard", axis=0, tiled=True),
    )


def fetch_again(matrix_first, matrix_second, gain_row, vector):
    return (
        lax.all_gather(matrix_first, "shard", axis=0, tiled=True),
        lax.all_gather(matrix_second, "shard", axis=0, tiled=True),
        lax.all_gather(gain_row, "shard", axis=0, tiled=True),
        lax.all_gather(vector, "shard", axis=0, tiled=True),
    )


def reduce_block(factor, grad_first, grad_second, grad_gain, grad_vector):
    grad_first = grad_first * factor
    grad_second = grad_second * factor
    grad_gain = grad_gain * factor
    grad_vector = grad_vector * factor
    shares = (
        lax.psum_scatter(
            grad_first.astype(jnp.bfloat16), "shard", scatter_dimension=0, tiled=True
        ).astype(jnp.float32),
        lax.psum_scatter(
            grad_second.astype(jnp.bfloat16), "shard", scatter_dimension=0, tiled=True
        ).astype(jnp.float32),
        lax.psum_scatter(
            grad_gain.astype(jnp.bfloat16), "shard", scatter_dimension=0, tiled=True
        ).astype(jnp.float32),
        lax.psum_scatter(
            grad_vector.astype(jnp.bfloat16), "shard", scatter_dimension=0, tiled=True
        ).astype(jnp.float32),
    )
    return (
        lax.psum(shares[0].astype(jnp.bfloat16), "rep").astype(jnp.float32),
        lax.psum(shares[1].astype(jnp.bfloat16), "rep").astype(jnp.float32),
        lax.psum(shares[2].astype(jnp.bfloat16), "rep").astype(jnp.float32),
        lax.psum(shares[3].astype(jnp.bfloat16), "rep").astype(jnp.float32),
    )


def per_device(
    hidden,
    segments,
    pad_mask,
    encoder,
    src_len,
    grad_out,
    ln_gain,
    self_qkv,
    self_out,
    self_vec,
    cross_qkv,
    cross_out,
    cross_vec,
    fc_in,
    fc_out,
    mlp_vec,
):
    width = hidden.shape[1]
    seq_count = src_len.shape[0]
    src_rows = encoder.shape[1]
    factor = 1.0 / math.sqrt(hidden.shape[0] * lax.axis_size("rep") * lax.axis_size("shard"))
    inputs = hidden.astype(jnp.float32)
    encoded = encoder.reshape(seq_count * src_rows, width)
    qkv_one, out_one, gain_one, vec_one = fetch(self_qkv, self_out, ln_gain[0], self_vec)
    normed_one, hat_one, inv_one = layer_norm(inputs, gain_one, vec_one[:width])
    normed_one = normed_one.astype(jnp.bfloat16)
    projected = jnp.dot(normed_one, qkv_one, preferred_element_type=jnp.float32)
    query_one = ((projected[:, :width] + vec_one[width : 2 * width]) * 0.125).astype(jnp.bfloat16)
    key_one = projected[:, width : 2 * width].astype(jnp.bfloat16)
    value_one = (projected[:, 2 * width :] + vec_one[2 * width : 3 * width]).astype(jnp.bfloat16)
    mixed_parts = []
    mask_fn = self_mask(segments, pad_mask)
    self_masks = [mask_fn]
    mixed, log_totals = attend_forward(
        split_heads(query_one), split_heads(key_one), split_heads(value_one), mask_fn
    )
    mixed_parts.append(mixed)
    log_one = [log_totals]
    attended_one = mixed_parts[0]
    after_one = (
        inputs
        + jnp.dot(attended_one, out_one, preferred_element_type=jnp.float32)
        + vec_one[3 * width :]
    )
    qkv_two, out_two, gain_two, vec_two = fetch(cross_qkv, cross_out, ln_gain[1], cross_vec)
    normed_two, hat_two, inv_two = layer_norm(after_one, gain_two, vec_two[:width])
    normed_two = normed_two.astype(jnp.bfloat16)
    query_two = (
        (
            jnp.dot(normed_two, qkv_two[:, :width], preferred_element_type=jnp.float32)
            + vec_two[width : 2 * width]
        )
        * 0.125
    ).astype(jnp.bfloat16)
    kv_two = jnp.dot(encoded, qkv_two[:, width:], preferred_element_type=jnp.float32)
    key_two = kv_two[:, :width].astype(jnp.bfloat16)
    value_two = (kv_two[:, width:] + vec_two[2 * width : 3 * width]).astype(jnp.bfloat16)
    mixed_parts = []
    sequence = 0
    mask_fn = cross_mask(src_len[sequence], src_rows)
    cross_masks = [mask_fn]
    mixed, log_totals = attend_forward(
        split_heads(query_two), split_heads(key_two), split_heads(value_two), mask_fn
    )
    mixed_parts.append(mixed)
    log_two = [log_totals]
    attended_two = mixed_parts[0]
    after_two = (
        after_one
        + jnp.dot(attended_two, out_two, preferred_element_type=jnp.float32)
        + vec_two[3 * width :]
    )
    fc_first, fc_second, gain_three, vec_three = fetch(fc_in, fc_out, ln_gain[2], mlp_vec)
    normed_three, hat_three, inv_three = layer_norm(after_two, gain_three, vec_three[:width])
    normed_three = normed_three.astype(jnp.bfloat16)
    pre_act = (
        jnp.dot(normed_three, fc_first, preferred_element_type=jnp.float32) + vec_three[2 * width :]
    )
    activated = smooth_unit(pre_act).astype(jnp.bfloat16)
    output = (
        after_two
        + jnp.dot(activated, fc_second, preferred_element_type=jnp.float32)
        + vec_three[width : 2 * width]
    ).astype(jnp.bfloat16)
    mlp_weights = fetch_again(fc_in, fc_out, ln_gain[2], mlp_vec)
    grad_top = grad_out.astype(jnp.float32)
    grad_fc_second = outer_sum(activated, grad_out)
    grad_units = times_transpose(grad_out, mlp_weights[1])
    unused_value, smooth_back = jax.vjp(smooth_unit, pre_act)
    grad_pre = smooth_back(grad_units)[0].astype(jnp.bfloat16)
    grad_fc_first = outer_sum(normed_three, grad_pre)
    grad_normed_three = times_transpose(grad_pre, mlp_weights[0])
    grad_rest_two, grad_gain_three, grad_shift_three = norm_back(
        grad_normed_three, hat_three, inv_three, mlp_weights[2]
    )
    grad_after_two = grad_top + grad_rest_two
    grad_vec_three = jnp.concatenate(
        [grad_shift_three, jnp.sum(grad_top, 0), jnp.sum(grad_pre.astype(jnp.float32), 0)]
    )
    mlp_grads = reduce_block(factor, grad_fc_first, grad_fc_second, grad_gain_three, grad_vec_three)
    cross_weights = fetch_again(cross_qkv, cross_out, ln_gain[1], cross_vec)
    grad_branch_two = grad_after_two.astype(jnp.bfloat16)
    grad_out_two = outer_sum(attended_two, grad_branch_two)
    grad_attended_two = times_transpose(grad_branch_two, cross_weights[1]).astype(jnp.bfloat16)
    query_parts = []
    key_parts = []
    value_parts = []
    sequence = 0
    grad_query, grad_keys, grad_values = attend_backward(
        split_heads(query_two),
        split_heads(key_two),
        split_heads(value_two),
        split_heads(grad_attended_two),
        log_two[sequence],
        cross_masks[sequence],
    )
    query_parts.append(grad_query)
    key_parts.append(grad_keys)
    value_parts.append(grad_values)
    grad_query_two = query_parts[0].astype(jnp.bfloat16) * 0.125
    grad_key_two = key_parts[0].astype(jnp.bfloat16)
    grad_value_two = value_parts[0].astype(jnp.bfloat16)
    grad_kv_two = jnp.concatenate([grad_key_two, grad_value_two], 1)
    grad_qkv_two = jnp.concatenate(
        [outer_sum(normed_two, grad_query_two), outer_sum(encoded, grad_kv_two)], 1
    )
    grad_normed_two = times_transpose(grad_query_two, cross_weights[0][:, :width])
    grad_encoded = times_transpose(grad_kv_two, cross_weights[0][:, width:]).astype(jnp.bfloat16)
    grad_rest_one, grad_gain_two, grad_shift_two = norm_back(
        grad_normed_two, hat_two, inv_two, cross_weights[2]
    )
    grad_after_one = grad_after_two + grad_rest_one
    grad_vec_two = jnp.concatenate(
        [
            grad_shift_two,
            jnp.sum(grad_query_two.astype(jnp.float32), 0),
            jnp.sum(grad_value_two.astype(jnp.float32), 0),
            jnp.sum(grad_branch_two.astype(jnp.float32), 0),
        ]
    )
    cross_grads = reduce_block(factor, grad_qkv_two, grad_out_two, grad_gain_two, grad_vec_two)
    self_weights = fetch_again(self_qkv, self_out, ln_gain[0], self_vec)
    grad_branch_one = grad_after_one.astype(jnp.bfloat16)
    grad_out_one = outer_sum(attended_one, grad_branch_one)
    grad_attended_one = times_transpose(grad_branch_one, self_weights[1]).astype(jnp.bfloat16)
    query_parts = []
    key_parts = []
    value_parts = []
    sequence = 0
    grad_query, grad_keys, grad_values = attend_backward(
        split_heads(query_one),
        split_heads(key_one),
        split_heads(value_one),
        split_heads(grad_attended_one),
        log_one[sequence],
        self_masks[sequence],
    )
    query_parts.append(grad_query)
    key_parts.append(grad_keys)
    value_parts.append(grad_values)
    grad_query_one = query_parts[0].astype(jnp.bfloat16) * 0.125
    grad_key_one = key_parts[0].astype(jnp.bfloat16)
    grad_value_one = value_parts[0].astype(jnp.bfloat16)
    grad_projected = jnp.concatenate([grad_query_one, grad_key_one, grad_value_one], 1)
    grad_qkv_one = outer_sum(normed_one, grad_projected)
    grad_normed_one = times_transpose(grad_projected, self_weights[0])
    grad_rest_zero, grad_gain_one, grad_shift_one = norm_back(
        grad_normed_one, hat_one, inv_one, self_weights[2]
    )
    grad_hidden = (grad_after_one + grad_rest_zero).astype(jnp.bfloat16)
    grad_vec_one = jnp.concatenate(
        [
            grad_shift_one,
            jnp.sum(grad_query_one.astype(jnp.float32), 0),
            jnp.sum(grad_value_one.astype(jnp.float32), 0),
            jnp.sum(grad_branch_one.astype(jnp.float32), 0),
        ]
    )
    self_grads = reduce_block(factor, grad_qkv_one, grad_out_one, grad_gain_one, grad_vec_one)
    grad_gains = jnp.stack([self_grads[2], cross_grads[2], mlp_grads[2]], 0)
    grad_states = grad_encoded.reshape(seq_count, src_rows, width)
    return (
        output,
        grad_hidden,
        grad_states,
        grad_gains,
        self_grads[0],
        self_grads[1],
        self_grads[3],
        cross_grads[0],
        cross_grads[1],
        cross_grads[3],
        mlp_grads[0],
        mlp_grads[1],
        mlp_grads[3],
    )


def solution(mesh):
    placed = (
        P(("rep", "shard"), None),
        P(("rep", "shard")),
        P(("rep", "shard")),
        P(("rep", "shard"), None, None),
        P(("rep", "shard")),
        P(("rep", "shard"), None),
        P(None, "shard"),
        P("shard", None),
        P("shard", None),
        P("shard"),
        P("shard", None),
        P("shard", None),
        P("shard"),
        P("shard", None),
        P("shard", None),
        P("shard"),
    )
    return jax.shard_map(
        per_device,
        mesh=mesh,
        in_specs=placed,
        out_specs=(
            P(("rep", "shard"), None),
            P(("rep", "shard"), None),
            P(("rep", "shard"), None, None),
            P(None, "shard"),
            P("shard", None),
            P("shard", None),
            P("shard"),
            P("shard", None),
            P("shard", None),
            P("shard"),
            P("shard", None),
            P("shard", None),
            P("shard"),
        ),
        check_vma=False,
    )
```

profile of v0, /device:TPU:0, one launch (start us, length us, event | category | flops | bytes accessed | tf_op | source)
XLA Modules:
  0.0 1678.3 jit_solution(155705495602616525)
XLA Ops:
  11.3 10.6 all-gather.5
  116.1 108.7 %while.59 = (s32[]{:T(128)}, bf16[2,512,16,64]{1,3,2,0:T(8,128)(2,1)}, f32[2,16,512]{2,1,0:T(8,128)S(1)}, s32[2]{0:T(128)S(1)}, s32[1024]{0:T(1024)S(1)}, /*inde...) while((s32[]{:T(128)}, ...), condition=%wide.region_5.6_spmd.clone.clone, body=%wide.region_2.5_spmd.clone.clone.sunk | while | flops 2226644480 | bytes 134500624 | solution.py:101
  120.7 18.0 %select_reduce_fusion.5 = (f32[16,512]{1,0:T(8,128)S(1)}, f32[16,512,1024]{2,1,0:T(8,128)}) fusion(pred[512,1024]{1,0:T(8,128)(4,1)S(1)} %fusion.213, bf16[1024,16,64]{0,2,1:T(8,128)(2,1)} %get-tuple-element.1004, bf16[2,512,16,64]{1,3,2,0:T(8,128)(2,1)} %get-tuple-element.1003, s32[]{:T(128)S(6)} %copy.146), kind=kOutput, calls=%fused_computation.21.clone.1 | convolution fusion | flops 1090510848 | bytes 37257220 | tf_op jit(solution)/shard_map/while/body/eval_jaxpr/qhd,khd->hqk/dot_general | solution.py:55
  138.7 15.2 fusion.214
  153.9 14.6 fusion.215
  174.0 18.4 %select_reduce_fusion.5 = (f32[16,512]{1,0:T(8,128)S(1)}, f32[16,512,1024]{2,1,0:T(8,128)}) fusion(pred[512,1024]{1,0:T(8,128)(4,1)S(1)} %fusion.213, bf16[1024,16,64]{0,2,1:T(8,128)(2,1)} %get-tuple-element.1004, bf16[2,512,16,64]{1,3,2,0:T(8,128)(2,1)} %get-tuple-element.1003, s32[]{:T(128)S(6)} %copy.146), kind=kOutput, calls=%fused_computation.21.clone.1 | convolution fusion | flops 1090510848 | bytes 37257220 | tf_op jit(solution)/shard_map/while/body/eval_jaxpr/qhd,khd->hqk/dot_general | solution.py:55
  192.4 15.0 fusion.214
  207.4 16.0 fusion.215
  280.8 99.0 %while.58 = (s32[]{:T(128)}, bf16[2,512,16,64]{1,3,2,0:T(8,128)(2,1)}, f32[2,16,512]{2,1,0:T(8,128)S(1)}, s32[]{:T(128)}, bf16[2,512,16,64]{1,3,2,0:T(8,128)(2,1...) while((s32[]{:T(128)}, bf16[2,512,16,64]{1,3,2,0:T(8,128)(2,1)}, ...), condition=%wide.region_11.12_spmd.clone, body=%wide.region_8.11_spmd.clone.sunk | while | flops 2223498240 | bytes 132387000 | solution.py:101
  281.6 18.7 %select_reduce_fusion.4 = (f32[16,512]{1,0:T(8,128)S(1)}, f32[16,512,1024]{2,1,0:T(8,128)}) fusion(pred[1024]{0:T(1024)(128)(4,1)S(1)} %iota_compare_fusion.8, bf16[1024,16,64]{0,2,1:T(8,128)(2,1)} %get-tuple-element.1030, bf16[2,512,16,64]{1,3,2,0:T(8,128)(2,1)} %get-tuple-element.1029, s32[]{:T(128)S(6)} %copy.155), kind=kOutput, calls=%fused_computation.6.clone.1 | convolution fusion | flops 1090510848 | bytes 36733956 | tf_op jit(solution)/shard_map/while/body/eval_jaxpr/qhd,khd->hqk/dot_general | solution.py:55
  300.3 16.6 fusion.209
  316.9 13.6 fusion.210
  332.5 17.9 %select_reduce_fusion.4 = (f32[16,512]{1,0:T(8,128)S(1)}, f32[16,512,1024]{2,1,0:T(8,128)}) fusion(pred[1024]{0:T(1024)(128)(4,1)S(1)} %iota_compare_fusion.8, bf16[1024,16,64]{0,2,1:T(8,128)(2,1)} %get-tuple-element.1030, bf16[2,512,16,64]{1,3,2,0:T(8,128)(2,1)} %get-tuple-element.1029, s32[]{:T(128)S(6)} %copy.155), kind=kOutput, calls=%fused_computation.6.clone.1 | convolution fusion | flops 1090510848 | bytes 36733956 | tf_op jit(solution)/shard_map/while/body/eval_jaxpr/qhd,khd->hqk/dot_general | solution.py:55
  350.4 14.8 fusion.209
  365.2 13.3 fusion.210
  394.1 29.1 %fusion.134 = f32[1024,8192]{1,0:T(8,128)} fusion(bf16[1024,8192]{1,0:T(8,128)(2,1)} %all-gather.21.cloned.1.call-done, f32[1024,1024]{0,1:T(8,128)} %copy-done.13, f32[1024]{0:T(1024)S(1)} %copy-done.82, f32[1024]{0:T(1024)S(1)} %bitcast.262, f32[1024]{0:T(1024)S(1)} %add_rsqrt_fusion, f32[1024]{0:T(1024)S(1)} %broadcast_multiply_fusion.6), kind=kOutput, calls=%fused_computation.237 | convolution fusion | flops 17185112064 | bytes 54542336 | tf_op jit(solution)/shard_map/dot_general | solution.py:272
  423.2 45.0 %convert_reduce_fusion = (f32[8192]{0:T(1024)}, bf16[1024,8192]{1,0:T(8,128)(2,1)}) fusion(f32[1024,8192]{1,0:T(8,128)} %fusion.134, f32[8192]{0:T(1024)S(1)} %copy-done.72, bf16[1024,1024]{1,0:T(8,128)(2,1)} %param.29, bf16[8192,1024]{1,0:T(8,128)(2,1)} %all-gather.23.cloned.1.call-done), kind=kOutput, calls=%fused_computation.111 | convolution fusion | flops 17372798976 | bytes 69271552 | tf_op jit(solution)/shard_map/dot_general | solution.py:45
  468.3 24.9 %fusion.142 = (f32[1024]{0:T(1024)}, f32[1024,1024]{1,0:T(8,128)}) fusion(bf16[1024,8192]{1,0:T(8,128)(2,1)} %get-tuple-element.676, bf16[1024,8192]{1,0:T(8,128)(2,1)} %all-gather.21.cloned.1.call-done), kind=kOutput, calls=%fused_computation.244 | convolution fusion | flops 17180917760 | bytes 37752832 | tf_op jit(solution)/shard_map/dot_general | solution.py:45
  535.2 219.8 %while.60 = (s32[]{:T(128)}, f32[1024,16,64]{0,2,1:T(8,128)}, f32[1024,16,64]{0,2,1:T(8,128)}, bf16[2,512,16,64]{1,3,2,0:T(8,128)(2,1)}, bf16[2,512,16,64]{1,3,2...) while((s32[]{:T(128)}, f32[1024,16,64]{0,2,1:T(8,128)}, ...), condition=%wide.region_18.19_spmd.clone, body=%wide.region_16.18_spmd.clone.sunk | while | flops 5473559552 | bytes 323195104 | solution.py:139
  536.1 18.2 %fusion.225 = f32[16,512,1024]{2,1,0:T(8,128)} fusion(bf16[1024,16,64]{0,2,1:T(8,128)(2,1)} %get-tuple-element.1063, bf16[2,512,16,64]{1,3,2,0:T(8,128)(2,1)} %get-tuple-element.1061, s32[]{:T(128)S(6)} %copy.165), kind=kOutput, calls=%fused_computation.55.clone.1 | convolution fusion | flops 1073741824 | bytes 36700164 | tf_op jit(solution)/shard_map/while/body/eval_jaxpr/qhd,khd->hqk/dot_general | solution.py:55
  554.3 16.6 bitcast_add_fusion.9
  570.8 24.4 %multiply_reduce_fusion.13 = (f32[16,512]{1,0:T(8,128)S(1)}, f32[16,512,1024]{2,1,0:T(8,128)}) fusion(f32[16,512,1024]{2,1,0:T(8,128)} %fusion.225, f32[16,512]{1,0:T(8,128)S(1)} %dynamic-slice_bitcast_fusion.7, pred[1024]{0:T(1024)(128)(4,1)S(1)} %iota_compare_fusion.9, bf16[1024,16,64]{0,2,1:T(8,128)(2,1)} %get-tuple-element.1066, ...), kind=kOutput, calls=%fused_computation.41.clone.1 | convolution fusion | flops 1107288064 | bytes 70321152 | tf_op jit(solution)/shard_map/while/body/eval_jaxpr/qhd,khd->hqk/dot_general | solution.py:118
  595.3 27.8 %multiply_convert_fusion.16 = bf16[16,512,1024]{2,1,0:T(8,128)(2,1)} fusion(f32[16,512,1024]{2,1,0:T(8,128)} %get-tuple-element.957, f32[16,512,1024]{2,1,0:T(8,128)} %fusion.225, f32[16,512]{1,0:T(8,128)S(1)} %get-tuple-element.958, f32[16,512]{1,0:T(8,128)S(1)} %dynamic-slice_bitcast_fusion.7, pred[1024]{0:T(1024)(128)(4,1)S(1)} %iota_compare_fusion.9), kind=kLoop, calls=%fused_computation.40.clone.1 | loop fusion | flops 41943040 | bytes 83952640 | tf_op jit(solution)/shard_map/while/body/eval_jaxpr/convert_element_type | solution.py:123
  623.1 10.3 bitcast_dynamic-update-slice_fusion.10
  645.5 17.5 %fusion.225 = f32[16,512,1024]{2,1,0:T(8,128)} fusion(bf16[1024,16,64]{0,2,1:T(8,128)(2,1)} %get-tuple-element.1063, bf16[2,512,16,64]{1,3,2,0:T(8,128)(2,1)} %get-tuple-element.1061, s32[]{:T(128)S(6)} %copy.165), kind=kOutput, calls=%fused_computation.55.clone.1 | convolution fusion | flops 1073741824 | bytes 36700164 | tf_op jit(solution)/shard_map/while/body/eval_jaxpr/qhd,khd->hqk/dot_general | solution.py:55
  663.0 17.6 %bitcast_add_fusion.9 = f32[1024,16,64]{0,2,1:T(8,128)} fusion(f32[1024,16,64]{0,2,1:T(8,128)} %get-tuple-element.1047, f32[16,512,1024]{2,1,0:T(8,128)} %fusion.225, f32[16,512]{1,0:T(8,128)S(1)} %dynamic-slice_bitcast_fusion.7, pred[1024]{0:T(1024)(128)(4,1)S(1)} %iota_compare_fusion.9, pred[]{:T(512)S(6)} %compare.6, ...), kind=kOutput, calls=%fused_computation.48.clone.1 | convolution fusion | flops 1101004800 | bytes 43025412 | tf_op jit(solution)/shard_map/while/body/eval_jaxpr/hqk,qhd->khd/dot_general | solution.py:130
  680.7 24.4 %multiply_reduce_fusion.13 = (f32[16,512]{1,0:T(8,128)S(1)}, f32[16,512,1024]{2,1,0:T(8,128)}) fusion(f32[16,512,1024]{2,1,0:T(8,128)} %fusion.225, f32[16,512]{1,0:T(8,128)S(1)} %dynamic-slice_bitcast_fusion.7, pred[1024]{0:T(1024)(128)(4,1)S(1)} %iota_compare_fusion.9, bf16[1024,16,64]{0,2,1:T(8,128)(2,1)} %get-tuple-element.1066, ...), kind=kOutput, calls=%fused_computation.41.clone.1 | convolution fusion | flops 1107288064 | bytes 70321152 | tf_op jit(solution)/shard_map/while/body/eval_jaxpr/qhd,khd->hqk/dot_general | solution.py:118
  705.1 27.8 %multiply_convert_fusion.16 = bf16[16,512,1024]{2,1,0:T(8,128)(2,1)} fusion(f32[16,512,1024]{2,1,0:T(8,128)} %get-tuple-element.957, f32[16,512,1024]{2,1,0:T(8,128)} %fusion.225, f32[16,512]{1,0:T(8,128)S(1)} %get-tuple-element.958, f32[16,512]{1,0:T(8,128)S(1)} %dynamic-slice_bitcast_fusion.7, pred[1024]{0:T(1024)(128)(4,1)S(1)} %iota_compare_fusion.9), kind=kLoop, calls=%fused_computation.40.clone.1 | loop fusion | flops 41943040 | bytes 83952640 | tf_op jit(solution)/shard_map/while/body/eval_jaxpr/convert_element_type | solution.py:123
  809.5 229.8 %while.61 = (s32[]{:T(128)}, f32[1024,16,64]{0,2,1:T(8,128)}, f32[1024,16,64]{0,2,1:T(8,128)}, bf16[2,512,16,64]{1,3,2,0:T(8,128)(2,1)}, bf16[2,512,16,64]{1,3,2...) while((s32[]{:T(128)}, f32[1024,16,64]{0,2,1:T(8,128)}, ...), condition=%wide.region_23.24_spmd.clone.clone, body=%wide.region_21.23_spmd.clone.clone.sunk | while | flops 5476705792 | bytes 325308736 | solution.py:139
  813.8 18.1 %fusion.235 = f32[16,512,1024]{2,1,0:T(8,128)} fusion(bf16[1024,16,64]{0,2,1:T(8,128)(2,1)} %get-tuple-element.1107, bf16[2,512,16,64]{1,3,2,0:T(8,128)(2,1)} %get-tuple-element.1103, s32[]{:T(128)S(6)} %copy.177), kind=kOutput, calls=%fused_computation.88.clone.1 | convolution fusion | flops 1073741824 | bytes 36700164 | tf_op jit(solution)/shard_map/while/body/eval_jaxpr/qhd,khd->hqk/dot_general | solution.py:55
  831.9 17.3 %bitcast_add_fusion.11 = f32[1024,16,64]{0,2,1:T(8,128)} fusion(f32[1024,16,64]{0,2,1:T(8,128)} %get-tuple-element.1086, f32[16,512,1024]{2,1,0:T(8,128)} %fusion.235, f32[16,512]{1,0:T(8,128)S(1)} %dynamic-slice_bitcast_fusion.8, pred[512,1024]{1,0:T(8,128)(4,1)S(1)} %fusion.236, pred[]{:T(512)S(6)} %compare.7, ...), kind=kOutput, calls=%fused_computation.76.clone.1 | convolution fusion | flops 1101004800 | bytes 43548676 | tf_op jit(solution)/shard_map/while/body/eval_jaxpr/hqk,qhd->khd/dot_general | solution.py:130
  849.2 25.3 %multiply_reduce_fusion.14 = (f32[16,512]{1,0:T(8,128)S(1)}, f32[16,512,1024]{2,1,0:T(8,128)}) fusion(f32[16,512,1024]{2,1,0:T(8,128)} %fusion.235, f32[16,512]{1,0:T(8,128)S(1)} %dynamic-slice_bitcast_fusion.8, pred[512,1024]{1,0:T(8,128)(4,1)S(1)} %fusion.236, bf16[1024,16,64]{0,2,1:T(8,128)(2,1)} %get-tuple-element.1110, ...), kind=kOutput, calls=%fused_computation.69.clone.1 | convolution fusion | flops 1107288064 | bytes 70844416 | tf_op jit(solution)/shard_map/while/body/eval_jaxpr/qhd,khd->hqk/dot_general | solution.py:118
  874.6 27.8 %multiply_convert_fusion.17 = bf16[16,512,1024]{2,1,0:T(8,128)(2,1)} fusion(f32[16,512,1024]{2,1,0:T(8,128)} %get-tuple-element.971, f32[16,512,1024]{2,1,0:T(8,128)} %fusion.235, f32[16,512]{1,0:T(8,128)S(1)} %get-tuple-element.972, f32[16,512]{1,0:T(8,128)S(1)} %dynamic-slice_bitcast_fusion.8, pred[512,1024]{1,0:T(8,128)(4,1)S(1)} %fusion.236), kind=kLoop, calls=%fused_computation.68.clone.1 | loop fusion | flops 41943040 | bytes 84475904 | tf_op jit(solution)/shard_map/while/body/eval_jaxpr/convert_element_type | solution.py:123
  928.2 17.5 %fusion.235 = f32[16,512,1024]{2,1,0:T(8,128)} fusion(bf16[1024,16,64]{0,2,1:T(8,128)(2,1)} %get-tuple-element.1107, bf16[2,512,16,64]{1,3,2,0:T(8,128)(2,1)} %get-tuple-element.1103, s32[]{:T(128)S(6)} %copy.177), kind=kOutput, calls=%fused_computation.88.clone.1 | convolution fusion | flops 1073741824 | bytes 36700164 | tf_op jit(solution)/shard_map/while/body/eval_jaxpr/qhd,khd->hqk/dot_general | solution.py:55
  945.8 18.3 %bitcast_add_fusion.11 = f32[1024,16,64]{0,2,1:T(8,128)} fusion(f32[1024,16,64]{0,2,1:T(8,128)} %get-tuple-element.1086, f32[16,512,1024]{2,1,0:T(8,128)} %fusion.235, f32[16,512]{1,0:T(8,128)S(1)} %dynamic-slice_bitcast_fusion.8, pred[512,1024]{1,0:T(8,128)(4,1)S(1)} %fusion.236, pred[]{:T(512)S(6)} %compare.7, ...), kind=kOutput, calls=%fused_computation.76.clone.1 | convolution fusion | flops 1101004800 | bytes 43548676 | tf_op jit(solution)/shard_map/while/body/eval_jaxpr/hqk,qhd->khd/dot_general | solution.py:130
  964.1 25.3 %multiply_reduce_fusion.14 = (f32[16,512]{1,0:T(8,128)S(1)}, f32[16,512,1024]{2,1,0:T(8,128)}) fusion(f32[16,512,1024]{2,1,0:T(8,128)} %fusion.235, f32[16,512]{1,0:T(8,128)S(1)} %dynamic-slice_bitcast_fusion.8, pred[512,1024]{1,0:T(8,128)(4,1)S(1)} %fusion.236, bf16[1024,16,64]{0,2,1:T(8,128)(2,1)} %get-tuple-element.1110, ...), kind=kOutput, calls=%fused_computation.69.clone.1 | convolution fusion | flops 1107288064 | bytes 70844416 | tf_op jit(solution)/shard_map/while/body/eval_jaxpr/qhd,khd->hqk/dot_general | solution.py:118
  989.4 27.8 %multiply_convert_fusion.17 = bf16[16,512,1024]{2,1,0:T(8,128)(2,1)} fusion(f32[16,512,1024]{2,1,0:T(8,128)} %get-tuple-element.971, f32[16,512,1024]{2,1,0:T(8,128)} %fusion.235, f32[16,512]{1,0:T(8,128)S(1)} %get-tuple-element.972, f32[16,512]{1,0:T(8,128)S(1)} %dynamic-slice_bitcast_fusion.8, pred[512,1024]{1,0:T(8,128)(4,1)S(1)} %fusion.236), kind=kLoop, calls=%fused_computation.68.clone.1 | loop fusion | flops 41943040 | bytes 84475904 | tf_op jit(solution)/shard_map/while/body/eval_jaxpr/convert_element_type | solution.py:123
  1051.2 12.9 multiply_convert_fusion.5
  1093.4 35.2 %multiply_convert_fusion.2 = bf16[8192,1024]{1,0:T(8,128)(2,1)} fusion(bf16[1024,1024]{1,0:T(8,128)(2,1)} %param.29, f32[1024,8192]{1,0:T(8,128)} %fusion.134, f32[8192]{0:T(1024)S(1)} %copy-done.73), kind=kOutput, calls=%fused_computation.112 | convolution fusion | flops 17280532480 | bytes 52461568 | tf_op jit(solution)/shard_map/dot_general | solution.py:39
  1129.3 27.6 %multiply_convert_fusion.3 = bf16[1024,8192]{1,0:T(8,128)(2,1)} fusion(bf16[1024,8192]{1,0:T(8,128)(2,1)} %get-tuple-element.676, f32[1024,1024]{0,1:T(8,128)} %copy-done.13, f32[1024]{0:T(1024)S(1)} %copy-done.83, f32[1024]{0:T(1024)S(1)} %bitcast.265, f32[1024]{0:T(1024)S(1)} %copy-done.61, f32[1024]{0:T(1024)S(1)} %copy-done.48), kind=kOutput, calls=%fused_computation.113 | convolution fusion | flops 17201889280 | bytes 37765120 | tf_op jit(solution)/shard_map/dot_general | solution.py:39
  1160.2 32.2 %reduce-scatter.11.cloned.1.call-done = bf16[128,3072]{1,0:T(8,128)(2,1)} async-done(((bf16[1024,3072]{1,0:T(8,128)(2,1)}), bf16[128,3072]{1,0:T(8,128)(2,1)}) %reduce-scatter.11.cloned.1.call-update) | async-done | bytes 786448 | tf_op jit(solution)/shard_map/reduce_scatter | solution.py:174
  1192.4 119.5 %reduce-scatter.17.cloned.1.call-done = bf16[1024,1024]{1,0:T(8,128)(2,1)} async-done(((bf16[8192,1024]{1,0:T(8,128)(2,1)}), bf16[1024,1024]{1,0:T(8,128)(2,1)}) %reduce-scatter.17.cloned.1.call-update) | async-done | bytes 2097168 | tf_op jit(solution)/shard_map/reduce_scatter | solution.py:177
  1311.9 119.4 %reduce-scatter.15.cloned.1.call-done = bf16[128,8192]{1,0:T(8,128)(2,1)} async-done(((bf16[1024,8192]{1,0:T(8,128)(2,1)}), bf16[128,8192]{1,0:T(8,128)(2,1)}) %reduce-scatter.15.cloned.1.call-update) | async-done | bytes 2097168 | tf_op jit(solution)/shard_map/reduce_scatter | solution.py:174
  1431.3 27.6 %add_convert_fusion = bf16[1024,1024]{0,1:T(8,128)(2,1)} fusion(f32[1024,1024]{0,1:T(8,128)} %copy-done.13, bf16[8192,1024]{1,0:T(8,128)(2,1)} %all-gather.23.cloned.1.call-done, f32[1024]{0:T(1024)S(1)} %copy-done.81, f32[1024,8192]{1,0:T(8,128)} %fusion.134, f32[8192]{0:T(1024)S(1)} %copy-done.73), kind=kOutput, calls=%fused_computation.164 | convolution fusion | flops 17266900992 | bytes 56659968 | tf_op jit(solution)/shard_map/dot_general | solution.py:277
  1463.2 12.0 fusion.140
  1484.6 25.0 %all-reduce.6 = (bf16[1024]{0:T(1024)(128)(2,1)S(1)}, bf16[1024]{0:T(1024)(128)(2,1)S(1)}, bf16[1024]{0:T(1024)(128)(2,1)S(1)}, bf16[4096]{0:T(1024)(128)(2,1)S(...) all-reduce(bf16[1024]{0:T(1024)(128)(2,1)S(1)} %copy-done.80, ...), channel_id=7, replica_groups=mesh['rep'=4,'shard'=8] {'shard'}, use_global_device_ids=true, to_apply=%region_33.34.clone | all-reduce | flops 21504 | bytes 86016
  1510.0 13.5 all-reduce.7
  1546.0 113.3 %all-reduce.11.cloned.1.call-done = (bf16[128,3072]{1,0:T(8,128)(2,1)}, bf16[128,1024]{1,0:T(8,128)(2,1)}, bf16[128,3072]{1,0:T(8,128)(2,1)}, bf16[128,1024]{1,0...) async-done(((bf16[128,3072]{1,0:T(8,128)(2,1)}, bf16[128,1024]{1,0:T(8,128)(2,1)}, bf16[128,3072]{1,0:T(8,128)(2,1)}, bf16[128,1024]{1,0:T(8,128)(2,1)}, ...) | async-done | bytes 6291472 | tf_op jit(solution)/shard_map/psum | solution.py:188
  (428 shorter events, 449.4 us)
Async XLA Ops:
  7.2 217.6 %copy-start = (bf16[1,1024,1024]{2,1,0:T(8,128)(2,1)S(1)}, bf16[1,1024,1024]{2,1,0:T(8,128)(2,1)}, u32[]{:S(2)}) copy-start(bf16[1,1024,1024]{2,1,0:T(8,128)(2,1)} %param.27) | copy-start | bytes 6291460
  7.2 16.0 copy-start.94
  7.2 16.0 copy-start.95
  7.2 16.1 copy-start.96
  7.2 72.6 %all-gather.13.cloned.1.call-start = ((), (), s32[]{:S(2)}) async-start(), calls=%async_computation.6 | async-start | bytes 7077888 | tf_op jit(solution)/shard_map/all_gather | solution.py:152
  8.0 216.8 %all-gather.17.cloned.1.call-start = ((), (), s32[]{:S(2)}) async-start(), calls=%async_computation.8 | async-start | bytes 7077888 | tf_op jit(solution)/shard_map/all_gather | solution.py:152
  8.7 245.1 %all-gather.15.cloned.1.call-start = ((), (), s32[]{:S(2)}) async-start(), calls=%async_computation.7 | async-start | bytes 2359296 | tf_op jit(solution)/shard_map/all_gather | solution.py:153
  9.5 376.1 %all-gather.19.cloned.1.call-start = ((), (), s32[]{:S(2)}) async-start(), calls=%async_computation.9 | async-start | bytes 2359296 | tf_op jit(solution)/shard_map/all_gather | solution.py:153
  10.0 384.1 %all-gather.21.cloned.1.call-start = ((), (), s32[]{:S(2)}) async-start(), calls=%async_computation.10 | async-start | bytes 18874368 | tf_op jit(solution)/shard_map/all_gather | solution.py:152
  10.6 412.6 %all-gather.23.cloned.1.call-start = ((), (), s32[]{:S(2)}) async-start(), calls=%async_computation.11 | async-start | bytes 18874368 | tf_op jit(solution)/shard_map/all_gather | solution.py:153
  11.2 1148.9 %reduce-scatter.13.cloned.1.call-start = ((), (), s32[]{:S(2)}) async-start(), calls=%async_computation.15 | async-start | bytes 2359296 | tf_op jit(solution)/shard_map/reduce_scatter | solution.py:177
  40.4 39.4 %copy-start.62 = (f32[1,1024]{1,0:T(1,128)}, f32[1,1024]{1,0:T(1,128)S(1)}, u32[]{:S(2)}) copy-start(f32[1,1024]{1,0:T(1,128)S(1)} %convert_element_type.357) | copy-start | bytes 12292
  67.7 12.1 copy-start.88
  73.6 16.2 copy-start.49
  75.9 14.0 copy-start.65
  109.1 7.0 copy-start.35
  109.1 7.0 copy-start.42
  138.7 15.2 copy-start.7
  138.7 15.2 copy-start.24
  192.4 15.0 copy-start.7
  192.4 15.0 copy-start.24
  300.3 16.6 copy-start.9
  300.3 16.6 copy-start.22
  350.4 14.8 copy-start.9
  350.4 14.8 copy-start.22
  391.6 112.2 %copy-start.47 = (f32[1024]{0:T(1024)}, f32[1024]{0:T(1024)S(1)}, u32[]{:S(2)}) copy-start(f32[1024]{0:T(1024)S(1)} %broadcast_multiply_fusion.6) | copy-start | bytes 12292
  394.1 109.7 %copy-start.60 = (f32[1024]{0:T(1024)}, f32[1024]{0:T(1024)S(1)}, u32[]{:S(2)}) copy-start(f32[1024]{0:T(1024)S(1)} %add_rsqrt_fusion) | copy-start | bytes 12292
  394.1 29.1 %copy-start.72 = (f32[8192]{0:T(1024)S(1)}, f32[8192]{0:T(1024)}, u32[]{:S(2)}) copy-start(f32[8192]{0:T(1024)} %slice_convert_fusion.2) | copy-start | bytes 98308
  504.5 6.7 copy-start.34
  515.0 645.2 %reduce-scatter.9.cloned.1.call-start = ((), (), s32[]{:S(2)}) async-start(), calls=%async_computation.13 | async-start | bytes 2359296 | tf_op jit(solution)/shard_map/reduce_scatter | solution.py:177
  528.1 7.1 copy-start.38
  623.1 10.3 copy-start.4
  623.1 10.3 copy-start.6
  732.9 10.3 copy-start.4
  732.9 10.3 copy-start.6
  760.5 7.3 copy-start.32
  807.9 352.3 %reduce-scatter.7.cloned.1.call-start = ((), (), s32[]{:S(2)}) async-start(), calls=%async_computation.12 | async-start | bytes 7077888 | tf_op jit(solution)/shard_map/reduce_scatter | solution.py:174
  902.4 10.3 copy-start.1
  902.4 10.3 copy-start.8
  1017.2 10.3 copy-start.1
  1017.2 10.3 copy-start.8
  1064.1 128.3 %reduce-scatter.11.cloned.1.call-start = ((), (), s32[]{:S(2)}) async-start(), calls=%async_computation.14 | async-start | bytes 7077888 | tf_op jit(solution)/shard_map/reduce_scatter | solution.py:174
  1066.8 8.2 copy-start.27
  1092.6 219.3 %reduce-scatter.17.cloned.1.call-start = ((), (), s32[]{:S(2)}) async-start(), calls=%async_computation.17 | async-start | bytes 18874368 | tf_op jit(solution)/shard_map/reduce_scatter | solution.py:177
  1128.6 302.7 %reduce-scatter.15.cloned.1.call-start = ((), (), s32[]{:S(2)}) async-start(), calls=%async_computation.16 | async-start | bytes 18874368 | tf_op jit(solution)/shard_map/reduce_scatter | solution.py:174
  1157.0 274.4 %copy-start.81 = (f32[1024]{0:T(1024)S(1)}, f32[1024]{0:T(1024)}, u32[]{:S(2)}) copy-start(f32[1024]{0:T(1024)} %get-tuple-element.701) | copy-start | bytes 12292
  1157.0 502.3 %all-reduce.11.cloned.1.call-start = ((), (), s32[]{:S(2)}) async-start(), calls=%async_computation.18 | async-start | bytes 12582912 | tf_op jit(solution)/shard_map/psum | solution.py:188
  1659.2 7.5 copy-start.29
  (78 other events, 281.0 us)
Sparse Core Ops, SparseCore 0:
  10.0 48.2 all-gather.12
  60.2 45.5 all-gather.16
  107.6 27.8 all-gather.14
  137.3 27.8 all-gather.18
  167.0 89.8 all-gather.20
  258.6 89.8 all-gather.22
  515.1 42.3 reduce-scatter.12
  808.0 42.2 reduce-scatter.8
  1064.2 62.7 reduce-scatter.6
  1130.6 61.7 reduce-scatter.10
  1195.9 115.9 reduce-scatter.16
  1315.3 115.9 reduce-scatter.14
  1434.1 225.0 all-reduce.10
where the time goes:
time: 1690 us; the launch traced here: 1680 us
  matrix products  748 us (44%)
  waiting for transfers between devices  388 us (23%)
  other arithmetic  263 us (16%)
  local copies, waits for them, and re-layouts  160 us (9%)
  blocking collectives  91 us (5%)
  between operations  17 us (1%)
    reduce_scatter x3, waiting for transfers between devices, reduce_block(): lax.psum_scatter(grad_first.astype(jnp.bfloat16), 'shard', scatter_dimens...  152 us
    dot_general x8, matrix products, masked_scores(): jnp.einsum('qhd,khd->hqk', query_block, key_heads, preferred_element_type...  144 us
    reduce_scatter x3, waiting for transfers between devices, reduce_block(): lax.psum_scatter(grad_second.astype(jnp.bfloat16), 'shard', scatter_dimen...  120 us
    psum x1, waiting for transfers between devices, reduce_block(): lax.psum(shares[0].astype(jnp.bfloat16), 'rep').astype(jnp.float32)  113 us
    convert_element_type x4, other arithmetic, one_block(): grad_scores = (weights_p * (grad_weights - jnp.sum(weights_p * grad_weigh...  111 us
    dot_general x7, matrix products, times_transpose(): lax.dot_general(grad, weight, (((1,), (1,)), ((), ())), preferred_element...  109 us
    dot_general x4, matrix products, one_block(): jnp.einsum('qhd,khd->hqk', grad_block, value_heads, preferred_element_typ...  99.5 us
    dot_general x7, matrix products, outer_sum(): lax.dot_general(left, right, (((0,), (0,)), ((), ())), preferred_element_...  99 us
  transfers between devices with their start and end apart: 13, of which 4 were waited for; matrix products, arithmetic and copies ran while one was open for 62% of the time, Pallas kernels for 0%

commit v1 on v0

v1 whole, which is shorter than its diff:
```python
import functools
import math

import jax
import jax.numpy as jnp
from jax import lax
from jax.experimental import pallas as pl
from jax.experimental.pallas import tpu as pltpu
from jax.sharding import PartitionSpec as P

HEADS = 16
HEAD_DIM = 64
EPSILON = 1e-05
MASKED = -1e30
GELU_A = math.sqrt(2.0 / math.pi)
GELU_B = GELU_A * 0.044715

D = 1024
ROWS = 1024
GROUP = 256
GROUPS = 4
PIECES = 8
QBLOCK = 512
KBLOCK = 256
TILE = 512
F32 = jnp.float32
BF16 = jnp.bfloat16
VMEM_LIMIT = 62 * 1024 * 1024


def dot(left, right):
    return jnp.dot(left, right, preferred_element_type=F32)


def dot_t(left, right):
    return lax.dot_general(left, right, (((1,), (1,)), ((), ())), preferred_element_type=F32)


def dot_a(left, right):
    return lax.dot_general(left, right, (((0,), (0,)), ((), ())), preferred_element_type=F32)


def normalize(values):
    center = jnp.mean(values, -1, keepdims=True)
    offset = values - center
    scale_inv = lax.rsqrt(jnp.mean(offset * offset, -1, keepdims=True) + EPSILON)
    return offset * scale_inv, scale_inv


def norm_back(grad, values, gain):
    normed, scale_inv = normalize(values)
    scaled = grad * gain
    back = scale_inv * (
        scaled
        - jnp.mean(scaled, -1, keepdims=True)
        - normed * jnp.mean(scaled * normed, -1, keepdims=True)
    )
    return back, jnp.sum(grad * normed, 0, keepdims=True), jnp.sum(grad, 0, keepdims=True)


def split_three(values):
    high = values.astype(BF16)
    rest = values - high.astype(F32)
    middle = rest.astype(BF16)
    return high, middle, (rest - middle.astype(F32)).astype(BF16)


def place(me, rank):
    return lax.bitwise_xor(me, rank)


def qkv_copies(me, group, first, second, weights, sems):
    copies = []
    slot = group % 2
    for rank in range(PIECES):
        rows = pl.ds(pl.multiple_of(place(me, rank) * 128, 128), 128)
        for index, (piece, offset) in enumerate(
            ((first[rank], 0), (first[rank], D), (second[rank], 0))
        ):
            source = pl.ds(pl.multiple_of(offset + group * GROUP, GROUP), GROUP)
            target = pl.ds(index * GROUP, GROUP)
            copies.append(
                pltpu.make_async_copy(
                    piece.at[:, source],
                    weights.at[slot, rows, target],
                    sems.at[slot, rank * 3 + index],
                )
            )
    return copies


def out_copies(me, second, out_weights, sems):
    copies = []
    for rank in range(PIECES):
        rows = pl.ds(pl.multiple_of(place(me, rank) * 128, 128), 128)
        copies.append(
            pltpu.make_async_copy(
                second[rank].at[:, pl.ds(D, D)], out_weights.at[rows, :], sems.at[rank]
            )
        )
    return copies


def start_all(copies):
    for copy in copies:
        copy.start()


def wait_all(copies):
    for copy in copies:
        copy.wait()


def build_self_bias(seg_col, seg_row, pad_row, bias):
    for first in range(0, ROWS, QBLOCK):
        count = first + QBLOCK
        rows = first + lax.broadcasted_iota(jnp.int32, (QBLOCK, count), 0)
        cols = lax.broadcasted_iota(jnp.int32, (QBLOCK, count), 1)
        same = seg_col[first : first + QBLOCK, :] == seg_row[:, :count]
        real = (pad_row[:, :count] == 1) | (cols == rows)
        allowed = (cols <= rows) & same & real
        bias[first : first + QBLOCK, :count] = jnp.where(allowed, 0.0, MASKED)


def lanes_of(half):
    lane = lax.broadcasted_iota(jnp.int32, (1, 128), 1)
    mine = (lane < 64) if half == 0 else (lane >= 64)
    return lane, mine, (64 if half == 0 else 0)


def key_mask(shape, length):
    rows = lax.broadcasted_iota(jnp.int32, shape, 0)
    return jnp.where(rows < length, 0.0, MASKED).astype(BF16)


def forward_pair(query, key, value, length, bias, out_ref, log_ref, pair, causal):
    lane, _, _ = lanes_of(0)
    columns = slice(pair * 128, pair * 128 + 128)
    logs = [[], []]
    for first in range(0, ROWS, QBLOCK):
        count = first + QBLOCK if causal else key.shape[0]
        outs = []
        for half in range(2):
            _, mine, extra = lanes_of(half)
            q_block = query[first : first + QBLOCK]
            if causal:
                q_ext = jnp.where(mine, q_block, jnp.zeros_like(q_block))
                scores = dot_t(q_ext, key[:count]) + bias[first : first + QBLOCK, :count]
            else:
                q_ext = jnp.where(mine, q_block, (lane == extra).astype(BF16))
                k_ext = jnp.where(lane == extra, key_mask(key.shape, length), key)
                scores = dot_t(q_ext, k_ext)
            row_max = jnp.max(scores, 1, keepdims=True)
            weights = jnp.exp(scores - row_max).astype(BF16)
            v_ext = jnp.where(mine, value[:count], jnp.ones_like(value[:count]))
            mixed = dot(weights, v_ext)
            total = mixed[:, extra : extra + 1]
            outs.append((mixed, total))
            log_ref[0, first : first + QBLOCK, 2 * pair + half : 2 * pair + half + 1] = (
                row_max + jnp.log(total)
            )
        numerator = jnp.where(lane < 64, outs[0][0], outs[1][0])
        denominator = jnp.where(lane < 64, outs[0][1], outs[1][1])
        out_ref[first : first + QBLOCK, columns] = (numerator / denominator).astype(BF16)


def attend_forward_body(cross, *refs):
    it = iter(refs)
    scalars = next(it)
    x_ref = next(it)
    if cross:
        enc_ref = next(it)
    else:
        seg_col, seg_row, pad_row = next(it), next(it), next(it)
    gain, shift, out_bias, q_bias, v_bias = (next(it) for _ in range(5))
    first = [next(it) for _ in range(PIECES)]
    second = [next(it) for _ in range(PIECES)]
    x_out, q_ref, k_ref, v_ref, o_ref, log_ref = (next(it) for _ in range(6))
    a_ref, weights, out_weights, sems, out_sems = (next(it) for _ in range(5))
    bias = None if cross else next(it)
    group = pl.program_id(0)
    me = scalars[0]
    length = scalars[1]

    @pl.when(group == 0)
    def _():
        start_all(qkv_copies(me, 0, first, second, weights, sems))
        start_all(out_copies(me, second, out_weights, out_sems))
        values = x_ref[...].astype(F32)
        normed, _ = normalize(values)
        a_ref[...] = (normed * gain[...] + shift[...]).astype(BF16)
        x_out[...] = values + out_bias[...]
        if not cross:
            build_self_bias(seg_col, seg_row, pad_row, bias)

    @pl.when(group < GROUPS - 1)
    def _():
        start_all(qkv_copies(me, group + 1, first, second, weights, sems))

    wait_all(qkv_copies(me, group, first, second, weights, sems))

    def block(index):
        return weights[group % 2, :, index * GROUP : (index + 1) * GROUP]

    kv_rows = enc_ref[...] if cross else a_ref[...]
    q_ref[...] = ((dot(a_ref[...], block(0)) + q_bias[...]) * 0.125).astype(BF16)
    k_ref[...] = dot(kv_rows, block(1)).astype(BF16)
    v_ref[...] = (dot(kv_rows, block(2)) + v_bias[...]).astype(BF16)
    for pair in range(2):
        columns = slice(pair * 128, pair * 128 + 128)
        forward_pair(
            q_ref[:, columns],
            k_ref[:, columns],
            v_ref[:, columns],
            length,
            bias,
            o_ref,
            log_ref,
            pair,
            not cross,
        )

    @pl.when(group == 0)
    def _():
        wait_all(out_copies(me, second, out_weights, out_sems))

    rows = pl.ds(pl.multiple_of(group * GROUP, GROUP), GROUP)
    x_out[...] += dot(o_ref[...], out_weights[rows, :])


def whole(shape):
    zeros = (0,) * len(shape)
    return pl.BlockSpec(shape, lambda *_: zeros, pipeline_mode=pl.Buffered(1))


def whole_out(shape):
    zeros = (0,) * len(shape)
    return pl.BlockSpec(shape, lambda *_: zeros, pipeline_mode=pl.Buffered(1))


def group_block(rows=ROWS):
    return pl.BlockSpec((rows, GROUP), lambda g, s: (0, g))


ANY = pl.BlockSpec(memory_space=pl.ANY)


def cost(flops, nbytes, exps=0):
    return pl.CostEstimate(flops=int(flops), bytes_accessed=int(nbytes), transcendentals=int(exps))


def attend_forward(scalars, x, extras, vectors, first, second):
    cross = len(extras) == 1
    gain, shift, out_bias, q_bias, v_bias = vectors
    if cross:
        extra_specs = [whole((ROWS, D))]
    else:
        extra_specs = [whole((ROWS, 1)), whole((1, ROWS)), whole((1, ROWS))]
    scratch = [
        pltpu.VMEM((ROWS, D), BF16),
        pltpu.VMEM((2, D, 3 * GROUP), BF16),
        pltpu.VMEM((D, D), BF16),
        pltpu.SemaphoreType.DMA((2, 3 * PIECES)),
        pltpu.SemaphoreType.DMA((PIECES,)),
    ]
    if not cross:
        scratch.append(pltpu.VMEM((ROWS, ROWS), F32))
    return pl.pallas_call(
        functools.partial(attend_forward_body, cross),
        grid_spec=pltpu.PrefetchScalarGridSpec(
            num_scalar_prefetch=1,
            grid=(GROUPS,),
            in_specs=[whole((ROWS, D))]
            + extra_specs
            + [whole((1, D))] * 3
            + [group_block(1)] * 2
            + [ANY] * (2 * PIECES),
            out_specs=[whole_out((ROWS, D))]
            + [group_block()] * 4
            + [pl.BlockSpec((1, ROWS, 4), lambda g, s: (g, 0, 0))],
            scratch_shapes=scratch,
        ),
        out_shape=[jax.ShapeDtypeStruct((ROWS, D), F32)]
        + [jax.ShapeDtypeStruct((ROWS, D), BF16)] * 4
        + [jax.ShapeDtypeStruct((GROUPS, ROWS, 4), F32)],
        compiler_params=pltpu.CompilerParams(vmem_limit_bytes=VMEM_LIMIT),
        cost_estimate=cost(2 * ROWS * D * D * (4 + 8), 30e6, HEADS * ROWS * ROWS),
        name="cross_forward" if cross else "self_forward",
    )(scalars, x, *extras, gain, shift, out_bias, q_bias, v_bias, *first, *second)


def backward_pair(refs, go_ref, length, bias, accs, pair, causal):
    q_ref, k_ref, v_ref, o_ref, log_ref = refs
    dq_ref, dk_ref, dv_ref, dk_acc, dv_acc = accs
    columns = slice(pair * 128, pair * 128 + 128)
    query, key, value = q_ref[:, columns], k_ref[:, columns], v_ref[:, columns]
    go = go_ref[:, columns]
    q_turned, go_turned = query.T, go.T
    product = go.astype(F32) * o_ref[:, columns].astype(F32)
    zeros = jnp.zeros_like(query)
    q_ext, go_ext, k_ext, v_ext, k_own = [], [], [], [], []
    for half in range(2):
        lane, mine, extra = lanes_of(half)
        delta = jnp.sum(jnp.where(mine, product, 0.0), 1, keepdims=True)
        logs = log_ref[0, :, 2 * pair + half : 2 * pair + half + 1]
        k_own.append(jnp.where(mine, key, zeros))

        def with_rows(base, column, last):
            high, middle, low = split_three(-column)
            filled = jnp.where(lane == extra, high, jnp.where(lane == extra + 1, middle, zeros))
            filled = jnp.where(lane == extra + 2, low, filled)
            filled = jnp.where(lane == extra + 3, last, filled)
            return jnp.where(mine, base, filled)

        ones = ((lane >= extra) & (lane < extra + 3)).astype(BF16)
        one = jnp.ones_like(query)
        q_ext.append(with_rows(query, logs, zeros if causal else one))
        go_ext.append(with_rows(go, delta, zeros))
        keys = jnp.where(mine, key, ones)
        if not causal:
            keys = jnp.where(lane == extra + 3, key_mask(key.shape, length), keys)
        k_ext.append(keys)
        v_ext.append(jnp.where(mine, value, ones))
    last_first = ROWS - KBLOCK
    for first in range(last_first, -1, -KBLOCK):
        rows = slice(first, first + KBLOCK)
        count = first + KBLOCK if causal else key.shape[0]
        grads_q = []
        for half in range(2):
            scores = dot_t(q_ext[half][rows], k_ext[half][:count])
            if causal:
                scores = scores + bias[rows, :count]
            weights = jnp.exp(scores)
            grad_weights = dot_t(go_ext[half][rows], v_ext[half][:count])
            grad_scores = (weights * grad_weights).astype(BF16)
            grads_q.append(dot(grad_scores, k_own[half][:count]))
            dims = slice(64 * half, 64 * half + 64)
            grad_value = dot(go_turned[dims, rows], weights.astype(BF16))
            grad_key = dot(q_turned[dims, rows], grad_scores)
            if first == last_first:
                dv_acc[dims, :] = grad_value
                dk_acc[dims, :] = grad_key
            else:
                dv_acc[dims, :count] += grad_value
                dk_acc[dims, :count] += grad_key
        dq_ref[rows, columns] = (grads_q[0] + grads_q[1]).astype(BF16) * 0.125
    dk_ref[:, columns] = dk_acc[...].astype(BF16).T
    dv_ref[:, columns] = dv_acc[...].astype(BF16).T


def scatter_rows(me, value, holder, keep, send, columns, height):
    holder[...] = value.astype(BF16).reshape(PIECES, height, value.shape[1])
    for slot in range(PIECES // 2):
        pair = place(slot, me // 2) * 2
        keep[slot, :, columns] = holder[pair + me % 2]
        send[slot, :, columns] = holder[pair + (1 - me % 2)]


def attend_backward_body(cross, *refs):
    it = iter(refs)
    scalars = next(it)
    gx_hbm, x_hbm = next(it), next(it)
    enc_t = next(it) if cross else None
    if not cross:
        seg_col, seg_row, pad_row = next(it), next(it), next(it)
    gain, shift = next(it), next(it)
    q_ref, k_ref, v_ref, o_ref, log_ref = (next(it) for _ in range(5))
    first = [next(it) for _ in range(PIECES)]
    second = [next(it) for _ in range(PIECES)]
    gx_out = next(it)
    genc_out = next(it) if cross else None
    keep_a, send_a, keep_b, send_b = (next(it) for _ in range(4))
    q_sum, v_sum, b_sum, gain_sum, shift_sum = (next(it) for _ in range(5))
    gx, x_ref, a_t, gb, da, weights, out_weights, sems, out_sems, sem = (
        next(it) for _ in range(10)
    )
    go, dq, dk, dv, dk_acc, dv_acc, holder, holder_out = (next(it) for _ in range(8))
    denc = next(it) if cross else None
    bias = None if cross else next(it)
    result = None if cross else next(it)
    group = pl.program_id(0)
    me = scalars[0]
    length = scalars[1]

    @pl.when(group == 0)
    def _():
        load_x = pltpu.make_async_copy(x_hbm, x_ref, sem.at[0])
        load_gx = pltpu.make_async_copy(gx_hbm, gx, sem.at[1])
        load_x.start()
        load_gx.start()
        start_all(out_copies(me, second, out_weights, out_sems))
        start_all(qkv_copies(me, 0, first, second, weights, sems))
        load_x.wait()
        normed, _ = normalize(x_ref[...].astype(F32))
        a_t[...] = (normed * gain[...] + shift[...]).astype(BF16).T
        load_gx.wait()
        gb[...] = gx[...].astype(BF16)
        b_sum[...] = jnp.sum(gb[...].astype(F32), 0, keepdims=True)
        if not cross:
            build_self_bias(seg_col, seg_row, pad_row, bias)
        wait_all(out_copies(me, second, out_weights, out_sems))

    @pl.when(group < GROUPS - 1)
    def _():
        start_all(qkv_copies(me, group + 1, first, second, weights, sems))

    rows = pl.ds(pl.multiple_of(group * GROUP, GROUP), GROUP)
    go[...] = dot_t(gb[...], out_weights[rows, :]).astype(BF16)
    grad_out = dot(o_ref[...].T, gb[...])
    holder_out[...] = grad_out.astype(BF16).reshape(2, 128, D)
    slot = place(group, me // 2)
    keep_b[slot, :, D : 2 * D] = holder_out[me % 2]
    send_b[slot, :, D : 2 * D] = holder_out[1 - me % 2]
    for pair in range(2):
        backward_pair(
            (q_ref, k_ref, v_ref, o_ref, log_ref),
            go,
            length,
            bias,
            (dq, dk, dv, dk_acc, dv_acc),
            pair,
            not cross,
        )
    wait_all(qkv_copies(me, group, first, second, weights, sems))

    def columns_of(index):
        return pl.ds(pl.multiple_of(index * D + group * GROUP, GROUP), GROUP)

    kv_t = enc_t if cross else a_t
    scatter_rows(me, dot(a_t[...], dq[...]), holder, keep_a, send_a, columns_of(0), 128)
    scatter_rows(me, dot(kv_t[...], dk[...]), holder, keep_a, send_a, columns_of(1), 128)
    scatter_rows(me, dot(kv_t[...], dv[...]), holder, keep_b, send_b, columns_of(0), 128)
    q_sum[...] = jnp.sum(dq[...].astype(F32), 0, keepdims=True)
    v_sum[...] = jnp.sum(dv[...].astype(F32), 0, keepdims=True)
    slot = group % 2
    from_q = dot_t(dq[...], weights[slot, :, 0:GROUP])
    from_kv = dot_t(dk[...], weights[slot, :, GROUP : 2 * GROUP]) + dot_t(
        dv[...], weights[slot, :, 2 * GROUP : 3 * GROUP]
    )
    if not cross:
        from_q = from_q + from_kv

    @pl.when(group == 0)
    def _():
        da[...] = from_q
        if cross:
            denc[...] = from_kv

    @pl.when(group > 0)
    def _():
        da[...] += from_q
        if cross:
            denc[...] += from_kv

    @pl.when(group == GROUPS - 1)
    def _():
        back, gain_grad, shift_grad = norm_back(da[...], x_ref[...].astype(F32), gain[...])
        gain_sum[...] = gain_grad
        shift_sum[...] = shift_grad
        if cross:
            gx[...] = gx[...] + back
            store = pltpu.make_async_copy(gx, gx_out, sem.at[0])
            store.start()
            gb[...] = denc[...].astype(BF16)
            store_enc = pltpu.make_async_copy(gb, genc_out, sem.at[1])
            store_enc.start()
            store_enc.wait()
        else:
            result[...] = (gx[...] + back).astype(BF16)
            store = pltpu.make_async_copy(result, gx_out, sem.at[0])
            store.start()
        store.wait()


def attend_backward(scalars, gx, x, extras, vectors, saved, first, second):
    cross = len(extras) == 1
    gain, shift = vectors
    if cross:
        extra_specs = [whole((D, ROWS))]
    else:
        extra_specs = [whole((ROWS, 1)), whole((1, ROWS)), whole((1, ROWS))]
    half = PIECES // 2
    scratch = [
        pltpu.VMEM((ROWS, D), F32),
        pltpu.VMEM((ROWS, D), x.dtype),
        pltpu.VMEM((D, ROWS), BF16),
        pltpu.VMEM((ROWS, D), BF16),
        pltpu.VMEM((ROWS, D), F32),
        pltpu.VMEM((2, D, 3 * GROUP), BF16),
        pltpu.VMEM((D, D), BF16),
        pltpu.SemaphoreType.DMA((2, 3 * PIECES)),
        pltpu.SemaphoreType.DMA((PIECES,)),
        pltpu.SemaphoreType.DMA((2,)),
        pltpu.VMEM((ROWS, GROUP), BF16),
        pltpu.VMEM((ROWS, GROUP), BF16),
        pltpu.VMEM((ROWS, GROUP), BF16),
        pltpu.VMEM((ROWS, GROUP), BF16),
        pltpu.VMEM((128, ROWS), F32),
        pltpu.VMEM((128, ROWS), F32),
        pltpu.VMEM((PIECES, 128, GROUP), BF16),
        pltpu.VMEM((2, 128, D), BF16),
    ]
    out_shape = [jax.ShapeDtypeStruct((ROWS, D), F32 if cross else BF16)]
    out_specs = [ANY]
    if cross:
        scratch.append(pltpu.VMEM((ROWS, D), F32))
        out_shape.append(jax.ShapeDtypeStruct((ROWS, D), BF16))
        out_specs.append(ANY)
    else:
        scratch.append(pltpu.VMEM((ROWS, ROWS), F32))
        scratch.append(pltpu.VMEM((ROWS, D), BF16))
    out_shape += [jax.ShapeDtypeStruct((half, 128, 2 * D), BF16)] * 4
    out_specs += [whole_out((half, 128, 2 * D))] * 4
    out_shape += [jax.ShapeDtypeStruct((1, D), F32)] * 5
    out_specs += [group_block(1)] * 2 + [whole_out((1, D))] * 3
    return pl.pallas_call(
        functools.partial(attend_backward_body, cross),
        grid_spec=pltpu.PrefetchScalarGridSpec(
            num_scalar_prefetch=1,
            grid=(GROUPS,),
            in_specs=[ANY, ANY]
            + extra_specs
            + [whole((1, D))] * 2
            + [group_block()] * 4
            + [pl.BlockSpec((1, ROWS, 4), lambda g, s: (g, 0, 0))]
            + [ANY] * (2 * PIECES),
            out_specs=out_specs,
            scratch_shapes=scratch,
        ),
        out_shape=out_shape,
        compiler_params=pltpu.CompilerParams(vmem_limit_bytes=VMEM_LIMIT),
        cost_estimate=cost(2 * ROWS * D * D * (8 + 20), 50e6, HEADS * ROWS * ROWS),
        name="cross_backward" if cross else "self_backward",
    )(scalars, gx, x, *extras, gain, shift, *saved, *first, *second)


def mlp_body(first_call, last_call, tiles, *refs):
    it = iter(refs)
    scalars = next(it)
    a_ref, a_t, go = next(it), next(it), next(it)
    b1 = next(it)
    acc_in = None if first_call else (next(it), next(it))
    if last_call:
        x_hbm, out_bias, gain = next(it), next(it), next(it)
    first = [next(it) for _ in range(PIECES)]
    second = [next(it) for _ in range(PIECES)]
    keep_a, send_a, keep_b, send_b, b1_sum = (next(it) for _ in range(5))
    acc_out = (next(it), next(it))
    if last_call:
        gain_sum, shift_sum = next(it), next(it)
    out_acc, da_acc, w1, w2, sems1, sems2, sem, holder, holder2 = (next(it) for _ in range(9))
    if last_call:
        x_ref, result = next(it), next(it)
    step = pl.program_id(0)
    me = scalars[0]
    height = TILE // 2

    def first_copies(tile, slot):
        copies = []
        for rank in range(PIECES):
            rows = pl.ds(pl.multiple_of(place(me, rank) * 128, 128), 128)
            columns = pl.ds(pl.multiple_of(tile * TILE, TILE), TILE)
            copies.append(
                pltpu.make_async_copy(
                    first[rank].at[:, columns], w1.at[slot, rows, :], sems1.at[slot, rank]
                )
            )
        return copies

    def second_copies():
        copies = []
        for rank in range(PIECES):
            rows = pl.ds(pl.multiple_of(place(me, rank) * height, height), height)
            copies.append(pltpu.make_async_copy(second[rank], w2.at[rows, :], sems2.at[rank]))
        return copies

    def acc_copies():
        return [
            pltpu.make_async_copy(acc_in[0], out_acc, sem.at[0]),
            pltpu.make_async_copy(acc_in[1], da_acc, sem.at[1]),
        ]

    slot = step % 2

    @pl.when(step == 0)
    def _():
        start_all(first_copies(0, 0))
        start_all(second_copies())
        if first_call:
            out_acc[...] = jnp.zeros_like(out_acc)
            da_acc[...] = jnp.zeros_like(da_acc)
        else:
            start_all(acc_copies())
        if last_call:
            pltpu.make_async_copy(x_hbm, x_ref, sem.at[2]).start()
        wait_all(second_copies())
        if not first_call:
            wait_all(acc_copies())

    @pl.when(step < tiles - 1)
    def _():
        start_all(first_copies(step + 1, 1 - slot))

    wait_all(first_copies(step, slot))
    w1_tile = w1[slot]
    w2_tile = w2[pl.ds(pl.multiple_of(step * TILE, TILE), TILE), :]
    unit = dot(a_ref[...], w1_tile) + b1[...]
    square = unit * unit
    bent = jnp.tanh(unit * (GELU_A + GELU_B * square))
    halved = 0.5 * unit
    active = (halved + halved * bent).astype(BF16)
    slope = 0.5 + 0.5 * bent + halved * (1.0 - bent * bent) * (GELU_A + 3.0 * GELU_B * square)
    grad_unit = (dot_t(go[...], w2_tile) * slope).astype(BF16)
    out_acc[...] += dot(active, w2_tile)
    holder2[...] = dot_a(active, go[...]).astype(BF16).reshape(2, height, D)
    keep_b[0] = holder2[me % 2]
    send_b[0] = holder2[1 - me % 2]
    b1_sum[...] = jnp.sum(grad_unit.astype(F32), 0, keepdims=True)
    scatter_rows(me, dot(a_t[...], grad_unit), holder, keep_a, send_a, slice(None), 128)
    da_acc[...] += dot_t(grad_unit, w1_tile)

    @pl.when(step == tiles - 1)
    def _():
        if last_call:
            pltpu.make_async_copy(x_hbm, x_ref, sem.at[2]).wait()
            values = x_ref[...]
            result[...] = (values + out_acc[...] + out_bias[...]).astype(BF16)
            store_out = pltpu.make_async_copy(result, acc_out[0], sem.at[0])
            store_out.start()
            back, gain_grad, shift_grad = norm_back(da_acc[...], values, gain[...])
            gain_sum[...] = gain_grad
            shift_sum[...] = shift_grad
            da_acc[...] = go[...].astype(F32) + back
        else:
            store_out = pltpu.make_async_copy(out_acc, acc_out[0], sem.at[0])
            store_out.start()
        store = pltpu.make_async_copy(da_acc, acc_out[1], sem.at[1])
        store.start()
        store_out.wait()
        store.wait()


def mlp_chunk(scalars, a, a_t, go, b1, acc, last, first, second):
    width = first[0].shape[1]
    tiles = width // TILE
    first_call, last_call = acc is None, last is not None
    half = PIECES // 2
    height = TILE // 2
    operands = [a, a_t, go, b1]
    in_specs = [whole((ROWS, D)), whole((D, ROWS)), whole((ROWS, D))]
    in_specs.append(pl.BlockSpec((1, TILE), lambda i, s: (0, i)))
    if not first_call:
        operands += list(acc)
        in_specs += [ANY, ANY]
    if last_call:
        operands += list(last)
        in_specs += [ANY, whole((1, D)), whole((1, D))]
    grad_a = pl.BlockSpec((half, 128, TILE), lambda i, s: (0, 0, i))
    grad_b = pl.BlockSpec((1, height, D), lambda i, s: (lax.bitwise_xor(i, s[0] // 2), 0, 0))
    out_specs = [grad_a, grad_a, grad_b, grad_b, pl.BlockSpec((1, TILE), lambda i, s: (0, i))]
    out_shape = (
        [jax.ShapeDtypeStruct((half, 128, width), BF16)] * 2
        + [jax.ShapeDtypeStruct((half, height, D), BF16)] * 2
        + [jax.ShapeDtypeStruct((1, width), F32)]
        + [jax.ShapeDtypeStruct((ROWS, D), BF16 if last_call else F32)]
        + [jax.ShapeDtypeStruct((ROWS, D), F32)]
    )
    out_specs += [ANY, ANY]
    if last_call:
        out_shape += [jax.ShapeDtypeStruct((1, D), F32)] * 2
        out_specs += [whole_out((1, D))] * 2
    scratch = [
        pltpu.VMEM((ROWS, D), F32),
        pltpu.VMEM((ROWS, D), F32),
        pltpu.VMEM((2, D, TILE), BF16),
        pltpu.VMEM((width, D), BF16),
        pltpu.SemaphoreType.DMA((2, PIECES)),
        pltpu.SemaphoreType.DMA((PIECES,)),
        pltpu.SemaphoreType.DMA((3,)),
        pltpu.VMEM((PIECES, 128, TILE), BF16),
        pltpu.VMEM((2, height, D), BF16),
    ]
    if last_call:
        scratch += [pltpu.VMEM((ROWS, D), F32), pltpu.VMEM((ROWS, D), BF16)]
    return pl.pallas_call(
        functools.partial(mlp_body, first_call, last_call, tiles),
        grid_spec=pltpu.PrefetchScalarGridSpec(
            num_scalar_prefetch=1,
            grid=(tiles,),
            in_specs=in_specs + [ANY] * (2 * PIECES),
            out_specs=out_specs,
            scratch_shapes=scratch,
        ),
        out_shape=out_shape,
        compiler_params=pltpu.CompilerParams(vmem_limit_bytes=VMEM_LIMIT),
        cost_estimate=cost(6 * 2 * ROWS * D * width, 30e6, ROWS * width),
        name="mlp",
    )(scalars, *operands, *first, *second)


def norm_turn_body(x_ref, gain, shift, a_ref, a_t):
    normed, _ = normalize(x_ref[...].astype(F32))
    values = (normed * gain[...] + shift[...]).astype(BF16)
    a_ref[...] = values
    a_t[...] = values.T


def norm_turn(x, gain, shift):
    return pl.pallas_call(
        norm_turn_body,
        out_shape=[
            jax.ShapeDtypeStruct((ROWS, D), BF16),
            jax.ShapeDtypeStruct((D, ROWS), BF16),
        ],
        compiler_params=pltpu.CompilerParams(vmem_limit_bytes=VMEM_LIMIT),
        name="norm_turn",
    )(x, gain, shift)


CHUNKS = 4


def gather_vectors(ln_gain, self_vec, cross_vec, mlp_vec):
    sizes = [3 * ln_gain.shape[1], self_vec.shape[0], cross_vec.shape[0], mlp_vec.shape[0]]
    packed = jnp.concatenate([ln_gain.reshape(-1), self_vec, cross_vec, mlp_vec])
    every = lax.all_gather(packed, "shard").astype(F32)
    ends = [sum(sizes[: i + 1]) for i in range(4)]
    gains = every[:, : ends[0]].reshape(-1, 3, ln_gain.shape[1]).transpose(1, 0, 2)
    gains = gains.reshape(3, 1, D)
    return [gains] + [every[:, a:b].reshape(1, -1) for a, b in zip(ends[:3], ends[1:])]


def cut_rows(full):
    rows = full.shape[0] // PIECES
    return [full[rows * r : rows * (r + 1)] for r in range(PIECES)]


def join_pieces(keep, send):
    return jnp.stack([keep, send], 1).reshape(PIECES, *keep.shape[1:])


def summed(value):
    shard = lax.psum_scatter(value.astype(BF16), "shard", scatter_dimension=0, tiled=True)
    return lax.psum(shard, "rep").astype(F32)


def per_device(
    hidden,
    segments,
    pad_mask,
    encoder,
    src_len,
    grad_out,
    ln_gain,
    self_qkv,
    self_out,
    self_vec,
    cross_qkv,
    cross_out,
    cross_vec,
    fc_in,
    fc_out,
    mlp_vec,
):
    shards = lax.axis_size("shard")
    factor = 1.0 / math.sqrt(ROWS * lax.axis_size("rep") * shards)
    encoded = encoder.reshape(ROWS, D)
    enc_t = encoded.T
    gains, vec_one, vec_two, vec_three = gather_vectors(ln_gain, self_vec, cross_vec, mlp_vec)
    me = jnp.int32(0)
    scalars = jnp.stack([me, src_len[0]])

    def gather(value):
        return lax.all_gather(value, "shard", axis=0, tiled=True)

    def attention_weights(qkv, out):
        both = gather(jnp.concatenate([qkv, out], 1))
        return cut_rows(both[:, : 2 * D]), cut_rows(both[:, 2 * D :])

    first_one, second_one = attention_weights(self_qkv, self_out)
    first_two, second_two = attention_weights(cross_qkv, cross_out)
    full_in, full_out = gather(fc_in), gather(fc_out)
    ff = full_in.shape[1]
    step = ff // PIECES // CHUNKS
    pieces_in = full_in.reshape(D, PIECES, CHUNKS, step)
    pieces_out = full_out.reshape(PIECES, CHUNKS, step, D)
    bias_in = vec_three[:, 2 * D :].reshape(PIECES, CHUNKS, step)

    masks = (segments.reshape(ROWS, 1), segments.reshape(1, ROWS), pad_mask.reshape(1, ROWS))

    def part(vector, index):
        return vector[:, index * D : (index + 1) * D]

    x_one, *saved_one = attend_forward(
        scalars,
        hidden,
        masks,
        (gains[0], part(vec_one, 0), part(vec_one, 3), part(vec_one, 1), part(vec_one, 2)),
        first_one,
        second_one,
    )
    x_two, *saved_two = attend_forward(
        scalars,
        x_one,
        (encoded,),
        (gains[1], part(vec_two, 0), part(vec_two, 3), part(vec_two, 1), part(vec_two, 2)),
        first_two,
        second_two,
    )
    normed, normed_t = norm_turn(x_two, gains[2], part(vec_three, 0))
    acc = None
    grads_in, grads_out, sums_in = [], [], []
    for chunk in range(CHUNKS):
        last = chunk == CHUNKS - 1
        keep_a, send_a, keep_b, send_b, b1_sum, *acc = mlp_chunk(
            scalars,
            normed,
            normed_t,
            grad_out,
            bias_in[:, chunk].reshape(1, -1),
            acc,
            (x_two, part(vec_three, 1), gains[2]) if last else None,
            cut_rows(pieces_in[:, :, chunk].reshape(D, -1)),
            [pieces_out[r, chunk] for r in range(PIECES)],
        )
        grads_in.append(join_pieces(keep_a, send_a).reshape(D, PIECES, 1, step))
        grads_out.append(join_pieces(keep_b, send_b).reshape(PIECES, 1, step, D))
        sums_in.append(b1_sum.reshape(PIECES, 1, step))
    output, grad_two, gain_three, shift_three = acc
    grad_fc_in = summed(jnp.concatenate(grads_in, 2).reshape(D, ff) * factor)
    grad_fc_out = summed(jnp.concatenate(grads_out, 1).reshape(ff, D) * factor)
    sum_fc = jnp.concatenate(sums_in, 1).reshape(-1)

    grad_one, grad_enc, *rest_two = attend_backward(
        scalars,
        grad_two,
        x_one,
        (enc_t,),
        (gains[1], part(vec_two, 0)),
        saved_two,
        first_two,
        second_two,
    )
    grad_hidden, *rest_one = attend_backward(
        scalars,
        grad_one,
        hidden,
        masks,
        (gains[0], part(vec_one, 0)),
        saved_one,
        first_one,
        second_one,
    )

    def attention_grads(rest):
        keep_a, send_a, keep_b, send_b, q_sum, v_sum, b_sum, gain_sum, shift_sum = rest
        grad_a = join_pieces(keep_a, send_a).reshape(D, 2 * D)
        grad_b = join_pieces(keep_b, send_b).reshape(D, 2 * D)
        qkv = jnp.concatenate([grad_a, grad_b[:, :D]], 1)
        vector = jnp.concatenate([shift_sum, q_sum, v_sum, b_sum], 1)[0]
        return (
            summed(qkv * factor),
            summed(grad_b[:, D:] * factor),
            summed(vector * factor),
            gain_sum,
        )

    grad_cross_qkv, grad_cross_out, grad_cross_vec, gain_two = attention_grads(rest_two)
    grad_self_qkv, grad_self_out, grad_self_vec, gain_one = attention_grads(rest_one)
    vector = jnp.concatenate([shift_three[0], jnp.sum(grad_out.astype(F32), 0), sum_fc])
    grad_mlp_vec = summed(vector * factor)
    stacked = jnp.concatenate([gain_one, gain_two, gain_three], 0) * factor
    grad_gain = lax.psum(
        lax.psum_scatter(stacked.astype(BF16), "shard", scatter_dimension=1, tiled=True), "rep"
    ).astype(F32)
    return (
        output,
        grad_hidden,
        grad_enc.reshape(1, ROWS, D),
        grad_gain,
        grad_self_qkv,
        grad_self_out,
        grad_self_vec,
        grad_cross_qkv,
        grad_cross_out,
        grad_cross_vec,
        grad_fc_in,
        grad_fc_out,
        grad_mlp_vec,
    )


def solution(mesh):
    placed = (
        P(("rep", "shard"), None),
        P(("rep", "shard")),
        P(("rep", "shard")),
        P(("rep", "shard"), None, None),
        P(("rep", "shard")),
        P(("rep", "shard"), None),
        P(None, "shard"),
        P("shard", None),
        P("shard", None),
        P("shard"),
        P("shard", None),
        P("shard", None),
        P("shard"),
        P("shard", None),
        P("shard", None),
        P("shard"),
    )
    return jax.shard_map(
        per_device,
        mesh=mesh,
        in_specs=placed,
        out_specs=(
            P(("rep", "shard"), None),
            P(("rep", "shard"), None),
            P(("rep", "shard"), None, None),
            P(None, "shard"),
            P("shard", None),
            P("shard", None),
            P("shard"),
            P("shard", None),
            P("shard", None),
            P("shard"),
            P("shard", None),
            P("shard", None),
            P("shard"),
        ),
        check_vma=False,
    )
```

time: 1690 us -> 1530 us (0.905)
  matrix products: 748 us -> 0 us
  Pallas kernels: 0 us -> 436 us
  waiting for transfers between devices: 388 us -> 674 us
  other arithmetic: 263 us -> 56.1 us
  local copies, waits for them, and re-layouts: 160 us -> 290 us
  blocking collectives: 91 us -> 46.2 us
    dot_general x49 -> x0, matrix products: 748 us -> none  [the longest x8 144 us: masked_scores(): jnp.einsum('qhd,khd->hqk', query_block, key_heads, preferred_element_type...]
    pallas_call x0 -> x9, Pallas kernels: none -> 436 us  [the longest x2 173 us: attend_backward(): pl.pallas_call(functools.partial(attend_backward_body, cross), grid_spec=...]
    all_gather x6 -> x4, waiting for transfers between devices: 0.03 us -> 161 us  [gather(): return lax.all_gather(value, 'shard', axis=0, tiled=True)]
    convert_element_type x32 -> x12, other arithmetic: 156 us -> 12.3 us  [the longest x8 11.6 us: summed(): return lax.psum(shard, 'rep').astype(F32)]
    slice x5 -> x10, local copies, waits for them, and re-layouts: 11.2 us -> 122 us  [the longest x4 119 us: cut_rows(): return [full[rows * r:rows * (r + 1)] for r in range(PIECES)]]
    psum x1, waiting for transfers between devices: 113 us -> 213 us  [summed(): return lax.psum(shard, 'rep').astype(F32)]
    reduce_sum x17 -> x1, other arithmetic: 98 us -> 0.37 us  [per_device(): jnp.sum(grad_out.astype(F32), 0)]
    all_gather x6 -> x1, blocking collectives: 52.6 us -> 10.7 us  [gather_vectors(): every = lax.all_gather(packed, 'shard').astype(F32)]
  transfers between devices with their start and end apart: 13 -> 12, of which waited for: 4 -> 9; matrix products, arithmetic and copies ran while one was open for 62% -> 6% of each run, Pallas kernels for 0% -> 17%
where the time goes in v1:
time: 1530 us; the launch traced here: 1520 us
  waiting for transfers between devices  674 us (44%)
  Pallas kernels  436 us (28%)
  local copies, waits for them, and re-layouts  290 us (19%)
  other arithmetic  56.1 us (4%)
  blocking collectives  46.2 us (3%)
  between operations  17.3 us (1%)
    reduce_scatter x5, waiting for transfers between devices, summed(): lax.psum_scatter(value.astype(BF16), 'shard', scatter_dimension=0, tiled=...  288 us
    psum x1, waiting for transfers between devices, summed(): return lax.psum(shard, 'rep').astype(F32)  213 us
    pallas_call x2, Pallas kernels, attend_backward(): pl.pallas_call(functools.partial(attend_backward_body, cross), grid_spec=...  173 us
    pallas_call x4, Pallas kernels, mlp_chunk(): pl.pallas_call(functools.partial(mlp_body, first_call, last_call, tiles),...  173 us
    all_gather x4, waiting for transfers between devices, gather(): return lax.all_gather(value, 'shard', axis=0, tiled=True)  161 us
    slice x4, local copies, waits for them, and re-layouts, cut_rows(): return [full[rows * r:rows * (r + 1)] for r in range(PIECES)]  119 us
    unnamed x174, local copies, waits for them, and re-layouts  88.4 us
    pallas_call x2, Pallas kernels, attend_forward(): pl.pallas_call(functools.partial(attend_forward_body, cross), grid_spec=p...  84.9 us
  transfers between devices with their start and end apart: 12, of which 9 were waited for; matrix products, arithmetic and copies ran while one was open for 6% of the time, Pallas kernels for 17%

profile of v1, /device:TPU:0, one launch (start us, length us, event | category | flops | bytes accessed | tf_op | source)
XLA Modules:
  0.0 1520.1 jit_solution(4637466464219814643)
XLA Ops:
  7.2 2.3 pad_maximum_fusion.12
  9.6 2.3 pad_maximum_fusion.13
  14.0 10.7 all-gather.1
  29.6 38.0 %all-gather.7.cloned.1.call-done = bf16[1024,4096]{1,0:T(8,128)(2,1)} async-done(((bf16[128,4096]{1,0:T(8,128)(2,1)}), bf16[1024,4096]{1,0:T(8,128)(2,1)}) %all-gather.7.cloned.1.call-update) | async-done | bytes 8388624 | tf_op jit(solution)/shard_map/all_gather | solution.py:774
  67.6 6.1 fusion.7
  73.7 50.8 %all-gather.9.cloned.1.call-done = bf16[1024,4096]{1,0:T(8,128)(2,1)} async-done(((bf16[128,4096]{1,0:T(8,128)(2,1)}), bf16[1024,4096]{1,0:T(8,128)(2,1)}) %all-gather.9.cloned.1.call-update) | async-done | bytes 8388624 | tf_op jit(solution)/shard_map/all_gather | solution.py:774
  124.5 6.1 fusion.6
  130.5 41.6 %self_forward.1 = (f32[1024,1024]{1,0:T(8,128)}, bf16[1024,1024]{1,0:T(8,128)(2,1)}, bf16[1024,1024]{1,0:T(8,128)(2,1)}, bf16[1024,1024]{1,0:T(8,128)(2,1)}, bf1...) custom-call(s32[2]{0:T(128)} %pad_add_fusion.refs_0_, bf16[1024,1024]{1,0:T(8,128)(2,1)} %refs_2_.1, ...), custom_call_target="tpu_custom_call" | custom-call | flops 25769803776 | bytes 30000000 | tf_op jit(solution)/shard_map/self_forward/pallas_call | solution.py:268
  172.1 43.3 %cross_forward.1 = (f32[1024,1024]{1,0:T(8,128)}, bf16[1024,1024]{1,0:T(8,128)(2,1)}, bf16[1024,1024]{1,0:T(8,128)(2,1)}, bf16[1024,1024]{1,0:T(8,128)(2,1)}, bf...) custom-call(s32[2]{0:T(128)} %pad_add_fusion.refs_0_, f32[1024,1024]{1,0:T(8,128)} %get-tuple-element.78.refs_1_.refs_2_, ...), custom_call_target="tpu_custom_call" | custom-call | flops 25769803776 | bytes 30000000 | tf_op jit(solution)/shard_map/cross_forward/pallas_call | solution.py:268
  215.4 5.7 norm_turn.1
  221.1 6.3 slice_bitcast_fusion.19
  227.4 8.1 slice_bitcast_fusion
  235.5 72.4 %all-gather.11.cloned.1.call-done = bf16[1024,8192]{1,0:T(8,128)(2,1)} async-done(((bf16[128,8192]{1,0:T(8,128)(2,1)}), bf16[1024,8192]{1,0:T(8,128)(2,1)}) %all-gather.11.cloned.1.call-update) | async-done | bytes 16777232 | tf_op jit(solution)/shard_map/all_gather | solution.py:774
  307.9 27.8 %reshape.141 = bf16[1024,8,4,256]{3,2,1,0:T(4,128)(2,1)} reshape(bf16[1024,8192]{1,0:T(8,128)(2,1)} %all-gather.11.cloned.1.call-done) | data formatting | bytes 33554432 | tf_op jit(solution)/shard_map/reshape | solution.py:785
  335.7 52.2 %slice_reduce_fusion.19 = (bf16[128,8,256]{2,1,0:T(8,128)(2,1)}, bf16[128,8,256]{2,1,0:T(8,128)(2,1)}, bf16[128,8,256]{2,1,0:T(8,128)(2,1)}, bf16[128,8,256]{2,1...) fusion(bf16[1024,8,4,256]{3,2,1,0:T(4,128)(2,1)} %reshape.141), kind=kLoop, calls=%fused_computation.38 | loop fusion | bytes 13631488 | tf_op jit(solution)/shard_map/slice | solution.py:735
  387.9 54.6 %slice_reduce_fusion = (bf16[128,8,256]{2,1,0:T(8,128)(2,1)}, bf16[128,8,256]{2,1,0:T(8,128)(2,1)}, bf16[128,8,256]{2,1,0:T(8,128)(2,1)}, bf16[128,8,256]{2,1,0:...) fusion(bf16[1024,8,4,256]{3,2,1,0:T(4,128)(2,1)} %reshape.141), kind=kLoop, calls=%fused_computation.19 | loop fusion | bytes 19922944 | tf_op jit(solution)/shard_map/slice | solution.py:735
  442.5 2.1 copy.297
  476.4 40.2 %mlp.4 = (bf16[4,128,2048]{2,1,0:T(8,128)(2,1)}, bf16[4,128,2048]{2,1,0:T(8,128)(2,1)}, bf16[4,256,1024]{2,1,0:T(8,128)(2,1)}, bf16[4,256,1024]{2,1,0:T(8,128)(2...) custom-call(s32[2]{0:T(128)} %pad_add_fusion.refs_0_, ...), custom_call_target="tpu_custom_call" | custom-call | flops 25769803776 | bytes 30000000 | tf_op jit(solution)/shard_map/mlp/pallas_call | solution.py:685
  516.6 43.5 %mlp.5 = (bf16[4,128,2048]{2,1,0:T(8,128)(2,1)}, bf16[4,128,2048]{2,1,0:T(8,128)(2,1)}, bf16[4,256,1024]{2,1,0:T(8,128)(2,1)}, bf16[4,256,1024]{2,1,0:T(8,128)(2...) custom-call(s32[2]{0:T(128)} %pad_add_fusion.refs_0_, ...), custom_call_target="tpu_custom_call" | custom-call | flops 25769803776 | bytes 30000000 | tf_op jit(solution)/shard_map/mlp/pallas_call | solution.py:685
  560.1 43.0 %mlp.6 = (bf16[4,128,2048]{2,1,0:T(8,128)(2,1)}, bf16[4,128,2048]{2,1,0:T(8,128)(2,1)}, bf16[4,256,1024]{2,1,0:T(8,128)(2,1)}, bf16[4,256,1024]{2,1,0:T(8,128)(2...) custom-call(s32[2]{0:T(128)} %pad_add_fusion.refs_0_, ...), custom_call_target="tpu_custom_call" | custom-call | flops 25769803776 | bytes 30000000 | tf_op jit(solution)/shard_map/mlp/pallas_call | solution.py:685
  603.1 46.0 %mlp.7 = (bf16[4,128,2048]{2,1,0:T(8,128)(2,1)}, bf16[4,128,2048]{2,1,0:T(8,128)(2,1)}, bf16[4,256,1024]{2,1,0:T(8,128)(2,1)}, bf16[4,256,1024]{2,1,0:T(8,128)(2...) custom-call(s32[2]{0:T(128)} %pad_add_fusion.refs_0_, ...), custom_call_target="tpu_custom_call" | custom-call | flops 25769803776 | bytes 30000000 | tf_op jit(solution)/shard_map/mlp/pallas_call | solution.py:685
  649.1 2.6 pad_maximum_fusion.7
  663.4 7.2 maximum_multiply_fusion
  670.7 23.2 %copy.214 = bf16[1024,8,4,256]{0,3,2,1:T(8,128)(2,1)} copy(bf16[1024,8,4,256]{3,1,0,2:T(8,128)(2,1)} %maximum_multiply_fusion) | data formatting | bytes 33554432 | tf_op jit(solution)/shard_map/mul | solution.py:830
  693.9 21.2 %copy.227 = bf16[1024,8192]{1,0:T(8,128)(2,1)} copy(bf16[1024,8192]{0,1:T(8,128)(2,1)} %bitcast.235) | data formatting | bytes 33554432
  716.6 2.5 copy.171
  719.2 96.6 %cross_backward.1 = (f32[1024,1024]{1,0:T(8,128)}, bf16[1024,1024]{1,0:T(8,128)(2,1)}, bf16[4,128,2048]{2,1,0:T(8,128)(2,1)}, bf16[4,128,2048]{2,1,0:T(8,128)(2,...) custom-call(s32[2]{0:T(128)} %pad_add_fusion.refs_0_, ...), custom_call_target="tpu_custom_call" | custom-call | flops 60129542144 | bytes 50000000 | tf_op jit(solution)/shard_map/cross_backward/pallas_call | solution.py:516
  815.8 76.1 %self_backward.1 = (bf16[1024,1024]{1,0:T(8,128)(2,1)}, bf16[4,128,2048]{2,1,0:T(8,128)(2,1)}, bf16[4,128,2048]{2,1,0:T(8,128)(2,1)}, bf16[4,128,2048]{2,1,0:T(8...) custom-call(s32[2]{0:T(128)} %pad_add_fusion.refs_0_, ...), custom_call_target="tpu_custom_call" | custom-call | flops 60129542144 | bytes 50000000 | tf_op jit(solution)/shard_map/self_backward/pallas_call | solution.py:516
  892.0 2.6 pad_maximum_fusion.1
  896.8 2.6 pad_maximum_fusion.3
  900.0 2.3 slice_multiply_fusion
  902.4 2.7 pad_maximum_fusion
  905.7 3.7 maximum_multiply_fusion.2
  914.6 3.7 maximum_multiply_fusion.3
  930.3 2.8 maximum_multiply_fusion.1
  933.1 6.8 copy.219
  941.7 4.1 copy.228
  945.8 37.5 %reduce-scatter.18.cloned.1.call-done = bf16[128,1024]{1,0:T(8,128)(2,1)} async-done(((bf16[1024,1024]{1,0:T(8,128)(2,1)}), bf16[128,1024]{1,0:T(8,128)(2,1)}) %reduce-scatter.18.cloned.1.call-update) | async-done | bytes 262160 | tf_op jit(solution)/shard_map/reduce_scatter | solution.py:743
  983.3 65.2 %reduce-scatter.12.cloned.1.call-done = bf16[128,3072]{1,0:T(8,128)(2,1)} async-done(((bf16[1024,3072]{1,0:T(8,128)(2,1)}), bf16[128,3072]{1,0:T(8,128)(2,1)}) %reduce-scatter.12.cloned.1.call-update) | async-done | bytes 786448 | tf_op jit(solution)/shard_map/reduce_scatter | solution.py:743
  1048.5 65.5 %reduce-scatter.16.cloned.1.call-done = bf16[128,3072]{1,0:T(8,128)(2,1)} async-done(((bf16[1024,3072]{1,0:T(8,128)(2,1)}), bf16[128,3072]{1,0:T(8,128)(2,1)}) %reduce-scatter.16.cloned.1.call-update) | async-done | bytes 786448 | tf_op jit(solution)/shard_map/reduce_scatter | solution.py:743
  1114.0 119.4 %reduce-scatter.20.cloned.1.call-done = bf16[1024,1024]{1,0:T(8,128)(2,1)} async-done(((bf16[8192,1024]{1,0:T(8,128)(2,1)}), bf16[1024,1024]{1,0:T(8,128)(2,1)}) %reduce-scatter.20.cloned.1.call-update) | async-done | bytes 2097168 | tf_op jit(solution)/shard_map/reduce_scatter | solution.py:743
  1236.1 23.5 %all-reduce.3 = (bf16[4096]{0:T(1024)(128)(2,1)S(1)}, bf16[4096]{0:T(1024)(128)(2,1)S(1)}, bf16[10240]{0:T(1024)(128)(2,1)S(1)}) all-reduce(bf16[4096]{0:T(1024)(128)(2,1)S(1)} %get-tuple-element.302, bf16[4096]{0:T(1024)(128)(2,1)S(1)} %get-tuple-element.301, ...), channel_id=6, replica_groups=mesh['rep'=4,'shard'=8] {'shard'}, use_global_device_ids=true, to_apply=%region_6.0.clone | all-reduce | flops 18432 | bytes 73728
  1259.8 10.8 reduce-scatter.22.cloned.1.call-done
  1271.5 12.0 all-reduce.4
  1285.8 213.0 %all-reduce.8.cloned.1.call-done = (bf16[128,8192]{0,1:T(8,128)(2,1)}, bf16[128,3072]{1,0:T(8,128)(2,1)}, bf16[128,1024]{1,0:T(8,128)(2,1)}, bf16[128,3072]{1,0:...) async-done(((bf16[128,8192]{0,1:T(8,128)(2,1)}, bf16[128,3072]{1,0:T(8,128)(2,1)}, bf16[128,1024]{1,0:T(8,128)(2,1)}, bf16[128,3072]{1,0:T(8,128)(2,1)}, ...) | async-done | bytes 6291472 | tf_op jit(solution)/shard_map/psum | solution.py:744
  1502.4 2.4 convert_element_type.57
  1506.1 4.3 copy.224
  1510.4 2.5 convert_element_type.68
  (240 shorter events, 82.9 us)
Async XLA Ops:
  7.2 60.4 %all-gather.7.cloned.1.call-start = ((), (), s32[]{:S(2)}) async-start(), calls=%async_computation.7 | async-start | bytes 9437184 | tf_op jit(solution)/shard_map/all_gather | solution.py:774
  9.5 4.4 copy-start.54
  9.5 4.4 copy-start.56
  9.5 4.4 copy-start.57
  9.5 4.4 copy-start.58
  9.5 15.4 %copy-start.42 = (s32[1024]{0:T(1024)S(1)}, s32[1024]{0:T(1024)}, u32[]{:S(2)}) copy-start(s32[1024]{0:T(1024)} %param.17) | copy-start | bytes 12292
  9.5 114.9 %all-gather.9.cloned.1.call-start = ((), (), s32[]{:S(2)}) async-start(), calls=%async_computation.8 | async-start | bytes 9437184 | tf_op jit(solution)/shard_map/all_gather | solution.py:774
  11.9 209.2 %all-gather.13.cloned.1.call-start = ((), (), s32[]{:S(2)}) async-start(), calls=%async_computation.10 | async-start | bytes 18874368 | tf_op jit(solution)/shard_map/all_gather | solution.py:774
  12.6 295.3 %all-gather.11.cloned.1.call-start = ((), (), s32[]{:S(2)}) async-start(), calls=%async_computation.9 | async-start | bytes 18874368 | tf_op jit(solution)/shard_map/all_gather | solution.py:774
  13.2 928.5 %reduce-scatter.24.cloned.1.call-start = ((), (), s32[]{:S(2)}) async-start(), calls=%async_computation.17 | async-start | bytes 18874368
  442.5 8.1 copy-start.20
  442.5 9.1 copy-start.19
  442.5 10.0 copy-start.18
  442.5 10.9 copy-start.17
  442.5 11.8 copy-start.16
  444.6 10.7 copy-start.15
  446.6 9.6 copy-start.14
  448.6 8.5 copy-start.13
  450.6 7.4 copy-start.12
  451.6 7.4 copy-start.11
  452.5 7.3 copy-start.10
  453.4 7.4 copy-start.8
  454.3 7.4 copy-start.7
  455.3 7.3 copy-start.6
  456.2 7.3 copy-start.5
  457.1 7.3 copy-start.4
  458.0 7.3 copy-start.3
  458.9 7.3 copy-start.2
  459.8 7.3 copy-start.1
  715.1 230.7 %reduce-scatter.14.cloned.1.call-start = ((), (), s32[]{:S(2)}) async-start(), calls=%async_computation.12 | async-start | bytes 2359296 | tf_op jit(solution)/shard_map/reduce_scatter | solution.py:743
  896.8 86.5 %reduce-scatter.18.cloned.1.call-start = ((), (), s32[]{:S(2)}) async-start(), calls=%async_computation.14 | async-start | bytes 2359296 | tf_op jit(solution)/shard_map/reduce_scatter | solution.py:743
  902.4 146.1 %reduce-scatter.12.cloned.1.call-start = ((), (), s32[]{:S(2)}) async-start(), calls=%async_computation.11 | async-start | bytes 7077888 | tf_op jit(solution)/shard_map/reduce_scatter | solution.py:743
  909.4 204.6 %reduce-scatter.16.cloned.1.call-start = ((), (), s32[]{:S(2)}) async-start(), calls=%async_computation.13 | async-start | bytes 7077888 | tf_op jit(solution)/shard_map/reduce_scatter | solution.py:743
  918.4 315.0 %reduce-scatter.20.cloned.1.call-start = ((), (), s32[]{:S(2)}) async-start(), calls=%async_computation.15 | async-start | bytes 18874368 | tf_op jit(solution)/shard_map/reduce_scatter | solution.py:743
  940.0 330.7 %reduce-scatter.22.cloned.1.call-start = ((), (), s32[]{:S(2)}) async-start(), calls=%async_computation.16 | async-start | bytes 294912
  941.6 557.1 %all-reduce.8.cloned.1.call-start = ((), (), s32[]{:S(2)}) async-start(), calls=%async_computation.18 | async-start | bytes 12582912 | tf_op jit(solution)/shard_map/psum | solution.py:744
  945.7 287.8 %copy-start.59 = (u32[32]{0:T(128)S(1)}, u32[32]{0:T(128)}, u32[]{:S(2)}) copy-start(u32[32]{0:T(128)} %constant.8) | copy-start | bytes 388
  945.8 289.7 %copy-start.22 = (bf16[1024,1024]{1,0:T(8,128)(2,1)S(1)}, bf16[1024,1024]{1,0:T(8,128)(2,1)}, u32[]{:S(2)}) copy-start(bf16[1024,1024]{1,0:T(8,128)(2,1)} %refs_3_.7) | copy-start | bytes 6291460
  1233.4 2.5 copy-start.44
  1233.4 2.5 copy-start.45
  1233.4 2.5 copy-start.46
  1233.4 2.5 copy-start.48
  1233.4 2.5 copy-start.49
  1233.5 2.5 copy-start.50
  1233.5 2.5 copy-start.51
  1233.5 2.6 copy-start.55
  1498.7 6.1 copy-start.37
  1504.8 5.6 copy-start.9
  (24 other events, 43.6 us)
Sparse Core Ops, SparseCore 0:
  10.5 57.0 all-gather.6
  70.1 54.3 all-gather.8
  126.4 89.8 all-gather.12
  218.0 89.8 all-gather.10
  715.2 115.9 reduce-scatter.23
  896.9 41.4 reduce-scatter.13
  942.0 41.2 reduce-scatter.17
  986.7 61.7 reduce-scatter.11
  1052.2 61.7 reduce-scatter.15
  1117.4 115.9 reduce-scatter.19
  1237.0 33.6 reduce-scatter.21
  1274.1 224.5 all-reduce.7

commit v2 on v1

v2 whole, which is shorter than its diff:
```python
import functools
import math

import jax
import jax.numpy as jnp
from jax import lax
from jax.experimental import pallas as pl
from jax.experimental.pallas import tpu as pltpu
from jax.sharding import PartitionSpec as P

HEADS = 16
HEAD_DIM = 64
EPSILON = 1e-05
MASKED = -1e30
GELU_A = math.sqrt(2.0 / math.pi)
GELU_B = GELU_A * 0.044715

D = 1024
ROWS = 1024
GROUP = 256
GROUPS = 4
PIECES = 8
QBLOCK = 512
KBLOCK = 256
TILE = 1024
F32 = jnp.float32
BF16 = jnp.bfloat16
VMEM_LIMIT = 62 * 1024 * 1024


def dot(left, right):
    return jnp.dot(left, right, preferred_element_type=F32)


def dot_t(left, right):
    return lax.dot_general(left, right, (((1,), (1,)), ((), ())), preferred_element_type=F32)


def dot_a(left, right):
    return lax.dot_general(left, right, (((0,), (0,)), ((), ())), preferred_element_type=F32)


def normalize(values):
    center = jnp.mean(values, -1, keepdims=True)
    offset = values - center
    scale_inv = lax.rsqrt(jnp.mean(offset * offset, -1, keepdims=True) + EPSILON)
    return offset * scale_inv, scale_inv


def norm_back(grad, values, gain):
    normed, scale_inv = normalize(values)
    scaled = grad * gain
    back = scale_inv * (
        scaled
        - jnp.mean(scaled, -1, keepdims=True)
        - normed * jnp.mean(scaled * normed, -1, keepdims=True)
    )
    return back, jnp.sum(grad * normed, 0, keepdims=True), jnp.sum(grad, 0, keepdims=True)


def split_three(values):
    high = values.astype(BF16)
    rest = values - high.astype(F32)
    middle = rest.astype(BF16)
    return high, middle, (rest - middle.astype(F32)).astype(BF16)


def place(me, rank):
    return lax.bitwise_xor(me, rank)


WHOLE = ((None, 0, 4 * D),)


def shard_rows(me, rank, rows_each):
    if rank is None:
        return pl.ds(0, rows_each * PIECES)
    return pl.ds(pl.multiple_of(place(me, rank) * rows_each, rows_each), rows_each)


def qkv_copies(me, group, layout, parts, weights, sems):
    copies = []
    slot = group % 2
    for number, ((rank, first, count), part_ref) in enumerate(zip(layout, parts)):
        rows = shard_rows(me, rank, D // PIECES)
        for index in range(3):
            if first <= index * D < first + count:
                start = index * D - first + group * GROUP
                source = pl.ds(pl.multiple_of(start, GROUP), GROUP)
                copies.append(
                    pltpu.make_async_copy(
                        part_ref.at[:, source],
                        weights.at[slot, rows, pl.ds(index * GROUP, GROUP)],
                        sems.at[slot, number * 3 + index],
                    )
                )
    return copies


def out_copies(me, layout, parts, out_weights, sems):
    copies = []
    for number, ((rank, first, count), part_ref) in enumerate(zip(layout, parts)):
        if first <= 3 * D < first + count:
            rows = shard_rows(me, rank, D // PIECES)
            source = pl.ds(3 * D - first, D)
            copies.append(
                pltpu.make_async_copy(
                    part_ref.at[:, source], out_weights.at[rows, :], sems.at[number]
                )
            )
    return copies


def start_all(copies):
    for copy in copies:
        copy.start()


def wait_all(copies):
    for copy in copies:
        copy.wait()


def build_self_bias(seg_col, seg_row, pad_row, bias):
    for first in range(0, ROWS, QBLOCK):
        count = first + QBLOCK
        rows = first + lax.broadcasted_iota(jnp.int32, (QBLOCK, count), 0)
        cols = lax.broadcasted_iota(jnp.int32, (QBLOCK, count), 1)
        same = seg_col[first : first + QBLOCK, :] == seg_row[:, :count]
        real = (pad_row[:, :count] == 1) | (cols == rows)
        allowed = (cols <= rows) & same & real
        bias[first : first + QBLOCK, :count] = jnp.where(allowed, 0.0, MASKED)


def lanes_of(half):
    lane = lax.broadcasted_iota(jnp.int32, (1, 128), 1)
    mine = (lane < 64) if half == 0 else (lane >= 64)
    return lane, mine, (64 if half == 0 else 0)


def key_mask(shape, length):
    rows = lax.broadcasted_iota(jnp.int32, shape, 0)
    return jnp.where(rows < length, 0.0, MASKED).astype(BF16)


def forward_pair(query, key, value, length, bias, out_ref, log_ref, pair, causal):
    lane, _, _ = lanes_of(0)
    columns = slice(pair * 128, pair * 128 + 128)
    logs = [[], []]
    for first in range(0, ROWS, QBLOCK):
        count = first + QBLOCK if causal else key.shape[0]
        outs = []
        for half in range(2):
            _, mine, extra = lanes_of(half)
            q_block = query[first : first + QBLOCK]
            if causal:
                q_ext = jnp.where(mine, q_block, jnp.zeros_like(q_block))
                scores = dot_t(q_ext, key[:count]) + bias[first : first + QBLOCK, :count]
            else:
                q_ext = jnp.where(mine, q_block, (lane == extra).astype(BF16))
                k_ext = jnp.where(lane == extra, key_mask(key.shape, length), key)
                scores = dot_t(q_ext, k_ext)
            row_max = jnp.max(scores, 1, keepdims=True)
            weights = jnp.exp(scores - row_max).astype(BF16)
            v_ext = jnp.where(mine, value[:count], jnp.ones_like(value[:count]))
            mixed = dot(weights, v_ext)
            total = mixed[:, extra : extra + 1]
            outs.append((mixed, total))
            log_ref[0, first : first + QBLOCK, 2 * pair + half : 2 * pair + half + 1] = (
                row_max + jnp.log(total)
            )
        numerator = jnp.where(lane < 64, outs[0][0], outs[1][0])
        denominator = jnp.where(lane < 64, outs[0][1], outs[1][1])
        out_ref[first : first + QBLOCK, columns] = (numerator / denominator).astype(BF16)


def attend_forward_body(cross, layout, *refs):
    it = iter(refs)
    scalars = next(it)
    x_ref, a_ref, side = next(it), next(it), next(it)
    out_bias, q_bias, v_bias, gain, shift = (next(it) for _ in range(5))
    parts = [next(it) for _ in layout]
    x_out, next_a, next_t, q_ref, k_ref, v_ref, o_ref, log_ref = (next(it) for _ in range(8))
    weights, out_weights, sems, out_sems = (next(it) for _ in range(4))
    group = pl.program_id(0)
    me = scalars[0]
    length = scalars[1]

    @pl.when(group == 0)
    def _():
        start_all(qkv_copies(me, 0, layout, parts, weights, sems))
        start_all(out_copies(me, layout, parts, out_weights, out_sems))
        x_out[...] = x_ref[...].astype(F32) + out_bias[...]

    @pl.when(group < GROUPS - 1)
    def _():
        start_all(qkv_copies(me, group + 1, layout, parts, weights, sems))

    wait_all(qkv_copies(me, group, layout, parts, weights, sems))

    def block(index):
        return weights[group % 2, :, index * GROUP : (index + 1) * GROUP]

    kv_rows = side[...] if cross else a_ref[...]
    q_ref[...] = ((dot(a_ref[...], block(0)) + q_bias[...]) * 0.125).astype(BF16)
    k_ref[...] = dot(kv_rows, block(1)).astype(BF16)
    v_ref[...] = (dot(kv_rows, block(2)) + v_bias[...]).astype(BF16)
    for pair in range(2):
        columns = slice(pair * 128, pair * 128 + 128)
        forward_pair(
            q_ref[:, columns],
            k_ref[:, columns],
            v_ref[:, columns],
            length,
            side,
            o_ref,
            log_ref,
            pair,
            not cross,
        )

    @pl.when(group == 0)
    def _():
        wait_all(out_copies(me, layout, parts, out_weights, out_sems))

    rows = pl.ds(pl.multiple_of(group * GROUP, GROUP), GROUP)
    x_out[...] += dot(o_ref[...], out_weights[rows, :])

    @pl.when(group == GROUPS - 1)
    def _():
        normed, _ = normalize(x_out[...])
        values = (normed * gain[...] + shift[...]).astype(BF16)
        next_a[...] = values
        next_t[...] = values.T


def whole(shape):
    zeros = (0,) * len(shape)
    return pl.BlockSpec(shape, lambda *_: zeros, pipeline_mode=pl.Buffered(1))


def group_block(rows=ROWS):
    return pl.BlockSpec((rows, GROUP), lambda g, s: (0, g))


ANY = pl.BlockSpec(memory_space=pl.ANY)
PARAMS = pltpu.CompilerParams(vmem_limit_bytes=VMEM_LIMIT)


def shaped(shape, dtype=BF16):
    return jax.ShapeDtypeStruct(shape, dtype)


def skipping(body, leading, count):
    def run(*refs):
        body(*refs[:leading], *refs[leading + count :])

    return run


def cost(flops, nbytes, exps=0):
    return pl.CostEstimate(flops=int(flops), bytes_accessed=int(nbytes), transcendentals=int(exps))


def attend_forward(scalars, x, a, side, vectors, held, deps=()):
    cross = side.dtype == BF16
    layout, parts = held
    return pl.pallas_call(
        skipping(functools.partial(attend_forward_body, cross, layout), 1, len(deps)),
        grid_spec=pltpu.PrefetchScalarGridSpec(
            num_scalar_prefetch=1,
            grid=(GROUPS,),
            in_specs=[ANY] * len(deps)
            + [whole((ROWS, D))] * 3
            + [whole((1, D))]
            + [group_block(1)] * 2
            + [whole((1, D))] * 2
            + [ANY] * len(parts),
            out_specs=[whole((ROWS, D))] * 3
            + [group_block()] * 4
            + [pl.BlockSpec((1, ROWS, 4), lambda g, s: (g, 0, 0))],
            scratch_shapes=[
                pltpu.VMEM((2, D, 3 * GROUP), BF16),
                pltpu.VMEM((D, D), BF16),
                pltpu.SemaphoreType.DMA((2, 3 * len(parts))),
                pltpu.SemaphoreType.DMA((len(parts),)),
            ],
        ),
        out_shape=[shaped((ROWS, D), F32), shaped((ROWS, D)), shaped((D, ROWS))]
        + [shaped((ROWS, D))] * 4
        + [shaped((GROUPS, ROWS, 4), F32)],
        compiler_params=PARAMS,
        cost_estimate=cost(2 * ROWS * D * D * (4 + 8), 30e6, HEADS * ROWS * ROWS),
        name="cross_forward" if cross else "self_forward",
    )(scalars, *deps, x, a, side, *vectors, *parts)


def backward_pair(refs, go_ref, length, bias, accs, pair, causal):
    q_ref, k_ref, v_ref, o_ref, log_ref = refs
    grads, dk_acc, dv_acc = accs
    columns = slice(pair * 128, pair * 128 + 128)
    query, key, value = q_ref[:, columns], k_ref[:, columns], v_ref[:, columns]
    go = go_ref[:, columns]
    q_turned, go_turned = query.T, go.T
    product = go.astype(F32) * o_ref[:, columns].astype(F32)
    zeros = jnp.zeros_like(query)
    q_ext, go_ext, k_ext, v_ext, k_own = [], [], [], [], []
    for half in range(2):
        lane, mine, extra = lanes_of(half)
        delta = jnp.sum(jnp.where(mine, product, 0.0), 1, keepdims=True)
        logs = log_ref[0, :, 2 * pair + half : 2 * pair + half + 1]
        k_own.append(jnp.where(mine, key, zeros))

        def with_rows(base, column, last):
            high, middle, low = split_three(-column)
            filled = jnp.where(lane == extra, high, jnp.where(lane == extra + 1, middle, zeros))
            filled = jnp.where(lane == extra + 2, low, filled)
            filled = jnp.where(lane == extra + 3, last, filled)
            return jnp.where(mine, base, filled)

        ones = ((lane >= extra) & (lane < extra + 3)).astype(BF16)
        one = jnp.ones_like(query)
        q_ext.append(with_rows(query, logs, zeros if causal else one))
        go_ext.append(with_rows(go, delta, zeros))
        keys = jnp.where(mine, key, ones)
        if not causal:
            keys = jnp.where(lane == extra + 3, key_mask(key.shape, length), keys)
        k_ext.append(keys)
        v_ext.append(jnp.where(mine, value, ones))
    last_first = ROWS - KBLOCK
    for first in range(last_first, -1, -KBLOCK):
        rows = slice(first, first + KBLOCK)
        count = first + KBLOCK if causal else key.shape[0]
        grads_q = []
        for half in range(2):
            scores = dot_t(q_ext[half][rows], k_ext[half][:count])
            if causal:
                scores = scores + bias[rows, :count]
            weights = jnp.exp(scores)
            grad_weights = dot_t(go_ext[half][rows], v_ext[half][:count])
            grad_scores = (weights * grad_weights).astype(BF16)
            grads_q.append(dot(grad_scores, k_own[half][:count]))
            dims = slice(64 * half, 64 * half + 64)
            grad_value = dot(go_turned[dims, rows], weights.astype(BF16))
            grad_key = dot(q_turned[dims, rows], grad_scores)
            if first == last_first:
                dv_acc[dims, :] = grad_value
                dk_acc[dims, :] = grad_key
            else:
                dv_acc[dims, :count] += grad_value
                dk_acc[dims, :count] += grad_key
        grads[rows, columns] = (grads_q[0] + grads_q[1]).astype(BF16) * 0.125
    for index, total in ((1, dk_acc), (2, dv_acc)):
        first = index * GROUP + pair * 128
        grads[:, first : first + 128] = total[...].astype(BF16).T


HALF = PIECES // 2


def scatter_rows(me, base, holder, targets, columns):
    shards = holder.shape[0]
    if len(targets) == 1:
        for index in range(shards):
            targets[0][base + index, :, columns] = holder[index]
        return
    keep, send = targets
    for index in range(shards // 2):
        if shards == PIECES:
            slot, pair = index, place(index, me // 2) * 2
        else:
            slot, pair = place(base // 2 + index, me // 2), 2 * index
        keep[slot, :, columns] = holder[pair + me % 2]
        send[slot, :, columns] = holder[pair + (1 - me % 2)]


def attend_backward_body(cross, with_out, natural, *refs):
    it = iter(refs)
    scalars = next(it)
    a_hbm = next(it)
    enc_hbm = next(it) if cross else None
    bias = None if cross else next(it)
    gb, o_rows = (next(it), next(it)) if with_out else (None, None)
    go, q_ref, k_ref, v_ref, o_ref, log_ref = (next(it) for _ in range(6))
    grads = next(it)
    targets = [next(it)] if natural else [next(it), next(it)]
    q_sum, v_sum = next(it), next(it)
    a_t, dk_acc, dv_acc, holder, sem = (next(it) for _ in range(5))
    enc_t = next(it) if cross else None
    holder_out = next(it) if with_out else None
    step = pl.program_id(0)
    me = scalars[0]
    wide = 3 * GROUP

    def loads():
        copies = [pltpu.make_async_copy(a_hbm, a_t, sem.at[0])]
        if cross:
            copies.append(pltpu.make_async_copy(enc_hbm, enc_t, sem.at[1]))
        return copies

    @pl.when(step == 0)
    def _():
        start_all(loads())

    if with_out:
        shards = o_rows.shape[1] // 128
        holder_out[...] = dot(o_rows[...].T, gb[...]).astype(BF16).reshape(shards, 128, D)
        first = targets[0].shape[2] - D
        scatter_rows(me, step * shards, holder_out, targets, slice(first, first + D))
    for pair in range(2):
        backward_pair(
            (q_ref, k_ref, v_ref, o_ref, log_ref),
            go,
            scalars[1],
            bias,
            (grads, dk_acc, dv_acc),
            pair,
            not cross,
        )

    @pl.when(step == 0)
    def _():
        wait_all(loads())

    if cross:
        left = dot(a_t[...], grads[:, :GROUP]).astype(BF16)
        right = dot(enc_t[...], grads[:, GROUP:]).astype(BF16)
        holder[:, :, :GROUP] = left.reshape(PIECES, 128, GROUP)
        holder[:, :, GROUP:] = right.reshape(PIECES, 128, 2 * GROUP)
    else:
        holder[...] = dot(a_t[...], grads[...]).astype(BF16).reshape(PIECES, 128, wide)
    columns = pl.ds(pl.multiple_of(step * wide, GROUP), wide)
    scatter_rows(me, 0, holder, targets, columns)
    q_sum[...] = jnp.sum(grads[:, :GROUP].astype(F32), 0, keepdims=True)
    v_sum[...] = jnp.sum(grads[:, 2 * GROUP :].astype(F32), 0, keepdims=True)


def attend_backward(scalars, base, steps, a_t, side, go, saved, gb, natural, deps=()):
    cross = side.dtype == BF16
    wide = 3 * GROUP
    with_out = gb is not None
    total = steps * wide + (D if with_out else 0)

    def block():
        return pl.BlockSpec((ROWS, GROUP), lambda i, s: (0, base + i))

    scratch = [
        pltpu.VMEM((D, ROWS), BF16),
        pltpu.VMEM((128, ROWS), F32),
        pltpu.VMEM((128, ROWS), F32),
        pltpu.VMEM((PIECES, 128, wide), BF16),
        pltpu.SemaphoreType.DMA((2,)),
    ]
    operands = [a_t, side]
    in_specs = [ANY, ANY if cross else whole((ROWS, ROWS))]
    if cross:
        scratch.append(pltpu.VMEM((D, ROWS), BF16))
    if with_out:
        out_rows = D // steps
        operands += [gb, saved[3]]
        in_specs += [whole((ROWS, D)), pl.BlockSpec((ROWS, out_rows), lambda i, s: (0, i))]
        scratch.append(pltpu.VMEM((out_rows // 128, 128, D), BF16))
    targets = [(PIECES, 128, total)] if natural else [(HALF, 128, total)] * 2
    return pl.pallas_call(
        skipping(functools.partial(attend_backward_body, cross, with_out, natural), 1, len(deps)),
        grid_spec=pltpu.PrefetchScalarGridSpec(
            num_scalar_prefetch=1,
            grid=(steps,),
            in_specs=[ANY] * len(deps)
            + in_specs
            + [block()] * 5
            + [pl.BlockSpec((1, ROWS, 4), lambda i, s: (base + i, 0, 0))],
            out_specs=[pl.BlockSpec((ROWS, wide), lambda i, s: (0, i))]
            + [whole(shape) for shape in targets]
            + [pl.BlockSpec((1, GROUP), lambda i, s: (0, i))] * 2,
            scratch_shapes=scratch,
        ),
        out_shape=[shaped((ROWS, steps * wide))]
        + [shaped(shape) for shape in targets]
        + [shaped((1, steps * GROUP), F32)] * 2,
        compiler_params=PARAMS,
        cost_estimate=cost(2 * ROWS * D * D * (1 + 5 * steps), 20e6, 4 * steps * ROWS * ROWS),
        name="cross_backward" if cross else "self_backward",
    )(scalars, *deps, *operands, go, *saved)


def project_back_body(layout, below_layout, counts, *refs):
    cross = below_layout is not None
    it = iter(refs)
    scalars = next(it)
    grads = [next(it) for _ in counts]
    gx, x_ref, gain = next(it), next(it), next(it)
    parts = [next(it) for _ in layout]
    if cross:
        below = [next(it) for _ in below_layout]
    gx_out, gain_sum, shift_sum = (next(it) for _ in range(3))
    if cross:
        genc, b_sum, gb_out, go = (next(it) for _ in range(4))
    da, weights, sems = (next(it) for _ in range(3))
    if cross:
        denc, out_weights, out_sems = (next(it) for _ in range(3))
    group = pl.program_id(0)
    me = scalars[0]

    @pl.when(group == 0)
    def _():
        start_all(qkv_copies(me, 0, layout, parts, weights, sems))
        if cross:
            start_all(out_copies(me, below_layout, below, out_weights, out_sems))

    @pl.when(group < GROUPS - 1)
    def _():
        start_all(qkv_copies(me, group + 1, layout, parts, weights, sems))

    wait_all(qkv_copies(me, group, layout, parts, weights, sems))

    def go_on(grad, opening):
        tile = weights[group % 2]
        if cross:
            from_q = dot_t(grad[:, :GROUP], tile[:, :GROUP])
            from_kv = dot_t(grad[:, GROUP:], tile[:, GROUP:])
            denc[...] = from_kv if opening else denc[...] + from_kv
        else:
            from_q = dot_t(grad[...], tile)
        da[...] = from_q if opening else da[...] + from_q

    @pl.when(group == 0)
    def _():
        go_on(grads[0], True)

    first = 0
    for grad, count in zip(grads, counts):

        @pl.when((group >= max(first, 1)) & (group < first + count))
        def _(grad=grad):
            go_on(grad, False)

        first += count

    @pl.when(group == GROUPS - 1)
    def _():
        back, gain_grad, shift_grad = norm_back(da[...], x_ref[...].astype(F32), gain[...])
        gain_sum[...] = gain_grad
        shift_sum[...] = shift_grad
        total = gx[...] + back
        gx_out[...] = total.astype(gx_out.dtype)
        if cross:
            genc[...] = denc[...].astype(BF16)
            gb = total.astype(BF16)
            gb_out[...] = gb
            b_sum[...] = jnp.sum(gb.astype(F32), 0, keepdims=True)
            wait_all(out_copies(me, below_layout, below, out_weights, out_sems))
            go[...] = dot_t(gb, out_weights[...]).astype(BF16)


def project_back(scalars, grads, gx, x, gain, held, below=None, deps=()):
    cross = below is not None
    wide = 3 * GROUP
    layout, parts = held
    counts = [grad.shape[1] // wide for grad in grads]
    starts = [sum(counts[:i]) for i in range(len(counts))]

    def grad_spec(start, count):
        return pl.BlockSpec((ROWS, wide), lambda g, s: (0, jnp.clip(g - start, 0, count - 1)))

    operands = [*grads, gx, x, gain, *parts]
    in_specs = [grad_spec(start, count) for start, count in zip(starts, counts)]
    in_specs += [whole((ROWS, D)), whole((ROWS, D)), whole((1, D))] + [ANY] * len(parts)
    out_shape = [shaped((ROWS, D), F32 if cross else BF16)] + [shaped((1, D), F32)] * 2
    scratch = [
        pltpu.VMEM((ROWS, D), F32),
        pltpu.VMEM((2, D, wide), BF16),
        pltpu.SemaphoreType.DMA((2, 3 * len(parts))),
    ]
    if cross:
        operands += [*below[1]]
        in_specs += [ANY] * len(below[1])
        out_shape += [shaped((ROWS, D)), shaped((1, D), F32)] + [shaped((ROWS, D))] * 2
        scratch += [
            pltpu.VMEM((ROWS, D), F32),
            pltpu.VMEM((D, D), BF16),
            pltpu.SemaphoreType.DMA((len(below[1]),)),
        ]
    return pl.pallas_call(
        skipping(
            functools.partial(
                project_back_body, layout, below[0] if cross else None, tuple(counts)
            ),
            1,
            len(deps),
        ),
        grid_spec=pltpu.PrefetchScalarGridSpec(
            num_scalar_prefetch=1,
            grid=(GROUPS,),
            in_specs=[ANY] * len(deps) + in_specs,
            out_specs=[whole(out.shape) for out in out_shape],
            scratch_shapes=scratch,
        ),
        out_shape=out_shape,
        compiler_params=PARAMS,
        cost_estimate=cost(2 * ROWS * D * D * (4 if cross else 3), 30e6),
        name="cross_project" if cross else "self_project",
    )(scalars, *deps, *operands)


def mlp_up_body(a_ref, go, w1, b1, active_out, slope_out, grad_w2):
    unit = dot(a_ref[...], w1[...]) + b1[...]
    square = unit * unit
    gate = 0.5 + 0.5 * jnp.tanh(unit * (GELU_A + GELU_B * square))
    value = unit * gate
    active = value.astype(BF16)
    active_out[...] = active
    slope = gate + value * (1.0 - gate) * (2.0 * GELU_A + 6.0 * GELU_B * square)
    slope_out[...] = slope.astype(BF16)
    grad_w2[...] = dot_a(active, go[...]).astype(BF16)


def mlp_up(a, go, w1, b1, deps=()):
    ff = w1.shape[1]

    def fixed(shape):
        return pl.BlockSpec(shape, lambda i: (0, 0), pipeline_mode=pl.Buffered(1))

    tall = pl.BlockSpec((ROWS, TILE), lambda i: (0, i))
    return pl.pallas_call(
        skipping(mlp_up_body, 0, len(deps)),
        grid=(ff // TILE,),
        in_specs=[ANY] * len(deps)
        + [
            fixed((ROWS, D)),
            fixed((ROWS, D)),
            pl.BlockSpec((D, TILE), lambda i: (0, i)),
            pl.BlockSpec((1, TILE), lambda i: (0, i)),
        ],
        out_specs=[tall, tall, pl.BlockSpec((TILE, D), lambda i: (i, 0))],
        out_shape=[shaped((ROWS, ff)), shaped((ROWS, ff)), shaped((ff, D))],
        compiler_params=PARAMS,
        cost_estimate=cost(2 * 2 * ROWS * D * ff, 60e6, ROWS * ff),
        name="mlp_up",
    )(*deps, a, go, w1, b1)


def row_tile_copies(layout, parts, step, slot, weights, sems, act):
    for number, ((rank, first, count), part_ref) in enumerate(zip(layout, parts)):
        if rank is None:
            rows = pl.ds(pl.multiple_of(step * TILE, TILE), TILE)
            act(pltpu.make_async_copy(part_ref.at[rows, :], weights.at[slot], sems.at[slot]))
            continue
        low = (rank * D + first) // TILE

        @pl.when((step >= low) & (step < low + count // TILE))
        def _(part_ref=part_ref, low=low):
            rows = pl.ds(pl.multiple_of((step - low) * TILE, TILE), TILE)
            act(pltpu.make_async_copy(part_ref.at[rows, :], weights.at[slot], sems.at[slot]))


def tile_of(step, scalars, layout):
    if layout[0][0] is None:
        return step
    per_shard = D // TILE
    return place(scalars[0], step // per_shard) * per_shard + step % per_shard


def start_copy(copy):
    copy.start()


def wait_copy(copy):
    copy.wait()


def mlp_down_body(layout, below_layout, steps, *refs):
    it = iter(refs)
    scalars = next(it)
    a_t, go, slope, w1 = (next(it) for _ in range(4))
    x_hbm, gain = next(it), next(it)
    parts = [next(it) for _ in layout]
    below = [next(it) for _ in below_layout]
    grad_w1, b1_sum, gx_out, gb_out, ga, gain_sum, shift_sum, b_sum = (next(it) for _ in range(8))
    da, w2, sems, x_ref, out_weights, out_sems, sem = (next(it) for _ in range(7))
    step = pl.program_id(0)
    me = scalars[0]
    slot = step % 2

    @pl.when(step == 0)
    def _():
        row_tile_copies(layout, parts, 0, 0, w2, sems, start_copy)
        da[...] = jnp.zeros_like(da)

    @pl.when(step == 1)
    def _():
        start_all(out_copies(me, below_layout, below, out_weights, out_sems))
        pltpu.make_async_copy(x_hbm, x_ref, sem.at[0]).start()

    @pl.when(step < steps - 1)
    def _():
        row_tile_copies(layout, parts, step + 1, 1 - slot, w2, sems, start_copy)

    row_tile_copies(((None, 0, 0),), [parts[0]], 0, slot, w2, sems, wait_copy)
    grad_unit = (dot_t(go[...], w2[slot]) * slope[...].astype(F32)).astype(BF16)
    b1_sum[...] = jnp.sum(grad_unit.astype(F32), 0, keepdims=True)
    grad_w1[...] = dot(a_t[...], grad_unit).astype(BF16)
    da[...] += dot_t(grad_unit, w1[...])

    @pl.when(step == steps - 1)
    def _():
        pltpu.make_async_copy(x_hbm, x_ref, sem.at[0]).wait()
        back, gain_grad, shift_grad = norm_back(da[...], x_ref[...], gain[...])
        gain_sum[...] = gain_grad
        shift_sum[...] = shift_grad
        total = go[...].astype(F32) + back
        gx_out[...] = total
        gb = total.astype(BF16)
        gb_out[...] = gb
        b_sum[...] = jnp.sum(gb.astype(F32), 0, keepdims=True)
        wait_all(out_copies(me, below_layout, below, out_weights, out_sems))
        ga[...] = dot_t(gb, out_weights[...]).astype(BF16)


def mlp_down(scalars, a_t, go, slope, w1, x, gain, held, below, deps=()):
    ff = w1.shape[1]
    steps = ff // TILE
    layout, parts = held
    tall = pl.BlockSpec((ROWS, TILE), lambda i, s: (0, tile_of(i, s, layout)))
    out_shape = [shaped((D, ff)), shaped((1, ff), F32), shaped((ROWS, D), F32)]
    out_shape += [shaped((ROWS, D))] * 2 + [shaped((1, D), F32)] * 3
    return pl.pallas_call(
        skipping(functools.partial(mlp_down_body, layout, below[0], steps), 1, len(deps)),
        grid_spec=pltpu.PrefetchScalarGridSpec(
            num_scalar_prefetch=1,
            grid=(steps,),
            in_specs=[ANY] * len(deps)
            + [whole((D, ROWS)), whole((ROWS, D)), tall, tall, ANY, whole((1, D))]
            + [ANY] * (len(parts) + len(below[1])),
            out_specs=[tall, pl.BlockSpec((1, TILE), lambda i, s: (0, tile_of(i, s, layout)))]
            + [whole(out.shape) for out in out_shape[2:]],
            scratch_shapes=[
                pltpu.VMEM((ROWS, D), F32),
                pltpu.VMEM((2, TILE, D), BF16),
                pltpu.SemaphoreType.DMA((2,)),
                pltpu.VMEM((ROWS, D), F32),
                pltpu.VMEM((D, D), BF16),
                pltpu.SemaphoreType.DMA((len(below[1]),)),
                pltpu.SemaphoreType.DMA((1,)),
            ],
        ),
        out_shape=out_shape,
        compiler_params=PARAMS,
        cost_estimate=cost(3 * 2 * ROWS * D * ff, 60e6),
        name="mlp_down",
    )(scalars, *deps, a_t, go, slope, w1, x, gain, *parts, *below[1])


def mlp_out_body(layout, steps, *refs):
    it = iter(refs)
    scalars = next(it)
    active, x_hbm, vector = (next(it) for _ in range(3))
    parts = [next(it) for _ in layout]
    result = next(it)
    acc, w2, sems, x_ref, sem = (next(it) for _ in range(5))
    step = pl.program_id(0)
    slot = step % 2

    @pl.when(step == 0)
    def _():
        row_tile_copies(layout, parts, 0, 0, w2, sems, start_copy)
        acc[...] = jnp.zeros_like(acc)

    @pl.when(step == 1)
    def _():
        pltpu.make_async_copy(x_hbm, x_ref, sem.at[0]).start()

    @pl.when(step < steps - 1)
    def _():
        row_tile_copies(layout, parts, step + 1, 1 - slot, w2, sems, start_copy)

    row_tile_copies(((None, 0, 0),), [parts[0]], 0, slot, w2, sems, wait_copy)
    acc[...] += dot(active[...], w2[slot])

    @pl.when(step == steps - 1)
    def _():
        pltpu.make_async_copy(x_hbm, x_ref, sem.at[0]).wait()
        result[...] = (x_ref[...] + acc[...] + vector[...]).astype(BF16)


def mlp_out(scalars, active, x, vector, held, deps=()):
    ff = active.shape[1]
    steps = ff // TILE
    layout, parts = held
    return pl.pallas_call(
        skipping(functools.partial(mlp_out_body, layout, steps), 1, len(deps)),
        grid_spec=pltpu.PrefetchScalarGridSpec(
            num_scalar_prefetch=1,
            grid=(steps,),
            in_specs=[ANY] * len(deps)
            + [
                pl.BlockSpec((ROWS, TILE), lambda i, s: (0, tile_of(i, s, layout))),
                ANY,
                whole((1, D)),
            ]
            + [ANY] * len(parts),
            out_specs=whole((ROWS, D)),
            scratch_shapes=[
                pltpu.VMEM((ROWS, D), F32),
                pltpu.VMEM((2, TILE, D), BF16),
                pltpu.SemaphoreType.DMA((2,)),
                pltpu.VMEM((ROWS, D), F32),
                pltpu.SemaphoreType.DMA((1,)),
            ],
        ),
        out_shape=shaped((ROWS, D)),
        compiler_params=PARAMS,
        cost_estimate=cost(2 * ROWS * D * ff, 40e6),
        name="mlp_out",
    )(scalars, *deps, active, x, vector, *parts)


def prepare_body(x_ref, gain, shift, seg_col, seg_row, pad_row, a_ref, a_t, bias):
    normed, _ = normalize(x_ref[...].astype(F32))
    values = (normed * gain[...] + shift[...]).astype(BF16)
    a_ref[...] = values
    a_t[...] = values.T
    bias[...] = jnp.full_like(bias, MASKED)
    build_self_bias(seg_col, seg_row, pad_row, bias)


def prepare(x, gain, shift, masks):
    return pl.pallas_call(
        prepare_body,
        out_shape=[shaped((ROWS, D)), shaped((D, ROWS)), shaped((ROWS, ROWS), F32)],
        compiler_params=PARAMS,
        name="prepare",
    )(x, gain, shift, *masks)


CORE, XBIT, YBIT = 1, 2, 4


def gather_vectors(ln_gain, self_vec, cross_vec, mlp_vec):
    sizes = [3 * ln_gain.shape[1], self_vec.shape[0], cross_vec.shape[0], mlp_vec.shape[0]]
    packed = jnp.concatenate([ln_gain.reshape(-1), self_vec, cross_vec, mlp_vec])
    every = lax.all_gather(packed, "shard").astype(F32)
    ends = [sum(sizes[: i + 1]) for i in range(4)]
    gains = every[:, : ends[0]].reshape(-1, 3, ln_gain.shape[1]).transpose(1, 0, 2)
    gains = gains.reshape(3, 1, D)
    return [gains] + [every[:, a:b].reshape(1, -1) for a, b in zip(ends[:3], ends[1:])]


def join_heads_body(factor, counts, *refs):
    *sources, target, out = refs
    group = 0
    for source, count in zip(sources, counts):
        for inner in range(count):
            for index in range(3):
                first = index * D + group * GROUP
                start = inner * 3 * GROUP + index * GROUP
                target[:, first : first + GROUP] = (
                    source[:, start : start + GROUP].astype(F32) * factor
                )
            group += 1
        if source.shape[1] > count * 3 * GROUP:
            out[...] = source[:, count * 3 * GROUP :].astype(F32) * factor


def join_heads(parts, factor):
    rows = parts[0].shape[0]
    wide = 3 * GROUP
    counts = [(p.shape[1] - (D if p.shape[1] % wide else 0)) // wide for p in parts]
    return pl.pallas_call(
        functools.partial(join_heads_body, factor, counts),
        out_shape=[shaped((rows, 3 * D), F32), shaped((rows, D), F32)],
        compiler_params=PARAMS,
        name="join_heads",
    )(*parts)


def swap(value, axis, bit):
    size = lax.axis_size(axis)
    return lax.ppermute(value, axis, [(i, i ^ bit) for i in range(size)])


def add(left, right, zero):
    return (left.astype(F32) + (right.astype(F32) + zero)).astype(BF16)


def zero_of(token):
    return token.reshape(-1)[0].astype(F32) * 0.0


def held_back(value, token):
    return value + zero_of(token).astype(value.dtype)


def spread(own, axis):
    (by_x, by_y), zero = yield [(own, "shard", XBIT), (own, "shard", YBIT)]
    zero = zero.astype(own.dtype)
    size = own.shape[axis]
    half = size // 2
    low = lax.slice_in_dim(by_x, 0, half, axis=axis) + zero
    high = lax.slice_in_dim(by_y, half, size, axis=axis) + zero
    far = [(low, "shard", YBIT), (high, "shard", XBIT)]
    far, _ = yield far + [(v, "shard", CORE) for v in (own, by_x, by_y)]
    last, _ = yield [(far[0], "shard", CORE), (far[1], "shard", CORE)]
    layout = [(0, 0, size), (2, 0, size), (4, 0, size), (1, 0, size), (3, 0, size), (5, 0, size)]
    layout += [(6, 0, half), (6, half, half), (7, 0, half), (7, half, half)]
    return tuple(layout), [own, by_x, by_y, *far[2:], *far[:2], *last]


def over_copies(value):
    copies = lax.axis_size("rep")
    if copies == 1:
        return value
    odd = lax.axis_index("rep") % 2 == 1
    rows = value.shape[0] // 2
    low, high = value[:rows], value[rows:]
    (got,), zero = yield [(jnp.where(odd, low, high), "rep", 1)]
    total = add(jnp.where(odd, high, low), got, zero)
    bit = 2
    while bit < copies:
        (got,), zero = yield [(total, "rep", bit)]
        total = add(total, got, zero)
        bit *= 2
    (other,), _ = yield [(total, "rep", 1)]
    return jnp.concatenate([jnp.where(odd, other, total), jnp.where(odd, total, other)], 0)


def reduce(keep, send):
    half = keep.shape[2] // 2
    (got,), zero = yield [(send, "shard", CORE)]
    total = add(keep, got, zero)
    sum_a, sum_b = total[..., :half], total[..., half:]
    got, zero = yield [(sum_a[1::2], "shard", XBIT), (sum_b[2:], "shard", YBIT)]
    half_a, half_b = add(sum_a[0::2], got[0], zero), add(sum_b[:2], got[1], zero)
    got, zero = yield [(half_a[1], "shard", YBIT), (half_b[1], "shard", XBIT)]
    owned = [add(half_a[0], got[0], zero), add(half_b[0], got[1], zero)]
    owned = yield from over_copies(jnp.concatenate(owned, 1))
    return owned


def sum_everywhere(vector):
    for axis in ("shard", "rep"):
        bit = 1
        while bit < lax.axis_size(axis):
            (got,), zero = yield [(vector, axis, bit)]
            vector = vector + (got + zero)
            bit *= 2
    return vector


class Flow:
    def __init__(self):
        self.active = {}
        self.results = {}
        self.deps = []

    def start(self, name, steps):
        self._request(name, steps, next(steps))

    def _request(self, name, steps, wanted):
        self.deps += [array for array, _, _ in wanted]
        self.active[name] = (steps, [swap(*want) for want in wanted])

    def meet(self, token, *names):
        zero = zero_of(token)
        for name in [n for n in names if n in self.active]:
            steps, arrays = self.active[name]
            try:
                self._request(name, steps, steps.send((arrays, zero)))
            except StopIteration as end:
                del self.active[name]
                self.results[name] = end.value

    def take(self):
        deps, self.deps = self.deps, []
        return deps


def part(vector, index):
    return vector[:, index * D : (index + 1) * D]


def forward_vectors(gains, vectors, layer):
    vector, below = vectors[layer], vectors[layer + 1]
    return (
        part(vector, 3),
        part(vector, 1),
        part(vector, 2),
        gains[layer + 1],
        part(below, 0),
    )


def gather(value):
    return lax.all_gather(value, "shard", axis=0, tiled=True)


def scattered(value):
    return lax.psum_scatter(value, "shard", scatter_dimension=0, tiled=True)


def ring_device(
    hidden,
    segments,
    pad_mask,
    encoder,
    src_len,
    grad_out,
    ln_gain,
    self_qkv,
    self_out,
    self_vec,
    cross_qkv,
    cross_out,
    cross_vec,
    fc_in,
    fc_out,
    mlp_vec,
):
    shards = lax.axis_size("shard")
    factor = 1.0 / math.sqrt(ROWS * lax.axis_size("rep") * shards)
    me = lax.axis_index("shard").astype(jnp.int32)
    scalars = jnp.stack([me, src_len[0]])
    flow = Flow()
    ff = fc_in.shape[1]

    gains, *vectors = gather_vectors(ln_gain, self_vec, cross_vec, mlp_vec)
    own_one = held_back(jnp.concatenate([self_qkv, self_out], 1), gains)
    flow.start("self", spread(own_one, 1))
    by_x, by_y = flow.active["self"][1]
    near = zero_of(by_x) + zero_of(by_y)
    encoded = encoder.reshape(ROWS, D)
    enc_t = encoded.T
    masks = (segments.reshape(ROWS, 1), segments.reshape(1, ROWS), pad_mask.reshape(1, ROWS))
    a_one, a_one_t, bias = prepare(hidden, gains[0], part(vectors[0], 0), masks)
    out_sum = jnp.sum(grad_out.astype(F32), 0)
    while "self" in flow.active:
        flow.meet(a_one_t, "self")
    held_one = flow.results["self"]
    all_two = gather(held_back(jnp.concatenate([cross_qkv, cross_out], 1), near))
    all_in, all_out = gather(fc_in), gather(fc_out)
    held_two, held_out = (WHOLE, [all_two]), (WHOLE, [all_out])
    flow.take()
    x_one, a_two, a_two_t, *saved_one = attend_forward(
        scalars, hidden, a_one, bias, forward_vectors(gains, vectors, 0), held_one
    )
    x_two, a_three, a_three_t, *saved_two = attend_forward(
        scalars, x_one, a_two, encoded, forward_vectors(gains, vectors, 1), held_two
    )
    active, slope, grad_w2 = mlp_up(a_three, grad_out, all_in, part_from(vectors[2], 2))
    scattered_out = scattered(grad_w2)
    grad_w1, sum_fc, grad_two, gb_two, ga_two, gain_three, shift_three, out_two = mlp_down(
        scalars, a_three_t, grad_out, slope, all_in, x_two, gains[2], held_out, held_two
    )
    scattered_in = scattered(grad_w1)
    halves_two, *weights_two, q_two, v_two = attend_backward(
        scalars, 0, GROUPS, a_two_t, enc_t, ga_two, saved_two, gb_two, False
    )
    flow.start("cross", reduce(*weights_two))
    flow.start("out", over_copies(held_back(scattered_out, v_two)))
    grad_one, gain_two, shift_two, grad_enc, out_one, gb_one, ga_one = project_back(
        scalars,
        [halves_two],
        grad_two,
        x_one,
        gains[1],
        held_two,
        held_one,
        deps=flow.take(),
    )
    flow.meet(gain_two, "cross", "out")
    early = [gain_three[0], shift_three[0], out_sum, sum_fc[0]]
    early += [gain_two[0], shift_two[0], q_two[0], v_two[0], out_two[0]]
    flow.start("early", sum_everywhere(jnp.concatenate(early)))
    half = GROUPS // 2

    def self_backward(index):
        return attend_backward(
            scalars,
            index * half,
            half,
            a_one_t,
            bias,
            ga_one,
            saved_one,
            gb_one if index == 0 else None,
            False,
            deps=flow.take(),
        )

    grads_low, *weights, q_low, v_low = self_backward(0)
    flow.meet(v_low, "cross", "early")
    flow.start(("self", 0), reduce(*weights))
    grads_high, *weights, q_high, v_high = self_backward(1)
    flow.meet(v_high, "cross", "early", "out", ("self", 0))
    flow.start(("self", 1), reduce(*weights))
    flow.start("in", over_copies(held_back(scattered_in, v_high)))
    output = mlp_out(
        scalars, active, x_two, part(vectors[2], 1), held_out, deps=flow.take()
    )
    flow.meet(output, *flow.active)
    grad_hidden, gain_one, shift_one = project_back(
        scalars, [grads_low, grads_high], grad_one, hidden, gains[0], held_one, deps=flow.take()
    )
    late = [gain_one[0], shift_one[0], q_low[0], q_high[0], v_low[0], v_high[0], out_one[0]]
    flow.start("late", sum_everywhere(jnp.concatenate(late)))
    token = gain_one
    while flow.active:
        flow.take()
        quick = [n for n in flow.active if n != "in"]
        flow.meet(token, *quick)
        deps = flow.take()
        if "in" in flow.active:
            if deps:
                token = sum(zero_of(d) for d in deps)
            flow.meet(token, "in")
            deps += flow.take()
        if deps:
            token = sum(zero_of(d) for d in deps)
    scale = factor
    factor = factor + zero_of(gain_one)
    done = flow.results

    def own(vector):
        size = vector.shape[0] // shards
        return lax.dynamic_slice_in_dim(vector, me * size, size) * factor

    base = 3 * D + ff
    early, late = done["early"], done["late"]
    grad_gain = jnp.stack([own(late[:D]), own(early[base : base + D]), own(early[:D])], 0)
    return (
        output,
        grad_hidden,
        grad_enc.reshape(1, ROWS, D),
        grad_gain,
        *join_heads([done[("self", 0)], done[("self", 1)]], scale),
        own(late[D:]),
        *join_heads([done["cross"]], scale),
        own(early[base + D :]),
        done["in"].astype(F32) * factor,
        done["out"].astype(F32) * factor,
        own(early[D:base]),
    )


def part_from(vector, index):
    return vector[:, index * D :]


def gather_device(
    hidden,
    segments,
    pad_mask,
    encoder,
    src_len,
    grad_out,
    ln_gain,
    self_qkv,
    self_out,
    self_vec,
    cross_qkv,
    cross_out,
    cross_vec,
    fc_in,
    fc_out,
    mlp_vec,
):
    shards = lax.axis_size("shard")
    factor = 1.0 / math.sqrt(ROWS * lax.axis_size("rep") * shards)
    scalars = jnp.stack([jnp.int32(0), src_len[0]])
    encoded = encoder.reshape(ROWS, D)
    enc_t = encoded.T
    gains, *vectors = gather_vectors(ln_gain, self_vec, cross_vec, mlp_vec)
    held_one = (WHOLE, [gather(jnp.concatenate([self_qkv, self_out], 1))])
    held_two = (WHOLE, [gather(jnp.concatenate([cross_qkv, cross_out], 1))])
    all_in, held_out = gather(fc_in), (WHOLE, [gather(fc_out)])
    masks = (segments.reshape(ROWS, 1), segments.reshape(1, ROWS), pad_mask.reshape(1, ROWS))
    a_one, a_one_t, bias = prepare(hidden, gains[0], part(vectors[0], 0), masks)
    x_one, a_two, a_two_t, *saved_one = attend_forward(
        scalars, hidden, a_one, bias, forward_vectors(gains, vectors, 0), held_one
    )
    x_two, a_three, a_three_t, *saved_two = attend_forward(
        scalars, x_one, a_two, encoded, forward_vectors(gains, vectors, 1), held_two
    )
    active, slope, grad_w2 = mlp_up(a_three, grad_out, all_in, part_from(vectors[2], 2))
    grad_w1, sum_fc, grad_two, gb_two, ga_two, gain_three, shift_three, out_two = mlp_down(
        scalars, a_three_t, grad_out, slope, all_in, x_two, gains[2], held_out, held_two
    )
    halves_two, weights_two, q_two, v_two = attend_backward(
        scalars, 0, GROUPS, a_two_t, enc_t, ga_two, saved_two, gb_two, True
    )
    grad_one, gain_two, shift_two, grad_enc, out_one, gb_one, ga_one = project_back(
        scalars, [halves_two], grad_two, x_one, gains[1], held_two, held_one
    )
    halves_one, weights_one, q_one, v_one = attend_backward(
        scalars, 0, GROUPS, a_one_t, bias, ga_one, saved_one, gb_one, True
    )
    grad_hidden, gain_one, shift_one = project_back(
        scalars, [halves_one], grad_one, hidden, gains[0], held_one
    )
    output = mlp_out(scalars, active, x_two, part(vectors[2], 1), held_out)

    def summed(value):
        return lax.psum(scattered(value.astype(BF16)), "rep")

    def final(value):
        return summed(value).astype(F32) * factor

    ones = [shift_one[0], q_one[0], v_one[0], out_one[0]]
    twos = [shift_two[0], q_two[0], v_two[0], out_two[0]]
    threes = [shift_three[0], jnp.sum(grad_out.astype(F32), 0), sum_fc[0]]
    gain = jnp.concatenate([gain_one, gain_two, gain_three], 0)
    return (
        output,
        grad_hidden,
        grad_enc.reshape(1, ROWS, D),
        final(gain.T).T,
        *join_heads([summed(weights_one.reshape(D, -1))], factor),
        final(jnp.concatenate(ones)),
        *join_heads([summed(weights_two.reshape(D, -1))], factor),
        final(jnp.concatenate(twos)),
        final(grad_w1),
        final(grad_w2),
        final(jnp.concatenate(threes)),
    )


def per_device(*arrays):
    copies = lax.axis_size("rep")
    if lax.axis_size("shard") == PIECES and copies & (copies - 1) == 0:
        return ring_device(*arrays)
    return gather_device(*arrays)


def solution(mesh):
    placed = (
        P(("rep", "shard"), None),
        P(("rep", "shard")),
        P(("rep", "shard")),
        P(("rep", "shard"), None, None),
        P(("rep", "shard")),
        P(("rep", "shard"), None),
        P(None, "shard"),
        P("shard", None),
        P("shard", None),
        P("shard"),
        P("shard", None),
        P("shard", None),
        P("shard"),
        P("shard", None),
        P("shard", None),
        P("shard"),
    )
    return jax.shard_map(
        per_device,
        mesh=mesh,
        in_specs=placed,
        out_specs=(
            P(("rep", "shard"), None),
            P(("rep", "shard"), None),
            P(("rep", "shard"), None, None),
            P(None, "shard"),
            P("shard", None),
            P("shard", None),
            P("shard"),
            P("shard", None),
            P("shard", None),
            P("shard"),
            P("shard", None),
            P("shard", None),
            P("shard"),
        ),
        check_vma=False,
    )
```

time: 1530 us -> 842 us (0.55)
  waiting for transfers between devices: 674 us -> 197 us
  local copies, waits for them, and re-layouts: 290 us -> 59.4 us
  starting transfers between devices: 0.49 us -> 52.1 us
  blocking collectives: 46.2 us -> 10.7 us
  Pallas kernels: 436 us -> 412 us
  other arithmetic: 56.1 us -> 71.6 us
    reduce_scatter x5 -> x2, waiting for transfers between devices: 288 us -> 8.19 us  [scattered(): return lax.psum_scatter(value, 'shard', scatter_dimension=0, tiled=True)]
    psum x1 -> x0, waiting for transfers between devices: 213 us -> none  [summed(): return lax.psum(shard, 'rep').astype(F32)]
    ppermute x0 -> x49, waiting for transfers between devices: none -> 124 us  [swap(): return lax.ppermute(value, axis, [(i, i ^ bit) for i in range(size)])]
    slice x7 -> x41, local copies, waits for them, and re-layouts: 120 us -> 22.8 us  [the longest x25 16.2 us: zero_of(): return token.reshape(-1)[0].astype(F32) * 0.0]
    all_gather x4 -> x3, waiting for transfers between devices: 161 us -> 63.9 us  [gather(): return lax.all_gather(value, 'shard', axis=0, tiled=True)]
    unnamed x174 -> x170, local copies, waits for them, and re-layouts: 88.4 us -> 23.3 us
    ppermute x0 -> x49, starting transfers between devices: none -> 51.9 us  [swap(): return lax.ppermute(value, axis, [(i, i ^ bit) for i in range(size)])]
    mul x2 -> x0, local copies, waits for them, and re-layouts: 30 us -> none  [the longest x1 23.2 us: per_device(): grad_fc_in = summed(jnp.concatenate(grads_in, 2).reshape(D, ff) * factor)]
  transfers between devices with their start and end apart: 12 -> 54, of which waited for: 9 -> 15; matrix products, arithmetic and copies ran while one was open for 6% -> 14% of each run, Pallas kernels for 17% -> 49%
where the time goes in v2:
time: 842 us; the launch traced here: 836 us
  Pallas kernels  412 us (49%)
  waiting for transfers between devices  197 us (23%)
  other arithmetic  71.6 us (9%)
  local copies, waits for them, and re-layouts  59.4 us (7%)
  starting transfers between devices  52.1 us (6%)
  between operations  32.4 us (4%)
  blocking collectives  10.7 us (1%)
    ppermute x49, waiting for transfers between devices, swap(): return lax.ppermute(value, axis, [(i, i ^ bit) for i in range(size)])  124 us
    pallas_call x3, Pallas kernels, attend_backward(): pl.pallas_call(skipping(functools.partial(attend_backward_body, cross, wi...  118 us
    pallas_call x2, Pallas kernels, attend_forward(): pl.pallas_call(skipping(functools.partial(attend_forward_body, cross, lay...  91.9 us
    pallas_call x1, Pallas kernels, mlp_down(): pl.pallas_call(skipping(functools.partial(mlp_down_body, layout, below[0]...  70.6 us
    all_gather x3, waiting for transfers between devices, gather(): return lax.all_gather(value, 'shard', axis=0, tiled=True)  63.9 us
    ppermute x49, starting transfers between devices, swap(): return lax.ppermute(value, axis, [(i, i ^ bit) for i in range(size)])  51.9 us
    pallas_call x1, Pallas kernels, mlp_up(): pl.pallas_call(skipping(mlp_up_body, 0, len(deps)), grid=(ff // TILE,), i...  49.1 us
    pallas_call x2, Pallas kernels, project_back(): pl.pallas_call(skipping(functools.partial(project_back_body, layout, belo...  44.5 us
  transfers between devices with their start and end apart: 54, of which 15 were waited for; matrix products, arithmetic and copies ran while one was open for 14% of the time, Pallas kernels for 49%

profile of v2, /device:TPU:0, one launch (start us, length us, event | category | flops | bytes accessed | tf_op | source)
XLA Modules:
  0.0 835.7 jit_solution(4485202538047372555)
XLA Ops:
  8.0 10.7 %all-gather.1 = bf16[8,1,2688]{2,1,0:T(2,128)(2,1)S(1)} all-gather(bf16[1,1,2688]{2,1,0:T(2,128)(2,1)S(1)} %reshape.264), channel_id=2, replica_groups=mesh['rep'=4,'shard'=8] {'shard'}, dimensions={0}, use_global_device_ids=true | all-gather | bytes 48384 | tf_op jit(solution)/shard_map/all_gather | solution.py:842
  19.9 2.4 maximum_add_fusion.refs_9_.refs_8_.refs_13_
  24.3 23.6 %collective-permute-done.refs_10_.refs_9_.refs_14_ = bf16[128,4096]{1,0:T(8,128)(2,1)S(1)} collective-permute-done((bf16[128,4096]{1,0:T(8,128)(2,1)}, bf16[128,4096]{1,0:T(8,128)(2,1)S(1)}, u32[]{:S(2)}, u32[]{:S(2)}) %collective-permute-start) | collective-permute-done | bytes 1048608 | tf_op jit(solution)/shard_map/ppermute | solution.py:879
  57.3 6.9 prepare.1
  64.1 2.3 copy.41
  73.5 13.9 %collective-permute-done.5.refs_15_.refs_14_.refs_19_ = bf16[128,2048]{1,0:T(8,128)(2,1)S(1)} collective-permute-done((bf16[128,2048]{1,0:T(8,128)(2,1)}, bf16[128,2048]{1,0:T(8,128)(2,1)S(1)}, u32[]{:S(2)}, u32[]{:S(2)}) %collective-permute-start.5) | collective-permute-done | bytes 524320 | tf_op jit(solution)/shard_map/ppermute | solution.py:879
  91.8 45.9 %self_forward.1 = (f32[1024,1024]{1,0:T(8,128)}, bf16[1024,1024]{1,0:T(8,128)(2,1)}, bf16[1024,1024]{1,0:T(8,128)(2,1)}, bf16[1024,1024]{1,0:T(8,128)(2,1)}, bf1...) custom-call(s32[2]{0:T(128)} %pad_add_fusion.refs_0_, ...), custom_call_target="tpu_custom_call" | custom-call | flops 25769803776 | bytes 30000000 | tf_op jit(solution)/shard_map/self_forward/pallas_call | solution.py:268
  137.7 46.0 %cross_forward.1 = (f32[1024,1024]{1,0:T(8,128)}, bf16[1024,1024]{1,0:T(8,128)(2,1)}, bf16[1024,1024]{1,0:T(8,128)(2,1)}, bf16[1024,1024]{1,0:T(8,128)(2,1)}, bf...) custom-call(s32[2]{0:T(128)} %pad_add_fusion.refs_0_, ...), custom_call_target="tpu_custom_call" | custom-call | flops 25769803776 | bytes 30000000 | tf_op jit(solution)/shard_map/cross_forward/pallas_call | solution.py:268
  183.8 21.3 %all-gather.8.cloned.1.call-done.refs_2_.refs_4_ = bf16[1024,8192]{1,0:T(8,128)(2,1)} async-done(((bf16[128,8192]{1,0:T(8,128)(2,1)}), bf16[1024,8192]{1,0:T(8,128)(2,1)}) %all-gather.8.cloned.1.call-update) | async-done | bytes 16777232 | tf_op jit(solution)/shard_map/all_gather | solution.py:994
  205.1 49.1 %mlp_up.1 = (bf16[1024,8192]{1,0:T(8,128)(2,1)}, bf16[1024,8192]{1,0:T(8,128)(2,1)}, bf16[8192,1024]{1,0:T(8,128)(2,1)}) custom-call(bf16[1024,1024]{1,0:T(8,128)(2,1)} %get-tuple-element.79.refs_0_, bf16[1024,1024]{1,0:T(8,128)(2,1)} %refs_2_.1, bf16[1024,8192]{1,0:T(8,128)(2,1)} %all-gather.8.cloned.1.call-done.refs_2_.refs_4_, f32[1,8192]{1,0:T(1,128)} %slice.402.refs_3_), custom_call_target="tpu_custom_call" | custom-call | flops 34359738368 | bytes 60000000 | tf_op jit(solution)/shard_map/mlp_up/pallas_call | solution.py:625
  254.3 42.6 %all-gather.10.cloned.1.call-done.refs_7_.refs_11_ = bf16[8192,1024]{1,0:T(8,128)(2,1)} async-done(((bf16[1024,1024]{1,0:T(8,128)(2,1)}), bf16[8192,1024]{1,0:T(8,128)(2,1)}) %all-gather.10.cloned.1.call-update) | async-done | bytes 16777232 | tf_op jit(solution)/shard_map/all_gather | solution.py:994
  296.9 70.6 %mlp_down.1 = (bf16[1024,8192]{1,0:T(8,128)(2,1)}, f32[1,8192]{1,0:T(1,128)}, f32[1024,1024]{1,0:T(8,128)}, bf16[1024,1024]{1,0:T(8,128)(2,1)}, bf16[1024,1024]{...) custom-call(s32[2]{0:T(128)} %pad_add_fusion.refs_0_, ...), custom_call_target="tpu_custom_call" | custom-call | flops 51539607552 | bytes 60000000 | tf_op jit(solution)/shard_map/mlp_down/pallas_call | solution.py:727
  369.3 2.5 copy.35
  371.9 62.3 %cross_backward.1 = (bf16[1024,3072]{1,0:T(8,128)(2,1)}, bf16[4,128,4096]{2,1,0:T(8,128)(2,1)}, bf16[4,128,4096]{2,1,0:T(8,128)(2,1)}, f32[1,1024]{1,0:T(1,128)}, f32[1,1024]{1,0:T(1,128)}) custom-call(s32[2]{0:T(128)} %pad_add_fusion.refs_0_, bf16[1024,1024]{1,0:T(8,128)(2,1)} %get-tuple-element.75.refs_1_, bf16[1024,1024]{1,0:T(8,128)(2,1)} %bitcast.131, ...), custom_call_target="tpu_custom_call" | custom-call | flops 45097156608 | bytes 20000000 | tf_op jit(solution)/shard_map/cross_backward/pallas_call | solution.py:464
  434.3 2.3 convert_reduce_fusion
  441.1 1.8 collective-permute-start.11
  442.9 25.6 %cross_project.1 = (f32[1024,1024]{1,0:T(8,128)}, f32[1,1024]{1,0:T(1,128)}, f32[1,1024]{1,0:T(1,128)}, bf16[1024,1024]{1,0:T(8,128)(2,1)}, f32[1,1024]{1,0:T(1,...) custom-call(s32[2]{0:T(128)} %pad_add_fusion.refs_0_, bf16[4,128,4096]{2,1,0:T(8,128)(2,1)} %get-tuple-element.90.refs_1_, ...), custom_call_target="tpu_custom_call" | custom-call | flops 8589934592 | bytes 30000000 | tf_op jit(solution)/shard_map/cross_project/pallas_call | solution.py:584
  470.4 5.4 add_convert_fusion
  475.9 1.9 copy-done.4
  482.7 2.0 add_convert_fusion.8.refs_3_
  484.7 2.4 collective-permute-start.17
  487.1 30.4 %self_backward.2 = (bf16[1024,1536]{1,0:T(8,128)(2,1)}, bf16[4,128,2560]{2,1,0:T(8,128)(2,1)}, bf16[4,128,2560]{2,1,0:T(8,128)(2,1)}, f32[1,512]{1,0:T(1,128)}, f32[1,512]{1,0:T(1,128)}) custom-call(s32[2]{0:T(128)} %pad_add_fusion.refs_0_, bf16[2,128,2048]{2,1,0:T(8,128)(2,1)} %slice.321.refs_1_, bf16[2,128,2048]{2,1,0:T(8,128)(2,1)} %slice.406.refs_2_, ...), custom_call_target="tpu_custom_call" | custom-call | flops 23622320128 | bytes 20000000 | tf_op jit(solution)/shard_map/self_backward/pallas_call | solution.py:464
  521.4 8.0 collective-permute-done.10
  529.4 1.9 add_convert_fusion.7
  532.6 1.9 add_convert_fusion.6
  537.3 25.0 %self_backward.3 = (bf16[1024,1536]{1,0:T(8,128)(2,1)}, bf16[4,128,1536]{2,1,0:T(8,128)(2,1)}, bf16[4,128,1536]{2,1,0:T(8,128)(2,1)}, f32[1,512]{1,0:T(1,128)}, f32[1,512]{1,0:T(1,128)}) custom-call(s32[2]{0:T(128)} %pad_add_fusion.refs_0_, bf16[128,2048]{1,0:T(8,128)(2,1)} %slice_bitcast_fusion.2.refs_1_, bf16[128,2048]{1,0:T(8,128)(2,1)} %slice_bitcast_fusion.1.refs_2_, ...), custom_call_target="tpu_custom_call" | custom-call | flops 23622320128 | bytes 20000000 | tf_op jit(solution)/shard_map/self_backward/pallas_call | solution.py:464
  564.1 8.2 reduce-scatter.5.cloned.1.call-done
  584.0 39.0 %collective-permute-done.48 = bf16[512,1024]{1,0:T(8,128)(2,1)S(1)} collective-permute-done((bf16[512,1024]{1,0:T(8,128)(2,1)S(1)}, bf16[512,1024]{1,0:T(8,128)(2,1)S(1)}, u32[]{:S(2)}, u32[]{:S(2)}) %collective-permute-start.48) | collective-permute-done | bytes 1048608 | tf_op jit(solution)/shard_map/ppermute | solution.py:879
  625.7 2.5 add_convert_fusion.1
  630.5 26.0 %mlp_out.1 = bf16[1024,1024]{1,0:T(8,128)(2,1)} custom-call(s32[2]{0:T(128)} %pad_add_fusion.refs_0_, bf16[64,4096]{1,0:T(8,128)(2,1)} %copy-done.52, f32[16384]{0:T(1024)} %copy-done.54, bf16[512,1024]{1,0:T(8,128)(2,1)} %copy-done.24, bf16[2,128,1280]{2,1,0:T(8,128)(2,1)} %slice.333.refs_4_, bf16[2,128,1280]{2,1,0:T(8,128)(2,1)} %slice.415.refs_5_, ...), custom_call_target="tpu_custom_call" | custom-call | flops 17179869184 | bytes 40000000 | tf_op jit(solution)/shard_map/mlp_out/pallas_call | solution.py:790
  656.6 2.3 copy.45
  660.2 2.0 add_convert_fusion.2
  670.6 2.5 collective-permute-start.27
  674.6 6.1 collective-permute-done.22
  683.7 2.8 collective-permute-start.33
  687.7 18.8 %self_project.1 = (bf16[1024,1024]{1,0:T(8,128)(2,1)}, f32[1,1024]{1,0:T(1,128)}, f32[1,1024]{1,0:T(1,128)}) custom-call(s32[2]{0:T(128)} %pad_add_fusion.refs_0_, bf16[64,4096]{1,0:T(8,128)(2,1)} %copy-done.15, f32[16384]{0:T(1024)} %add_add_fusion.2.refs_2_, bf16[128,1280]{1,0:T(8,128)(2,1)} %slice_bitcast_fusion.7.refs_3_, ...), custom_call_target="tpu_custom_call" | custom-call | flops 6442450944 | bytes 30000000 | tf_op jit(solution)/shard_map/self_project/pallas_call | solution.py:584
  725.6 4.1 convert_multiply_fusion
  739.4 2.1 reshape.237
  763.6 2.7 join_heads.3
  767.8 2.7 collective-permute-start.39
  773.0 21.6 %collective-permute-done.40 = bf16[64,1536]{1,0:T(8,128)(2,1)} collective-permute-done((bf16[64,1536]{1,0:T(8,128)(2,1)}, bf16[64,1536]{1,0:T(8,128)(2,1)}, u32[]{:S(2)}, u32[]{:S(2)}) %collective-permute-start.40) | collective-permute-done | bytes 196640 | tf_op jit(solution)/shard_map/ppermute | solution.py:879
  797.6 2.5 collective-permute-start.38
  804.9 2.9 collective-permute-done.42
  808.7 2.0 collective-permute-start.44
  813.9 2.6 collective-permute-done.45
  817.3 4.3 collective-permute-done.44
  822.6 2.6 join_heads.2
  826.6 2.4 convert_multiply_fusion.1
  (376 shorter events, 131.5 us)
Async XLA Ops:
  7.2 130.5 %all-gather.6.cloned.1.call-start = ((), (), s32[]{:S(2)}) async-start(), calls=%async_computation.2 | async-start | bytes 9437184 | tf_op jit(solution)/shard_map/all_gather | solution.py:994
  22.3 25.6 %collective-permute-start = (bf16[128,4096]{1,0:T(8,128)(2,1)}, bf16[128,4096]{1,0:T(8,128)(2,1)S(1)}, u32[]{:S(2)}, u32[]{:S(2)}) collective-permute-start(bf16[128,4096]{1,0:T(8,128)(2,1)} %maximum_add_fusion.refs_9_.refs_8_.refs_13_), channel_id=1, source_target_pairs={{0,2},{1,3},{2,0},{3,1},{4,6},{5,7},{6,4},{7,5},{8,10},{9,11},{10,... | collective-permute-start | bytes 3145736 | tf_op jit(solution)/shard_map/ppermute | solution.py:879
  23.8 25.3 %collective-permute-start.1 = (bf16[128,4096]{1,0:T(8,128)(2,1)}, bf16[128,4096]{1,0:T(8,128)(2,1)S(1)}, u32[]{:S(2)}, u32[]{:S(2)}) collective-permute-start(bf16[128,4096]{1,0:T(8,128)(2,1)} %maximum_add_fusion.refs_9_.refs_8_.refs_13_), channel_id=1, source_target_pairs={{0,4},{1,5},{2,6},{3,7},{4,0},{5,1},{6,2},{7,3},{8,12},{9,13},{10,... | collective-permute-start | bytes 3145736 | tf_op jit(solution)/shard_map/ppermute | solution.py:879
  53.5 151.6 %all-gather.8.cloned.1.call-start = ((), (), s32[]{:S(2)}) async-start(), calls=%async_computation.3 | async-start | bytes 18874368 | tf_op jit(solution)/shard_map/all_gather | solution.py:994
  54.2 242.6 %all-gather.10.cloned.1.call-start = ((), (), s32[]{:S(2)}) async-start(), calls=%async_computation.4 | async-start | bytes 18874368 | tf_op jit(solution)/shard_map/all_gather | solution.py:994
  55.0 383.0 %reduce-scatter.3.cloned.1.call-start = ((), (), s32[]{:S(2)}) async-start(), calls=%async_computation.5 | async-start | bytes 18874368 | tf_op jit(solution)/shard_map/reduce_scatter | solution.py:998
  68.5 18.9 %collective-permute-start.5 = (bf16[128,2048]{1,0:T(8,128)(2,1)}, bf16[128,2048]{1,0:T(8,128)(2,1)S(1)}, u32[]{:S(2)}, u32[]{:S(2)}) collective-permute-start(bf16[128,2048]{1,0:T(8,128)(2,1)} %slice_add_fusion.1), channel_id=1, source_target_pairs={{0,4},{1,5},{2,6},{3,7},{4,0},{5,1},{6,2},{7,3},{8,12},{9,13},{10,... | collective-permute-start | bytes 1572872 | tf_op jit(solution)/shard_map/ppermute | solution.py:879
  70.5 16.9 %collective-permute-start.6 = (bf16[128,2048]{1,0:T(8,128)(2,1)}, bf16[128,2048]{1,0:T(8,128)(2,1)}, u32[]{:S(2)}, u32[]{:S(2)}) collective-permute-start(bf16[128,2048]{1,0:T(8,128)(2,1)} %slice_add_fusion), channel_id=1, source_target_pairs={{0,2},{1,3},{2,0},{3,1},{4,6},{5,7},{6,4},{7,5},{8,10},{9,11},{10,... | collective-permute-start | bytes 1572872 | tf_op jit(solution)/shard_map/ppermute | solution.py:879
  71.6 18.1 %collective-permute-start.2 = (bf16[128,4096]{1,0:T(8,128)(2,1)}, bf16[128,4096]{1,0:T(8,128)(2,1)}, u32[]{:S(2)}, u32[]{:S(2)}) collective-permute-start(bf16[128,4096]{1,0:T(8,128)(2,1)} %maximum_add_fusion.refs_9_.refs_8_.refs_13_), channel_id=1, source_target_pairs={{0,1},{1,0},{2,3},{3,2},{4,5},{5,4},{6,7},{7,6},{8,9},{9,8},{10,11... | collective-permute-start | bytes 3145736 | tf_op jit(solution)/shard_map/ppermute | solution.py:879
  71.6 19.4 %collective-permute-start.3 = (bf16[128,4096]{1,0:T(8,128)(2,1)S(1)}, bf16[128,4096]{1,0:T(8,128)(2,1)}, u32[]{:S(2)}, u32[]{:S(2)}) collective-permute-start(bf16[128,4096]{1,0:T(8,128)(2,1)S(1)} %collective-permute-done.refs_10_.refs_9_.refs_14_), channel_id=1, source_target_pairs={{0,1},{1,0},{2,3},{3,2},{4,5},{5,4},{6,7},{7,6},{8,9},{9,8},{10,11... | collective-permute-start | bytes 3145736 | tf_op jit(solution)/shard_map/ppermute | solution.py:879
  72.1 18.9 %collective-permute-start.4 = (bf16[128,4096]{1,0:T(8,128)(2,1)S(1)}, bf16[128,4096]{1,0:T(8,128)(2,1)}, u32[]{:S(2)}, u32[]{:S(2)}) collective-permute-start(bf16[128,4096]{1,0:T(8,128)(2,1)S(1)} %copy-done.7), channel_id=1, source_target_pairs={{0,1},{1,0},{2,3},{3,2},{4,5},{5,4},{6,7},{7,6},{8,9},{9,8},{10,11... | collective-permute-start | bytes 3145736 | tf_op jit(solution)/shard_map/ppermute | solution.py:879
  254.2 318.1 %reduce-scatter.5.cloned.1.call-start = ((), (), s32[]{:S(2)}) async-start(), calls=%async_computation.6 | async-start | bytes 18874368 | tf_op jit(solution)/shard_map/reduce_scatter | solution.py:998
  434.2 36.2 %collective-permute-start.9 = (bf16[4,128,4096]{2,1,0:T(8,128)(2,1)}, bf16[4,128,4096]{2,1,0:T(8,128)(2,1)}, u32[]{:S(2)}, u32[]{:S(2)}) collective-permute-start(bf16[4,128,4096]{2,1,0:T(8,128)(2,1)} %get-tuple-element.90.refs_1_), channel_id=1, source_target_pairs={{0,1},{1,0},{2,3},{3,2},{4,5},{5,4},{6,7},{7,6},{8,9},{9,8},{10,11... | collective-permute-start | bytes 12582920 | tf_op jit(solution)/shard_map/ppermute | solution.py:879
  441.1 41.6 %collective-permute-start.11 = (bf16[512,1024]{1,0:T(8,128)(2,1)S(1)}, bf16[512,1024]{1,0:T(8,128)(2,1)}, u32[]{:S(2)}, u32[]{:S(2)}) collective-permute-start(bf16[512,1024]{1,0:T(8,128)(2,1)S(1)} %broadcast_select_fusion.5.refs_2_), channel_id=1, source_target_pairs={{0,8},{8,0},{16,24},{24,16},{1,9},{9,1},{17,25},{25,17},{2,10},{10... | collective-permute-start | bytes 3145736 | tf_op jit(solution)/shard_map/ppermute | solution.py:879
  480.0 39.5 %collective-permute-start.14 = (f32[16384]{0:T(1024)S(1)}, f32[16384]{0:T(1024)S(1)}, u32[]{:S(2)}, u32[]{:S(2)}) collective-permute-start(f32[16384]{0:T(1024)S(1)} %constant_dynamic-update-slice_fusion.8.refs_4_), channel_id=1, source_target_pairs={{0,1},{1,0},{2,3},{3,2},{4,5},{5,4},{6,7},{7,6},{8,9},{9,8},{10,11... | collective-permute-start | bytes 196616 | tf_op jit(solution)/shard_map/ppermute | solution.py:879
  480.7 48.8 %collective-permute-start.10 = (bf16[2,128,2048]{2,1,0:T(8,128)(2,1)}, bf16[2,128,2048]{2,1,0:T(8,128)(2,1)}, u32[]{:S(2)}, u32[]{:S(2)}) collective-permute-start(bf16[2,128,2048]{2,1,0:T(8,128)(2,1)} %slice.321.refs_1_), channel_id=1, source_target_pairs={{0,2},{1,3},{2,0},{3,1},{4,6},{5,7},{6,4},{7,5},{8,10},{9,11},{10,... | collective-permute-start | bytes 3145736 | tf_op jit(solution)/shard_map/ppermute | solution.py:879
  482.0 50.7 %collective-permute-start.13 = (bf16[2,128,2048]{2,1,0:T(8,128)(2,1)}, bf16[2,128,2048]{2,1,0:T(8,128)(2,1)}, u32[]{:S(2)}, u32[]{:S(2)}) collective-permute-start(bf16[2,128,2048]{2,1,0:T(8,128)(2,1)} %slice.406.refs_2_), channel_id=1, source_target_pairs={{0,4},{1,5},{2,6},{3,7},{4,0},{5,1},{6,2},{7,3},{8,12},{9,13},{10,... | collective-permute-start | bytes 3145736 | tf_op jit(solution)/shard_map/ppermute | solution.py:879
  484.7 92.4 %collective-permute-start.17 = (bf16[512,1024]{1,0:T(8,128)(2,1)S(1)}, bf16[512,1024]{1,0:T(8,128)(2,1)}, u32[]{:S(2)}, u32[]{:S(2)}) collective-permute-start(bf16[512,1024]{1,0:T(8,128)(2,1)S(1)} %add_convert_fusion.8.refs_3_), channel_id=1, source_target_pairs={{0,16},{8,24},{16,0},{24,8},{1,17},{9,25},{17,1},{25,9},{2,18},{10... | collective-permute-start | bytes 3145736 | tf_op jit(solution)/shard_map/ppermute | solution.py:879
  519.4 106.3 %collective-permute-start.18 = (bf16[4,128,2560]{2,1,0:T(8,128)(2,1)}, bf16[4,128,2560]{2,1,0:T(8,128)(2,1)}, u32[]{:S(2)}, u32[]{:S(2)}) collective-permute-start(bf16[4,128,2560]{2,1,0:T(8,128)(2,1)} %get-tuple-element.110.refs_4_), channel_id=1, source_target_pairs={{0,1},{1,0},{2,3},{3,2},{4,5},{5,4},{6,7},{7,6},{8,9},{9,8},{10,11... | collective-permute-start | bytes 7864328 | tf_op jit(solution)/shard_map/ppermute | solution.py:879
  520.9 54.2 %collective-permute-start.16 = (f32[16384]{0:T(1024)}, f32[16384]{0:T(1024)S(1)}, u32[]{:S(2)}, u32[]{:S(2)}) collective-permute-start(f32[16384]{0:T(1024)} %add_add_fusion.4.refs_3_), channel_id=1, source_target_pairs={{0,2},{1,3},{2,0},{3,1},{4,6},{5,7},{6,4},{7,5},{8,10},{9,11},{10,... | collective-permute-start | bytes 196616 | tf_op jit(solution)/shard_map/ppermute | solution.py:879
  532.3 46.7 %collective-permute-start.12 = (bf16[128,2048]{1,0:T(8,128)(2,1)}, bf16[128,2048]{1,0:T(8,128)(2,1)S(1)}, u32[]{:S(2)}, u32[]{:S(2)}) collective-permute-start(bf16[128,2048]{1,0:T(8,128)(2,1)} %slice_bitcast_fusion.2.refs_1_), channel_id=1, source_target_pairs={{0,4},{1,5},{2,6},{3,7},{4,0},{5,1},{6,2},{7,3},{8,12},{9,13},{10,... | collective-permute-start | bytes 1572872 | tf_op jit(solution)/shard_map/ppermute | solution.py:879
  535.7 44.5 %collective-permute-start.15 = (bf16[128,2048]{1,0:T(8,128)(2,1)}, bf16[128,2048]{1,0:T(8,128)(2,1)}, u32[]{:S(2)}, u32[]{:S(2)}) collective-permute-start(bf16[128,2048]{1,0:T(8,128)(2,1)} %slice_bitcast_fusion.1.refs_2_), channel_id=1, source_target_pairs={{0,2},{1,3},{2,0},{3,1},{4,6},{5,7},{6,4},{7,5},{8,10},{9,11},{10,... | collective-permute-start | bytes 1572872 | tf_op jit(solution)/shard_map/ppermute | solution.py:879
  575.2 90.8 %collective-permute-start.24 = (bf16[64,8192]{1,0:T(8,128)(2,1)}, bf16[64,8192]{1,0:T(8,128)(2,1)}, u32[]{:S(2)}, u32[]{:S(2)}) collective-permute-start(bf16[64,8192]{1,0:T(8,128)(2,1)} %broadcast_select_fusion.2.refs_7_), channel_id=1, source_target_pairs={{0,8},{8,0},{16,24},{24,16},{1,9},{9,1},{17,25},{25,17},{2,10},{10... | collective-permute-start | bytes 3145736 | tf_op jit(solution)/shard_map/ppermute | solution.py:879
  577.2 83.0 %collective-permute-start.23 = (bf16[4,128,1536]{2,1,0:T(8,128)(2,1)}, bf16[4,128,1536]{2,1,0:T(8,128)(2,1)}, u32[]{:S(2)}, u32[]{:S(2)}) collective-permute-start(bf16[4,128,1536]{2,1,0:T(8,128)(2,1)} %get-tuple-element.113.refs_6_), channel_id=1, source_target_pairs={{0,1},{1,0},{2,3},{3,2},{4,5},{5,4},{6,7},{7,6},{8,9},{9,8},{10,11... | collective-permute-start | bytes 4718600 | tf_op jit(solution)/shard_map/ppermute | solution.py:879
  579.0 44.0 %collective-permute-start.48 = (bf16[512,1024]{1,0:T(8,128)(2,1)S(1)}, bf16[512,1024]{1,0:T(8,128)(2,1)S(1)}, u32[]{:S(2)}, u32[]{:S(2)}) collective-permute-start(bf16[512,1024]{1,0:T(8,128)(2,1)S(1)} %add_convert_fusion.5.refs_3_), channel_id=1, source_target_pairs={{0,8},{8,0},{16,24},{24,16},{1,9},{9,1},{17,25},{25,17},{2,10},{10... | collective-permute-start | bytes 3145736 | tf_op jit(solution)/shard_map/ppermute | solution.py:879
  580.2 90.4 %collective-permute-start.20 = (f32[16384]{0:T(1024)S(1)}, f32[16384]{0:T(1024)}, u32[]{:S(2)}, u32[]{:S(2)}) collective-permute-start(f32[16384]{0:T(1024)S(1)} %add_add_fusion.3.refs_2_), channel_id=1, source_target_pairs={{0,4},{1,5},{2,6},{3,7},{4,0},{5,1},{6,2},{7,3},{8,12},{9,13},{10,... | collective-permute-start | bytes 196616 | tf_op jit(solution)/shard_map/ppermute | solution.py:879
  623.0 45.6 %collective-permute-start.19 = (bf16[64,4096]{1,0:T(8,128)(2,1)S(1)}, bf16[64,4096]{1,0:T(8,128)(2,1)}, u32[]{:S(2)}, u32[]{:S(2)}) collective-permute-start(bf16[64,4096]{1,0:T(8,128)(2,1)S(1)} %broadcast_select_fusion.8.refs_1_), channel_id=1, source_target_pairs={{0,8},{8,0},{16,24},{24,16},{1,9},{9,1},{17,25},{25,17},{2,10},{10... | collective-permute-start | bytes 1572872 | tf_op jit(solution)/shard_map/ppermute | solution.py:879
  663.0 17.7 %collective-permute-start.22 = (bf16[2,128,1280]{2,1,0:T(8,128)(2,1)S(1)}, bf16[2,128,1280]{2,1,0:T(8,128)(2,1)S(1)}, u32[]{:S(2)}, u32[]{:S(2)}) collective-permute-start(bf16[2,128,1280]{2,1,0:T(8,128)(2,1)S(1)} %copy-done.51), channel_id=1, source_target_pairs={{0,4},{1,5},{2,6},{3,7},{4,0},{5,1},{6,2},{7,3},{8,12},{9,13},{10,... | collective-permute-start | bytes 1966088 | tf_op jit(solution)/shard_map/ppermute | solution.py:879
  664.6 19.2 %collective-permute-start.21 = (bf16[2,128,1280]{2,1,0:T(8,128)(2,1)S(1)}, bf16[2,128,1280]{2,1,0:T(8,128)(2,1)S(1)}, u32[]{:S(2)}, u32[]{:S(2)}) collective-permute-start(bf16[2,128,1280]{2,1,0:T(8,128)(2,1)S(1)} %copy-done.50), channel_id=1, source_target_pairs={{0,2},{1,3},{2,0},{3,1},{4,6},{5,7},{6,4},{7,5},{8,10},{9,11},{10,... | collective-permute-start | bytes 1966088 | tf_op jit(solution)/shard_map/ppermute | solution.py:879
  665.9 42.6 %collective-permute-start.32 = (bf16[2,128,768]{2,1,0:T(8,128)(2,1)}, bf16[2,128,768]{2,1,0:T(8,128)(2,1)}, u32[]{:S(2)}, u32[]{:S(2)}) collective-permute-start(bf16[2,128,768]{2,1,0:T(8,128)(2,1)} %slice.424.refs_6_), channel_id=1, source_target_pairs={{0,4},{1,5},{2,6},{3,7},{4,0},{5,1},{6,2},{7,3},{8,12},{9,13},{10,... | collective-permute-start | bytes 1179656 | tf_op jit(solution)/shard_map/ppermute | solution.py:879
  668.6 45.0 %collective-permute-start.31 = (bf16[2,128,768]{2,1,0:T(8,128)(2,1)S(1)}, bf16[2,128,768]{2,1,0:T(8,128)(2,1)}, u32[]{:S(2)}, u32[]{:S(2)}) collective-permute-start(bf16[2,128,768]{2,1,0:T(8,128)(2,1)S(1)} %slice.344.refs_5_), channel_id=1, source_target_pairs={{0,2},{1,3},{2,0},{3,1},{4,6},{5,7},{6,4},{7,5},{8,10},{9,11},{10,... | collective-permute-start | bytes 1179656 | tf_op jit(solution)/shard_map/ppermute | solution.py:879
  670.6 53.4 %collective-permute-start.27 = (bf16[64,4096]{1,0:T(8,128)(2,1)S(1)}, bf16[64,4096]{1,0:T(8,128)(2,1)}, u32[]{:S(2)}, u32[]{:S(2)}) collective-permute-start(bf16[64,4096]{1,0:T(8,128)(2,1)S(1)} %add_convert_fusion.12.refs_1_), channel_id=1, source_target_pairs={{0,16},{8,24},{16,0},{24,8},{1,17},{9,25},{17,1},{25,9},{2,18},{10... | collective-permute-start | bytes 1572872 | tf_op jit(solution)/shard_map/ppermute | solution.py:879
  680.7 42.5 %collective-permute-start.28 = (f32[16384]{0:T(1024)}, f32[16384]{0:T(1024)S(1)}, u32[]{:S(2)}, u32[]{:S(2)}) collective-permute-start(f32[16384]{0:T(1024)} %add_add_fusion.2.refs_2_), channel_id=1, source_target_pairs={{0,8},{8,0},{16,24},{24,16},{1,9},{9,1},{17,25},{25,17},{2,10},{10... | collective-permute-start | bytes 196616 | tf_op jit(solution)/shard_map/ppermute | solution.py:879
  683.7 61.6 %collective-permute-start.33 = (bf16[64,8192]{1,0:T(8,128)(2,1)S(1)}, bf16[64,8192]{1,0:T(8,128)(2,1)}, u32[]{:S(2)}, u32[]{:S(2)}) collective-permute-start(bf16[64,8192]{1,0:T(8,128)(2,1)S(1)} %add_convert_fusion.4.refs_7_), channel_id=1, source_target_pairs={{0,16},{8,24},{16,0},{24,8},{1,17},{9,25},{17,1},{25,9},{2,18},{10... | collective-permute-start | bytes 3145736 | tf_op jit(solution)/shard_map/ppermute | solution.py:879
  708.5 26.5 %collective-permute-start.29 = (bf16[128,1280]{1,0:T(8,128)(2,1)}, bf16[128,1280]{1,0:T(8,128)(2,1)}, u32[]{:S(2)}, u32[]{:S(2)}) collective-permute-start(bf16[128,1280]{1,0:T(8,128)(2,1)} %slice_bitcast_fusion.7.refs_3_), channel_id=1, source_target_pairs={{0,4},{1,5},{2,6},{3,7},{4,0},{5,1},{6,2},{7,3},{8,12},{9,13},{10,... | collective-permute-start | bytes 983048 | tf_op jit(solution)/shard_map/ppermute | solution.py:879
  713.6 23.4 %collective-permute-start.30 = (bf16[128,1280]{1,0:T(8,128)(2,1)}, bf16[128,1280]{1,0:T(8,128)(2,1)}, u32[]{:S(2)}, u32[]{:S(2)}) collective-permute-start(bf16[128,1280]{1,0:T(8,128)(2,1)} %slice_bitcast_fusion.6.refs_4_), channel_id=1, source_target_pairs={{0,2},{1,3},{2,0},{3,1},{4,6},{5,7},{6,4},{7,5},{8,10},{9,11},{10,... | collective-permute-start | bytes 983048 | tf_op jit(solution)/shard_map/ppermute | solution.py:879
  724.0 26.1 %collective-permute-start.43 = (f32[16384]{0:T(1024)S(1)}, f32[16384]{0:T(1024)S(1)}, u32[]{:S(2)}, u32[]{:S(2)}) collective-permute-start(f32[16384]{0:T(1024)S(1)} %add_add_fusion.1), channel_id=1, source_target_pairs={{0,16},{8,24},{16,0},{24,8},{1,17},{9,25},{17,1},{25,9},{2,18},{10... | collective-permute-start | bytes 196616 | tf_op jit(solution)/shard_map/ppermute | solution.py:879
  733.6 27.8 %collective-permute-start.46 = (bf16[64,4096]{1,0:T(8,128)(2,1)S(1)}, bf16[64,4096]{1,0:T(8,128)(2,1)}, u32[]{:S(2)}, u32[]{:S(2)}) collective-permute-start(bf16[64,4096]{1,0:T(8,128)(2,1)S(1)} %add_convert_fusion.11), channel_id=1, source_target_pairs={{0,8},{8,0},{16,24},{24,16},{1,9},{9,1},{17,25},{25,17},{2,10},{10... | collective-permute-start | bytes 1572872 | tf_op jit(solution)/shard_map/ppermute | solution.py:879
  735.0 16.2 %collective-permute-start.36 = (bf16[128,768]{1,0:T(8,128)(2,1)}, bf16[128,768]{1,0:T(8,128)(2,1)}, u32[]{:S(2)}, u32[]{:S(2)}) collective-permute-start(bf16[128,768]{1,0:T(8,128)(2,1)} %get-tuple-element.141), channel_id=1, source_target_pairs={{0,4},{1,5},{2,6},{3,7},{4,0},{5,1},{6,2},{7,3},{8,12},{9,13},{10,... | collective-permute-start | bytes 589832 | tf_op jit(solution)/shard_map/ppermute | solution.py:879
  737.0 16.3 %collective-permute-start.37 = (bf16[128,768]{1,0:T(8,128)(2,1)}, bf16[128,768]{1,0:T(8,128)(2,1)}, u32[]{:S(2)}, u32[]{:S(2)}) collective-permute-start(bf16[128,768]{1,0:T(8,128)(2,1)} %get-tuple-element.143), channel_id=1, source_target_pairs={{0,2},{1,3},{2,0},{3,1},{4,6},{5,7},{6,4},{7,5},{8,10},{9,11},{10,... | collective-permute-start | bytes 589832 | tf_op jit(solution)/shard_map/ppermute | solution.py:879
  745.4 12.0 %collective-permute-start.26 = (f32[5120]{0:T(1024)S(1)}, f32[5120]{0:T(1024)S(1)}, u32[]{:S(2)}, u32[]{:S(2)}) collective-permute-start(f32[5120]{0:T(1024)S(1)} %add_add_fusion.9), channel_id=1, source_target_pairs={{0,2},{1,3},{2,0},{3,1},{4,6},{5,7},{6,4},{7,5},{8,10},{9,11},{10,... | collective-permute-start | bytes 61448 | tf_op jit(solution)/shard_map/ppermute | solution.py:879
  750.1 16.1 %collective-permute-start.35 = (bf16[64,2560]{1,0:T(8,128)(2,1)}, bf16[64,2560]{1,0:T(8,128)(2,1)}, u32[]{:S(2)}, u32[]{:S(2)}) collective-permute-start(bf16[64,2560]{1,0:T(8,128)(2,1)} %broadcast_select_fusion.11), channel_id=1, source_target_pairs={{0,8},{8,0},{16,24},{24,16},{1,9},{9,1},{17,25},{25,17},{2,10},{10... | collective-permute-start | bytes 983048 | tf_op jit(solution)/shard_map/ppermute | solution.py:879
  751.2 74.0 %collective-permute-start.47 = (bf16[64,8192]{1,0:T(8,128)(2,1)S(1)}, bf16[64,8192]{1,0:T(8,128)(2,1)}, u32[]{:S(2)}, u32[]{:S(2)}) collective-permute-start(bf16[64,8192]{1,0:T(8,128)(2,1)S(1)} %add_convert_fusion.3), channel_id=1, source_target_pairs={{0,8},{8,0},{16,24},{24,16},{1,9},{9,1},{17,25},{25,17},{2,10},{10... | collective-permute-start | bytes 3145736 | tf_op jit(solution)/shard_map/ppermute | solution.py:879
  755.2 39.4 %collective-permute-start.40 = (bf16[64,1536]{1,0:T(8,128)(2,1)}, bf16[64,1536]{1,0:T(8,128)(2,1)}, u32[]{:S(2)}, u32[]{:S(2)}) collective-permute-start(bf16[64,1536]{1,0:T(8,128)(2,1)} %broadcast_select_fusion.14), channel_id=1, source_target_pairs={{0,8},{8,0},{16,24},{24,16},{1,9},{9,1},{17,25},{25,17},{2,10},{10... | collective-permute-start | bytes 589832 | tf_op jit(solution)/shard_map/ppermute | solution.py:879
  758.0 39.1 %collective-permute-start.34 = (f32[5120]{0:T(1024)S(1)}, f32[5120]{0:T(1024)S(1)}, u32[]{:S(2)}, u32[]{:S(2)}) collective-permute-start(f32[5120]{0:T(1024)S(1)} %add_add_fusion.8), channel_id=1, source_target_pairs={{0,4},{1,5},{2,6},{3,7},{4,0},{5,1},{6,2},{7,3},{8,12},{9,13},{10,... | collective-permute-start | bytes 61448 | tf_op jit(solution)/shard_map/ppermute | solution.py:879
  767.8 32.8 %collective-permute-start.39 = (bf16[64,2560]{1,0:T(8,128)(2,1)S(1)}, bf16[64,2560]{1,0:T(8,128)(2,1)S(1)}, u32[]{:S(2)}, u32[]{:S(2)}) collective-permute-start(bf16[64,2560]{1,0:T(8,128)(2,1)S(1)} %add_convert_fusion.16), channel_id=1, source_target_pairs={{0,16},{8,24},{16,0},{24,8},{1,17},{9,25},{17,1},{25,9},{2,18},{10... | collective-permute-start | bytes 983048 | tf_op jit(solution)/shard_map/ppermute | solution.py:879
  795.6 12.2 %collective-permute-start.42 = (bf16[64,1536]{1,0:T(8,128)(2,1)S(1)}, bf16[64,1536]{1,0:T(8,128)(2,1)S(1)}, u32[]{:S(2)}, u32[]{:S(2)}) collective-permute-start(bf16[64,1536]{1,0:T(8,128)(2,1)S(1)} %add_convert_fusion.18), channel_id=1, source_target_pairs={{0,16},{8,24},{16,0},{24,8},{1,17},{9,25},{17,1},{25,9},{2,18},{10... | collective-permute-start | bytes 589832 | tf_op jit(solution)/shard_map/ppermute | solution.py:879
  808.7 12.9 %collective-permute-start.44 = (bf16[64,2560]{1,0:T(8,128)(2,1)S(1)}, bf16[64,2560]{1,0:T(8,128)(2,1)S(1)}, u32[]{:S(2)}, u32[]{:S(2)}) collective-permute-start(bf16[64,2560]{1,0:T(8,128)(2,1)S(1)} %add_convert_fusion.15), channel_id=1, source_target_pairs={{0,8},{8,0},{16,24},{24,16},{1,9},{9,1},{17,25},{25,17},{2,10},{10... | collective-permute-start | bytes 983048 | tf_op jit(solution)/shard_map/ppermute | solution.py:879
  (77 other events, 594.4 us)
Sparse Core Ops, SparseCore 0:
  53.6 59.6 all-gather.5
  115.2 89.8 all-gather.7
  207.0 89.8 all-gather.9
  300.3 115.9 reduce-scatter.2
  419.7 152.5 reduce-scatter.4

commit v3 on v2

--- a/solution.py
+++ b/solution.py
@@ -70,6 +70,7 @@
 
 
 WHOLE = ((None, 0, 4 * D),)
+WHOLE_ROWS = ((None, 0, D),)
 
 
 def shard_rows(me, rank, rows_each):
@@ -640,33 +641,25 @@
     )(*deps, a, go, w1, b1)
 
 
-def row_tile_copies(layout, parts, step, slot, weights, sems, act):
-    for number, ((rank, first, count), part_ref) in enumerate(zip(layout, parts)):
+def row_tile_copies(me, layout, parts, step, slot, weights, sems):
+    for (rank, first, count), part_ref in zip(layout, parts):
+        target = weights.at[slot, pl.ds(first, count), :]
         if rank is None:
-            rows = pl.ds(pl.multiple_of(step * TILE, TILE), TILE)
-            act(pltpu.make_async_copy(part_ref.at[rows, :], weights.at[slot], sems.at[slot]))
-            continue
-        low = (rank * D + first) // TILE
-
-        @pl.when((step >= low) & (step < low + count // TILE))
-        def _(part_ref=part_ref, low=low):
-            rows = pl.ds(pl.multiple_of((step - low) * TILE, TILE), TILE)
-            act(pltpu.make_async_copy(part_ref.at[rows, :], weights.at[slot], sems.at[slot]))
-
-
-def tile_of(step, scalars, layout):
-    if layout[0][0] is None:
-        return step
-    per_shard = D // TILE
-    return place(scalars[0], step // per_shard) * per_shard + step % per_shard
-
-
-def start_copy(copy):
-    copy.start()
-
-
-def wait_copy(copy):
-    copy.wait()
+            rows = pl.ds(pl.multiple_of(place(me, step) * count, count), count)
+            pltpu.make_async_copy(part_ref.at[rows, :], target, sems.at[slot]).start()
+        else:
+
+            @pl.when(step == rank)
+            def _(part_ref=part_ref, target=target):
+                pltpu.make_async_copy(part_ref, target, sems.at[slot]).start()
+
+
+def wait_tile(slot, weights, sems):
+    pltpu.make_async_copy(weights.at[slot], weights.at[slot], sems.at[slot]).wait()
+
+
+def tile_of(step, scalars):
+    return place(scalars[0], step)
 
 
 def mlp_down_body(layout, below_layout, steps, *refs):
@@ -684,7 +677,7 @@
 
     @pl.when(step == 0)
     def _():
-        row_tile_copies(layout, parts, 0, 0, w2, sems, start_copy)
+        row_tile_copies(me, layout, parts, 0, 0, w2, sems)
         da[...] = jnp.zeros_like(da)
 
     @pl.when(step == 1)
@@ -694,9 +687,9 @@
 
     @pl.when(step < steps - 1)
     def _():
-        row_tile_copies(layout, parts, step + 1, 1 - slot, w2, sems, start_copy)
-
-    row_tile_copies(((None, 0, 0),), [parts[0]], 0, slot, w2, sems, wait_copy)
+        row_tile_copies(me, layout, parts, step + 1, 1 - slot, w2, sems)
+
+    wait_tile(slot, w2, sems)
     grad_unit = (dot_t(go[...], w2[slot]) * slope[...].astype(F32)).astype(BF16)
     b1_sum[...] = jnp.sum(grad_unit.astype(F32), 0, keepdims=True)
     grad_w1[...] = dot(a_t[...], grad_unit).astype(BF16)
@@ -721,7 +714,7 @@
     ff = w1.shape[1]
     steps = ff // TILE
     layout, parts = held
-    tall = pl.BlockSpec((ROWS, TILE), lambda i, s: (0, tile_of(i, s, layout)))
+    tall = pl.BlockSpec((ROWS, TILE), lambda i, s: (0, tile_of(i, s)))
     out_shape = [shaped((D, ff)), shaped((1, ff), F32), shaped((ROWS, D), F32)]
     out_shape += [shaped((ROWS, D))] * 2 + [shaped((1, D), F32)] * 3
     return pl.pallas_call(
@@ -732,7 +725,7 @@
             in_specs=[ANY] * len(deps)
             + [whole((D, ROWS)), whole((ROWS, D)), tall, tall, ANY, whole((1, D))]
             + [ANY] * (len(parts) + len(below[1])),
-            out_specs=[tall, pl.BlockSpec((1, TILE), lambda i, s: (0, tile_of(i, s, layout)))]
+            out_specs=[tall, pl.BlockSpec((1, TILE), lambda i, s: (0, tile_of(i, s)))]
             + [whole(out.shape) for out in out_shape[2:]],
             scratch_shapes=[
                 pltpu.VMEM((ROWS, D), F32),
@@ -754,6 +747,7 @@
 def mlp_out_body(layout, steps, *refs):
     it = iter(refs)
     scalars = next(it)
+    me = scalars[0]
     active, x_hbm, vector = (next(it) for _ in range(3))
     parts = [next(it) for _ in layout]
     result = next(it)
@@ -763,7 +757,7 @@
 
     @pl.when(step == 0)
     def _():
-        row_tile_copies(layout, parts, 0, 0, w2, sems, start_copy)
+        row_tile_copies(me, layout, parts, 0, 0, w2, sems)
         acc[...] = jnp.zeros_like(acc)
 
     @pl.when(step == 1)
@@ -772,9 +766,9 @@
 
     @pl.when(step < steps - 1)
     def _():
-        row_tile_copies(layout, parts, step + 1, 1 - slot, w2, sems, start_copy)
-
-    row_tile_copies(((None, 0, 0),), [parts[0]], 0, slot, w2, sems, wait_copy)
+        row_tile_copies(me, layout, parts, step + 1, 1 - slot, w2, sems)
+
+    wait_tile(slot, w2, sems)
     acc[...] += dot(active[...], w2[slot])
 
     @pl.when(step == steps - 1)
@@ -794,7 +788,7 @@
             grid=(steps,),
             in_specs=[ANY] * len(deps)
             + [
-                pl.BlockSpec((ROWS, TILE), lambda i, s: (0, tile_of(i, s, layout))),
+                pl.BlockSpec((ROWS, TILE), lambda i, s: (0, tile_of(i, s))),
                 ANY,
                 whole((1, D)),
             ]
@@ -879,28 +873,19 @@
     return lax.ppermute(value, axis, [(i, i ^ bit) for i in range(size)])
 
 
-def add(left, right, zero):
-    return (left.astype(F32) + (right.astype(F32) + zero)).astype(BF16)
-
-
-def zero_of(token):
-    return token.reshape(-1)[0].astype(F32) * 0.0
-
-
-def held_back(value, token):
-    return value + zero_of(token).astype(value.dtype)
+def add(left, right):
+    return (left.astype(F32) + right.astype(F32)).astype(BF16)
 
 
 def spread(own, axis):
-    (by_x, by_y), zero = yield [(own, "shard", XBIT), (own, "shard", YBIT)]
-    zero = zero.astype(own.dtype)
+    by_x, by_y = yield [(own, "shard", XBIT), (own, "shard", YBIT)]
     size = own.shape[axis]
     half = size // 2
-    low = lax.slice_in_dim(by_x, 0, half, axis=axis) + zero
-    high = lax.slice_in_dim(by_y, half, size, axis=axis) + zero
+    low = lax.slice_in_dim(by_x, 0, half, axis=axis)
+    high = lax.slice_in_dim(by_y, half, size, axis=axis)
     far = [(low, "shard", YBIT), (high, "shard", XBIT)]
-    far, _ = yield far + [(v, "shard", CORE) for v in (own, by_x, by_y)]
-    last, _ = yield [(far[0], "shard", CORE), (far[1], "shard", CORE)]
+    far = yield far + [(v, "shard", CORE) for v in (own, by_x, by_y)]
+    last = yield [(far[0], "shard", CORE), (far[1], "shard", CORE)]
     layout = [(0, 0, size), (2, 0, size), (4, 0, size), (1, 0, size), (3, 0, size), (5, 0, size)]
     layout += [(6, 0, half), (6, half, half), (7, 0, half), (7, half, half)]
     return tuple(layout), [own, by_x, by_y, *far[2:], *far[:2], *last]
@@ -913,26 +898,26 @@
     odd = lax.axis_index("rep") % 2 == 1
     rows = value.shape[0] // 2
     low, high = value[:rows], value[rows:]
-    (got,), zero = yield [(jnp.where(odd, low, high), "rep", 1)]
-    total = add(jnp.where(odd, high, low), got, zero)
+    (got,) = yield [(jnp.where(odd, low, high), "rep", 1)]
+    total = add(jnp.where(odd, high, low), got)
     bit = 2
     while bit < copies:
-        (got,), zero = yield [(total, "rep", bit)]
-        total = add(total, got, zero)
+        (got,) = yield [(total, "rep", bit)]
+        total = add(total, got)
         bit *= 2
-    (other,), _ = yield [(total, "rep", 1)]
+    (other,) = yield [(total, "rep", 1)]
     return jnp.concatenate([jnp.where(odd, other, total), jnp.where(odd, total, other)], 0)
 
 
 def reduce(keep, send):
     half = keep.shape[2] // 2
-    (got,), zero = yield [(send, "shard", CORE)]
-    total = add(keep, got, zero)
+    (got,) = yield [(send, "shard", CORE)]
+    total = add(keep, got)
     sum_a, sum_b = total[..., :half], total[..., half:]
-    got, zero = yield [(sum_a[1::2], "shard", XBIT), (sum_b[2:], "shard", YBIT)]
-    half_a, half_b = add(sum_a[0::2], got[0], zero), add(sum_b[:2], got[1], zero)
-    got, zero = yield [(half_a[1], "shard", YBIT), (half_b[1], "shard", XBIT)]
-    owned = [add(half_a[0], got[0], zero), add(half_b[0], got[1], zero)]
+    got = yield [(sum_a[1::2], "shard", XBIT), (sum_b[2:], "shard", YBIT)]
+    half_a, half_b = add(sum_a[0::2], got[0]), add(sum_b[:2], got[1])
+    got = yield [(half_a[1], "shard", YBIT), (half_b[1], "shard", XBIT)]
+    owned = [add(half_a[0], got[0]), add(half_b[0], got[1])]
     owned = yield from over_copies(jnp.concatenate(owned, 1))
     return owned
 
@@ -941,10 +926,25 @@
     for axis in ("shard", "rep"):
         bit = 1
         while bit < lax.axis_size(axis):
-            (got,), zero = yield [(vector, axis, bit)]
-            vector = vector + (got + zero)
+            (got,) = yield [(vector, axis, bit)]
+            vector = vector + got
             bit *= 2
     return vector
+
+
+def tie_body(*_):
+    pass
+
+
+def tie(arrays, tokens):
+    return pl.pallas_call(
+        tie_body,
+        in_specs=[ANY] * (len(arrays) + len(tokens)),
+        out_specs=[ANY] * len(arrays),
+        out_shape=[shaped(a.shape, a.dtype) for a in arrays],
+        input_output_aliases={i: i for i in range(len(arrays))},
+        name="tie",
+    )(*arrays, *tokens)
 
 
 class Flow:
@@ -960,15 +960,22 @@
         self.deps += [array for array, _, _ in wanted]
         self.active[name] = (steps, [swap(*want) for want in wanted])
 
-    def meet(self, token, *names):
-        zero = zero_of(token)
-        for name in [n for n in names if n in self.active]:
+    def meet(self, tokens, *names, more=()):
+        names = [n for n in names if n in self.active]
+        held = [array for n in names for array in self.active[n][1]]
+        held = tie([*more, *held], tokens)
+        more, held = held[: len(more)], held[len(more) :]
+        self.deps += more
+        for name in names:
             steps, arrays = self.active[name]
+            arrays, held = held[: len(arrays)], held[len(arrays) :]
+            self.deps += arrays
             try:
-                self._request(name, steps, steps.send((arrays, zero)))
+                self._request(name, steps, steps.send(arrays))
             except StopIteration as end:
                 del self.active[name]
                 self.results[name] = end.value
+        return more
 
     def take(self):
         deps, self.deps = self.deps, []
@@ -1024,25 +1031,35 @@
     ff = fc_in.shape[1]
 
     gains, *vectors = gather_vectors(ln_gain, self_vec, cross_vec, mlp_vec)
-    own_one = held_back(jnp.concatenate([self_qkv, self_out], 1), gains)
-    flow.start("self", spread(own_one, 1))
-    by_x, by_y = flow.active["self"][1]
-    near = zero_of(by_x) + zero_of(by_y)
+    all_one = gather(jnp.concatenate([self_qkv, self_out], 1))
+    all_two = gather(jnp.concatenate([cross_qkv, cross_out], 1))
+    held_one, held_two = (WHOLE, [all_one]), (WHOLE, [all_two])
+    all_in = gather(fc_in)
+    rows = fc_out.shape[0] // 2
+    low_out = gather(fc_out[:rows])
+    flow.start("high", spread(fc_out[rows:], 0))
     encoded = encoder.reshape(ROWS, D)
     enc_t = encoded.T
     masks = (segments.reshape(ROWS, 1), segments.reshape(1, ROWS), pad_mask.reshape(1, ROWS))
     a_one, a_one_t, bias = prepare(hidden, gains[0], part(vectors[0], 0), masks)
     out_sum = jnp.sum(grad_out.astype(F32), 0)
-    while "self" in flow.active:
-        flow.meet(a_one_t, "self")
-    held_one = flow.results["self"]
-    all_two = gather(held_back(jnp.concatenate([cross_qkv, cross_out], 1), near))
-    all_in, all_out = gather(fc_in), gather(fc_out)
-    held_two, held_out = (WHOLE, [all_two]), (WHOLE, [all_out])
     flow.take()
+    flow.meet([a_one_t, enc_t], "high")
     x_one, a_two, a_two_t, *saved_one = attend_forward(
-        scalars, hidden, a_one, bias, forward_vectors(gains, vectors, 0), held_one
-    )
+        scalars,
+        hidden,
+        a_one,
+        bias,
+        forward_vectors(gains, vectors, 0),
+        held_one,
+        deps=flow.take(),
+    )
+    flow.meet([a_two], "high")
+    flow.meet([saved_one[4]], "high")
+    layout, high_parts = flow.results["high"]
+    layout = ((None, 0, rows),) + tuple((r, rows + first, count) for r, first, count in layout)
+    held_out = (layout, [low_out, *high_parts])
+    flow.take()
     x_two, a_three, a_three_t, *saved_two = attend_forward(
         scalars, x_one, a_two, encoded, forward_vectors(gains, vectors, 1), held_two
     )
@@ -1055,8 +1072,9 @@
     halves_two, *weights_two, q_two, v_two = attend_backward(
         scalars, 0, GROUPS, a_two_t, enc_t, ga_two, saved_two, gb_two, False
     )
+    (scattered_out,) = flow.meet([v_two], more=[scattered_out])
+    flow.start("out", over_copies(scattered_out))
     flow.start("cross", reduce(*weights_two))
-    flow.start("out", over_copies(held_back(scattered_out, v_two)))
     grad_one, gain_two, shift_two, grad_enc, out_one, gb_one, ga_one = project_back(
         scalars,
         [halves_two],
@@ -1067,57 +1085,38 @@
         held_one,
         deps=flow.take(),
     )
-    flow.meet(gain_two, "cross", "out")
+    flow.meet([gain_two], "cross", "out")
     early = [gain_three[0], shift_three[0], out_sum, sum_fc[0]]
     early += [gain_two[0], shift_two[0], q_two[0], v_two[0], out_two[0]]
     flow.start("early", sum_everywhere(jnp.concatenate(early)))
-    half = GROUPS // 2
-
-    def self_backward(index):
-        return attend_backward(
-            scalars,
-            index * half,
-            half,
-            a_one_t,
-            bias,
-            ga_one,
-            saved_one,
-            gb_one if index == 0 else None,
-            False,
-            deps=flow.take(),
-        )
-
-    grads_low, *weights, q_low, v_low = self_backward(0)
-    flow.meet(v_low, "cross", "early")
-    flow.start(("self", 0), reduce(*weights))
-    grads_high, *weights, q_high, v_high = self_backward(1)
-    flow.meet(v_high, "cross", "early", "out", ("self", 0))
-    flow.start(("self", 1), reduce(*weights))
-    flow.start("in", over_copies(held_back(scattered_in, v_high)))
+    grads_one, weights_one, q_one, v_one = attend_backward(
+        scalars,
+        0,
+        GROUPS,
+        a_one_t,
+        bias,
+        ga_one,
+        saved_one,
+        gb_one,
+        True,
+        deps=flow.take(),
+    )
+    (weights_one,) = flow.meet([v_one], "cross", "out", "early", more=[weights_one])
+    scattered_one = scattered(weights_one)
+    grad_hidden, gain_one, shift_one = project_back(
+        scalars, [grads_one], grad_one, hidden, gains[0], held_one, deps=flow.take()
+    )
+    (scattered_in,) = flow.meet([gain_one], "cross", "out", "early", more=[scattered_in])
+    flow.start("in", over_copies(scattered_in))
+    late = [gain_one[0], shift_one[0], q_one[0], v_one[0], out_one[0]]
+    flow.start("late", sum_everywhere(jnp.concatenate(late)))
     output = mlp_out(
         scalars, active, x_two, part(vectors[2], 1), held_out, deps=flow.take()
     )
-    flow.meet(output, *flow.active)
-    grad_hidden, gain_one, shift_one = project_back(
-        scalars, [grads_low, grads_high], grad_one, hidden, gains[0], held_one, deps=flow.take()
-    )
-    late = [gain_one[0], shift_one[0], q_low[0], q_high[0], v_low[0], v_high[0], out_one[0]]
-    flow.start("late", sum_everywhere(jnp.concatenate(late)))
-    token = gain_one
+    (scattered_one,) = flow.meet([output], "cross", "in", "early", "late", more=[scattered_one])
+    flow.start("self", over_copies(scattered_one[0]))
     while flow.active:
-        flow.take()
-        quick = [n for n in flow.active if n != "in"]
-        flow.meet(token, *quick)
-        deps = flow.take()
-        if "in" in flow.active:
-            if deps:
-                token = sum(zero_of(d) for d in deps)
-            flow.meet(token, "in")
-            deps += flow.take()
-        if deps:
-            token = sum(zero_of(d) for d in deps)
-    scale = factor
-    factor = factor + zero_of(gain_one)
+        flow.meet(flow.take(), *flow.active)
     done = flow.results
 
     def own(vector):
@@ -1132,9 +1131,9 @@
         grad_hidden,
         grad_enc.reshape(1, ROWS, D),
         grad_gain,
-        *join_heads([done[("self", 0)], done[("self", 1)]], scale),
+        *join_heads([done["self"]], factor),
         own(late[D:]),
-        *join_heads([done["cross"]], scale),
+        *join_heads([done["cross"]], factor),
         own(early[base + D :]),
         done["in"].astype(F32) * factor,
         done["out"].astype(F32) * factor,
@@ -1172,7 +1171,7 @@
     gains, *vectors = gather_vectors(ln_gain, self_vec, cross_vec, mlp_vec)
     held_one = (WHOLE, [gather(jnp.concatenate([self_qkv, self_out], 1))])
     held_two = (WHOLE, [gather(jnp.concatenate([cross_qkv, cross_out], 1))])
-    all_in, held_out = gather(fc_in), (WHOLE, [gather(fc_out)])
+    all_in, held_out = gather(fc_in), (WHOLE_ROWS, [gather(fc_out)])
     masks = (segments.reshape(ROWS, 1), segments.reshape(1, ROWS), pad_mask.reshape(1, ROWS))
     a_one, a_one_t, bias = prepare(hidden, gains[0], part(vectors[0], 0), masks)
     x_one, a_two, a_two_t, *saved_one = attend_forward(

time: 842 us -> 782 us (0.929)
  blocking collectives: 10.7 us -> 38.9 us
  local copies, waits for them, and re-layouts: 59.4 us -> 37.9 us
  other arithmetic: 71.6 us -> 51.3 us
  between operations: 32.4 us -> 16.3 us
  starting transfers between devices: 52.1 us -> 38.5 us
  waiting for transfers between devices: 197 us -> 186 us
    all_gather x1, blocking collectives: 10.7 us -> 38.9 us  [gather_vectors(): every = lax.all_gather(packed, 'shard').astype(F32)]
    slice x31 -> x5, local copies, waits for them, and re-layouts: 21.3 us -> 7.29 us  [the longest x2 2.07 us: reduce(): got = (yield [(sum_a[1::2], 'shard', XBIT), (sum_b[2:], 'shard', YBIT)])]
    ppermute x49 -> x36, starting transfers between devices: 51.9 us -> 38.2 us  [swap(): return lax.ppermute(value, axis, [(i, i ^ bit) for i in range(size)])]
    convert_element_type x25 -> x12, other arithmetic: 35.5 us -> 22 us  [add(): return (left.astype(F32) + right.astype(F32)).astype(BF16)]
    add x16 -> x10, other arithmetic: 13.4 us -> 2.65 us  [sum_everywhere(): vector = vector + got]
    all_gather x3 -> x4, waiting for transfers between devices: 63.9 us -> 56.4 us  [gather(): return lax.all_gather(value, 'shard', axis=0, tiled=True)]
    pallas_call x3 -> x2, Pallas kernels: 118 us -> 111 us  [attend_backward(): pl.pallas_call(skipping(functools.partial(attend_backward_body, cross, wi...]
    unnamed x170 -> x218, local copies, waits for them, and re-layouts: 23.3 us -> 25.5 us
  transfers between devices with their start and end apart: 54 -> 43, of which waited for: 15 -> 14; matrix products, arithmetic and copies ran while one was open for 14% -> 8% of each run, Pallas kernels for 49% -> 53%
where the time goes in v3:
time: 782 us; the launch traced here: 776 us
  Pallas kernels  408 us (52%)
  waiting for transfers between devices  186 us (24%)
  other arithmetic  51.3 us (7%)
  blocking collectives  38.9 us (5%)
  starting transfers between devices  38.5 us (5%)
  local copies, waits for them, and re-layouts  37.9 us (5%)
  between operations  16.3 us (2%)
    ppermute x36, waiting for transfers between devices, swap(): return lax.ppermute(value, axis, [(i, i ^ bit) for i in range(size)])  125 us
    pallas_call x2, Pallas kernels, attend_backward(): pl.pallas_call(skipping(functools.partial(attend_backward_body, cross, wi...  111 us
    pallas_call x2, Pallas kernels, attend_forward(): pl.pallas_call(skipping(functools.partial(attend_forward_body, cross, lay...  92.4 us
    pallas_call x1, Pallas kernels, mlp_down(): pl.pallas_call(skipping(functools.partial(mlp_down_body, layout, below[0]...  73.7 us
    all_gather x4, waiting for transfers between devices, gather(): return lax.all_gather(value, 'shard', axis=0, tiled=True)  56.4 us
    pallas_call x1, Pallas kernels, mlp_up(): pl.pallas_call(skipping(mlp_up_body, 0, len(deps)), grid=(ff // TILE,), i...  49.1 us
    pallas_call x2, Pallas kernels, project_back(): pl.pallas_call(skipping(functools.partial(project_back_body, layout, belo...  44.5 us
    all_gather x1, blocking collectives, gather_vectors(): every = lax.all_gather(packed, 'shard').astype(F32)  38.9 us
  transfers between devices with their start and end apart: 43, of which 14 were waited for; matrix products, arithmetic and copies ran while one was open for 8% of the time, Pallas kernels for 53%

profile of v3, /device:TPU:0, one launch (start us, length us, event | category | flops | bytes accessed | tf_op | source)
XLA Modules:
  0.0 776.3 jit_solution(5456124220697526442)
XLA Ops:
  7.2 2.3 pad_maximum_fusion
  13.9 3.0 collective-permute-start
  18.4 38.9 %all-gather.1 = bf16[8,1,2688]{2,1,0:T(2,128)(2,1)S(1)} all-gather(bf16[1,1,2688]{2,1,0:T(2,128)(2,1)S(1)} %reshape.90), channel_id=2, replica_groups=mesh['rep'=4,'shard'=8] {'shard'}, dimensions={0}, use_global_device_ids=true | all-gather | bytes 48384 | tf_op jit(solution)/shard_map/all_gather | solution.py:836
  58.5 3.9 copy.75
  65.0 6.9 prepare.1
  74.6 1.9 slice.151.refs_3_
  76.5 1.9 slice.152.refs_4_
  79.1 44.7 %self_forward.1 = (f32[1024,1024]{1,0:T(8,128)}, bf16[1024,1024]{1,0:T(8,128)(2,1)}, bf16[1024,1024]{1,0:T(8,128)(2,1)}, bf16[1024,1024]{1,0:T(8,128)(2,1)}, bf1...) custom-call(s32[2]{0:T(128)} %pad_add_fusion.refs_0_, ...), custom_call_target="tpu_custom_call" | custom-call | flops 25769803776 | bytes 30000000 | tf_op jit(solution)/shard_map/self_forward/pallas_call | solution.py:269
  123.7 11.7 %all-gather.9.cloned.1.call-done.refs_9_.refs_18_.refs_8_ = bf16[1024,4096]{1,0:T(8,128)(2,1)} async-done(((bf16[128,4096]{1,0:T(8,128)(2,1)}), bf16[1024,4096]{1,0:T(8,128)(2,1)}) %all-gather.9.cloned.1.call-update) | async-done | bytes 8388624 | tf_op jit(solution)/shard_map/all_gather | solution.py:1001
  135.4 47.8 %cross_forward.1 = (f32[1024,1024]{1,0:T(8,128)}, bf16[1024,1024]{1,0:T(8,128)(2,1)}, bf16[1024,1024]{1,0:T(8,128)(2,1)}, bf16[1024,1024]{1,0:T(8,128)(2,1)}, bf...) custom-call(s32[2]{0:T(128)} %pad_add_fusion.refs_0_, ...), custom_call_target="tpu_custom_call" | custom-call | flops 25769803776 | bytes 30000000 | tf_op jit(solution)/shard_map/cross_forward/pallas_call | solution.py:269
  183.1 44.0 %all-gather.11.cloned.1.call-done.refs_2_.refs_4_ = bf16[1024,8192]{1,0:T(8,128)(2,1)} async-done(((bf16[128,8192]{1,0:T(8,128)(2,1)}), bf16[1024,8192]{1,0:T(8,128)(2,1)}) %all-gather.11.cloned.1.call-update) | async-done | bytes 16777232 | tf_op jit(solution)/shard_map/all_gather | solution.py:1001
  227.2 49.1 %mlp_up.1 = (bf16[1024,8192]{1,0:T(8,128)(2,1)}, bf16[1024,8192]{1,0:T(8,128)(2,1)}, bf16[8192,1024]{1,0:T(8,128)(2,1)}) custom-call(bf16[1024,1024]{1,0:T(8,128)(2,1)} %get-tuple-element.112.refs_0_, bf16[1024,1024]{1,0:T(8,128)(2,1)} %refs_2_.1, bf16[1024,8192]{1,0:T(8,128)(2,1)} %all-gather.11.cloned.1.call-done.refs_2_.refs_4_, f32[1,8192]{1,0:T(1,128)} %slice.207.refs_3_), custom_call_target="tpu_custom_call" | custom-call | flops 34359738368 | bytes 60000000 | tf_op jit(solution)/shard_map/mlp_up/pallas_call | solution.py:626
  280.4 12.7 %collective-permute-done.2.__0_ = bf16[256,1024]{1,0:T(8,128)(2,1)S(1)} collective-permute-done((bf16[256,1024]{1,0:T(8,128)(2,1)}, bf16[256,1024]{1,0:T(8,128)(2,1)S(1)}, u32[]{:S(2)}, u32[]{:S(2)}) %collective-permute-start.2) | collective-permute-done | bytes 524320 | tf_op jit(solution)/shard_map/ppermute | solution.py:873
  295.5 2.0 collective-permute-done.7.__0_
  299.8 73.7 %mlp_down.1 = (bf16[1024,8192]{1,0:T(8,128)(2,1)}, f32[1,8192]{1,0:T(1,128)}, f32[1024,1024]{1,0:T(8,128)}, bf16[1024,1024]{1,0:T(8,128)(2,1)}, bf16[1024,1024]{...) custom-call(s32[2]{0:T(128)} %pad_add_fusion.refs_0_, ...), custom_call_target="tpu_custom_call" | custom-call | flops 51539607552 | bytes 60000000 | tf_op jit(solution)/shard_map/mlp_down/pallas_call | solution.py:720
  373.5 61.3 %cross_backward.1 = (bf16[1024,3072]{1,0:T(8,128)(2,1)}, bf16[4,128,4096]{2,1,0:T(8,128)(2,1)}, bf16[4,128,4096]{2,1,0:T(8,128)(2,1)}, f32[1,1024]{1,0:T(1,128)}, f32[1,1024]{1,0:T(1,128)}) custom-call(s32[2]{0:T(128)} %pad_add_fusion.refs_0_, bf16[1024,1024]{1,0:T(8,128)(2,1)} %get-tuple-element.124.refs_1_, bf16[1024,1024]{1,0:T(8,128)(2,1)} %bitcast.71, ...), custom_call_target="tpu_custom_call" | custom-call | flops 45097156608 | bytes 20000000 | tf_op jit(solution)/shard_map/cross_backward/pallas_call | solution.py:465
  435.1 2.1 convert_reduce_fusion
  438.9 1.8 collective-permute-start.10
  440.7 24.8 %cross_project.1 = (f32[1024,1024]{1,0:T(8,128)}, f32[1,1024]{1,0:T(1,128)}, f32[1,1024]{1,0:T(1,128)}, bf16[1024,1024]{1,0:T(8,128)(2,1)}, f32[1,1024]{1,0:T(1,...) custom-call(s32[2]{0:T(128)} %pad_add_fusion.refs_0_, bf16[1024,1024]{1,0:T(8,128)(2,1)} %tie.15.refs_1_, ...), custom_call_target="tpu_custom_call" | custom-call | flops 8589934592 | bytes 30000000 | tf_op jit(solution)/shard_map/cross_project/pallas_call | solution.py:585
  467.6 5.2 add_convert_fusion
  473.0 1.9 copy-done.2
  478.0 3.0 add_convert_fusion.6.refs_5_
  481.0 2.4 collective-permute-start.13
  485.9 49.3 %self_backward.1 = (bf16[1024,3072]{1,0:T(8,128)(2,1)}, bf16[8,128,4096]{2,1,0:T(8,128)(2,1)}, f32[1,1024]{1,0:T(1,128)}, f32[1,1024]{1,0:T(1,128)}) custom-call(s32[2]{0:T(128)} %pad_add_fusion.refs_0_, bf16[4,128,4096]{2,1,0:T(8,128)(2,1)} %get-tuple-element.139.refs_1_, bf16[2,128,2048]{2,1,0:T(8,128)(2,1)} %slice.171.refs_2_, ...), custom_call_target="tpu_custom_call" | custom-call | flops 45097156608 | bytes 20000000 | tf_op jit(solution)/shard_map/self_backward/pallas_call | solution.py:465
  540.4 2.1 add_convert_fusion.4
  547.4 19.7 %self_project.1 = (bf16[1024,1024]{1,0:T(8,128)(2,1)}, f32[1,1024]{1,0:T(1,128)}, f32[1,1024]{1,0:T(1,128)}) custom-call(s32[2]{0:T(128)} %pad_add_fusion.refs_0_, bf16[8,128,4096]{2,1,0:T(8,128)(2,1)} %get-tuple-element.159.refs_1_, bf16[2,128,2048]{2,1,0:T(8,128)(2,1)} %get-tuple-element.155.refs_2_, bf16[2,128,2048]{2,1,0:T(8,128)(2,1)} %get-tuple-element.156.refs_3_, ...), custom_call_target="tpu_custom_call" | custom-call | flops 6442450944 | bytes 30000000 | tf_op jit(solution)/shard_map/self_project/pallas_call | solution.py:585
  570.3 2.6 broadcast_select_fusion.2.refs_8_
  572.9 1.7 collective-permute-start.20
  579.0 25.4 %mlp_out.1.__5_ = bf16[1024,1024]{1,0:T(8,128)(2,1)} custom-call(s32[2]{0:T(128)} %pad_add_fusion.refs_0_, bf16[128,8192]{1,0:T(8,128)(2,1)} %get-tuple-element.163.refs_1_, bf16[128,2048]{1,0:T(8,128)(2,1)} %get-tuple-element.164.refs_2_, bf16[128,2048]{1,0:T(8,128)(2,1)} %get-tuple-element.165.refs_3_, bf16[64,4096]{1,0:T(8,128)(2,1)} %broadcast_select_fusion.10.refs_4_, ...), custom_call_target="tpu_custom_call" | custom-call | flops 17179869184 | bytes 40000000 | tf_op jit(solution)/shard_map/mlp_out/pallas_call | solution.py:784
  604.4 5.6 collective-permute-done.19.__1_
  610.0 3.8 reduce-scatter.8.cloned.1.call-done.__0_
  613.8 1.7 add_convert_fusion.2.__9_
  615.6 2.5 collective-permute-start.25
  620.4 2.0 add_convert_fusion.9.__7_
  625.0 2.4 collective-permute-done.26.__3_
  627.5 37.0 %collective-permute-done.24.__1_ = f32[16384]{0:T(1024)S(1)} collective-permute-done((f32[16384]{0:T(1024)S(1)}, f32[16384]{0:T(1024)S(1)}, u32[]{:S(2)}, u32[]{:S(2)}) %collective-permute-start.24) | collective-permute-done | bytes 65568 | tf_op jit(solution)/shard_map/ppermute | solution.py:873
  664.4 22.1 %collective-permute-done.23.__0_ = bf16[64,4096]{1,0:T(8,128)(2,1)} collective-permute-done((bf16[64,4096]{1,0:T(8,128)(2,1)}, bf16[64,4096]{1,0:T(8,128)(2,1)}, u32[]{:S(2)}, u32[]{:S(2)}) %collective-permute-start.23) | collective-permute-done | bytes 524320 | tf_op jit(solution)/shard_map/ppermute | solution.py:873
  689.5 3.7 collective-permute-start.30
  698.6 2.6 convert_multiply_fusion
  701.3 33.6 %collective-permute-done.29.__1_ = f32[16384]{0:T(1024)S(1)} collective-permute-done((f32[16384]{0:T(1024)S(1)}, f32[16384]{0:T(1024)S(1)}, u32[]{:S(2)}, u32[]{:S(2)}) %collective-permute-start.29) | collective-permute-done | bytes 65568 | tf_op jit(solution)/shard_map/ppermute | solution.py:873
  734.9 3.6 collective-permute-done.28.__0_
  741.2 1.8 broadcast_select_fusion.1
  744.3 1.9 collective-permute-start.34
  746.5 2.5 convert_multiply_fusion.1
  751.5 2.7 join_heads.3
  754.2 4.0 collective-permute-done.33.__0_
  760.9 1.9 collective-permute-start.35
  763.9 2.7 join_heads.2
  (358 shorter events, 74.6 us)
Async XLA Ops:
  7.2 71.9 %all-gather.7.cloned.1.call-start = ((), (), s32[]{:S(2)}) async-start(), calls=%async_computation.3 | async-start | bytes 9437184 | tf_op jit(solution)/shard_map/all_gather | solution.py:1001
  9.6 125.8 %all-gather.9.cloned.1.call-start = ((), (), s32[]{:S(2)}) async-start(), calls=%async_computation.4 | async-start | bytes 9437184 | tf_op jit(solution)/shard_map/all_gather | solution.py:1001
  10.7 216.4 %all-gather.11.cloned.1.call-start = ((), (), s32[]{:S(2)}) async-start(), calls=%async_computation.5 | async-start | bytes 18874368 | tf_op jit(solution)/shard_map/all_gather | solution.py:1001
  11.5 288.2 %all-gather.13.cloned.1.call-start = ((), (), s32[]{:S(2)}) async-start(), calls=%async_computation.6 | async-start | bytes 9437184 | tf_op jit(solution)/shard_map/all_gather | solution.py:1001
  13.8 423.4 %reduce-scatter.6.cloned.1.call-start = ((), (), s32[]{:S(2)}) async-start(), calls=%async_computation.8 | async-start | bytes 18874368 | tf_op jit(solution)/shard_map/reduce_scatter | solution.py:1005
  13.9 59.8 %collective-permute-start = (bf16[512,1024]{1,0:T(8,128)(2,1)}, bf16[512,1024]{1,0:T(8,128)(2,1)S(1)}, u32[]{:S(2)}, u32[]{:S(2)}) collective-permute-start(bf16[512,1024]{1,0:T(8,128)(2,1)} %get-tuple-element.200.refs_5_.refs_8_.refs_14_), channel_id=1, source_target_pairs={{0,2},{1,3},{2,0},{3,1},{4,6},{5,7},{6,4},{7,5},{8,10},{9,11},{10,... | collective-permute-start | bytes 3145736 | tf_op jit(solution)/shard_map/ppermute | solution.py:873
  16.9 56.8 %collective-permute-start.1 = (bf16[512,1024]{1,0:T(8,128)(2,1)}, bf16[512,1024]{1,0:T(8,128)(2,1)}, u32[]{:S(2)}, u32[]{:S(2)}) collective-permute-start(bf16[512,1024]{1,0:T(8,128)(2,1)} %get-tuple-element.200.refs_5_.refs_8_.refs_14_), channel_id=1, source_target_pairs={{0,4},{1,5},{2,6},{3,7},{4,0},{5,1},{6,2},{7,3},{8,12},{9,13},{10,... | collective-permute-start | bytes 3145736 | tf_op jit(solution)/shard_map/ppermute | solution.py:873
  276.3 292.3 %reduce-scatter.4.cloned.1.call-start = ((), (), s32[]{:S(2)}) async-start(), calls=%async_computation.7 | async-start | bytes 18874368 | tf_op jit(solution)/shard_map/reduce_scatter | solution.py:1005
  277.5 2.9 collective-permute-start.4
  277.9 15.3 %collective-permute-start.5 = (bf16[512,1024]{1,0:T(8,128)(2,1)S(1)}, bf16[512,1024]{1,0:T(8,128)(2,1)S(1)}, u32[]{:S(2)}, u32[]{:S(2)}) collective-permute-start(bf16[512,1024]{1,0:T(8,128)(2,1)S(1)} %copy-done.37), channel_id=1, source_target_pairs={{0,1},{1,0},{2,3},{3,2},{4,5},{5,4},{6,7},{7,6},{8,9},{9,8},{10,11... | collective-permute-start | bytes 3145736 | tf_op jit(solution)/shard_map/ppermute | solution.py:873
  278.2 16.8 %collective-permute-start.6 = (bf16[512,1024]{1,0:T(8,128)(2,1)}, bf16[512,1024]{1,0:T(8,128)(2,1)}, u32[]{:S(2)}, u32[]{:S(2)}) collective-permute-start(bf16[512,1024]{1,0:T(8,128)(2,1)} %get-tuple-element.106.refs_2_.refs_7_.refs_10_.refs_16_), channel_id=1, source_target_pairs={{0,1},{1,0},{2,3},{3,2},{4,5},{5,4},{6,7},{7,6},{8,9},{9,8},{10,11... | collective-permute-start | bytes 3145736 | tf_op jit(solution)/shard_map/ppermute | solution.py:873
  278.4 14.7 %collective-permute-start.2 = (bf16[256,1024]{1,0:T(8,128)(2,1)}, bf16[256,1024]{1,0:T(8,128)(2,1)S(1)}, u32[]{:S(2)}, u32[]{:S(2)}) collective-permute-start(bf16[256,1024]{1,0:T(8,128)(2,1)} %slice.151.refs_3_), channel_id=1, source_target_pairs={{0,4},{1,5},{2,6},{3,7},{4,0},{5,1},{6,2},{7,3},{8,12},{9,13},{10,... | collective-permute-start | bytes 1572872 | tf_op jit(solution)/shard_map/ppermute | solution.py:873
  279.2 14.0 %collective-permute-start.3 = (bf16[256,1024]{1,0:T(8,128)(2,1)}, bf16[256,1024]{1,0:T(8,128)(2,1)S(1)}, u32[]{:S(2)}, u32[]{:S(2)}) collective-permute-start(bf16[256,1024]{1,0:T(8,128)(2,1)} %slice.152.refs_4_), channel_id=1, source_target_pairs={{0,2},{1,3},{2,0},{3,1},{4,6},{5,7},{6,4},{7,5},{8,10},{9,11},{10,... | collective-permute-start | bytes 1572872 | tf_op jit(solution)/shard_map/ppermute | solution.py:873
  295.0 2.5 collective-permute-start.7
  295.0 4.0 collective-permute-start.8
  373.4 240.3 %reduce-scatter.8.cloned.1.call-start = ((), (), s32[]{:S(2)}) async-start(), calls=%async_computation.9 | async-start | bytes 9437184 | tf_op jit(solution)/shard_map/reduce_scatter | solution.py:1005
  434.8 32.2 %collective-permute-start.9 = (bf16[4,128,4096]{2,1,0:T(8,128)(2,1)}, bf16[4,128,4096]{2,1,0:T(8,128)(2,1)}, u32[]{:S(2)}, u32[]{:S(2)}) collective-permute-start(bf16[4,128,4096]{2,1,0:T(8,128)(2,1)} %get-tuple-element.133.refs_3_), channel_id=1, source_target_pairs={{0,1},{1,0},{2,3},{3,2},{4,5},{5,4},{6,7},{7,6},{8,9},{9,8},{10,11... | collective-permute-start | bytes 12582920 | tf_op jit(solution)/shard_map/ppermute | solution.py:873
  438.9 28.1 %collective-permute-start.10 = (bf16[512,1024]{1,0:T(8,128)(2,1)S(1)}, bf16[512,1024]{1,0:T(8,128)(2,1)}, u32[]{:S(2)}, u32[]{:S(2)}) collective-permute-start(bf16[512,1024]{1,0:T(8,128)(2,1)S(1)} %broadcast_select_fusion.5.refs_2_), channel_id=1, source_target_pairs={{0,8},{8,0},{16,24},{24,16},{1,9},{9,1},{17,25},{25,17},{2,10},{10... | collective-permute-start | bytes 3145736 | tf_op jit(solution)/shard_map/ppermute | solution.py:873
  467.0 68.3 %collective-permute-start.14 = (f32[16384]{0:T(1024)S(1)}, f32[16384]{0:T(1024)S(1)}, u32[]{:S(2)}, u32[]{:S(2)}) collective-permute-start(f32[16384]{0:T(1024)S(1)} %constant_dynamic-update-slice_fusion.8.refs_6_), channel_id=1, source_target_pairs={{0,1},{1,0},{2,3},{3,2},{4,5},{5,4},{6,7},{7,6},{8,9},{9,8},{10,11... | collective-permute-start | bytes 196616 | tf_op jit(solution)/shard_map/ppermute | solution.py:873
  481.0 54.3 %collective-permute-start.13 = (bf16[512,1024]{1,0:T(8,128)(2,1)}, bf16[512,1024]{1,0:T(8,128)(2,1)S(1)}, u32[]{:S(2)}, u32[]{:S(2)}) collective-permute-start(bf16[512,1024]{1,0:T(8,128)(2,1)} %add_convert_fusion.6.refs_5_), channel_id=1, source_target_pairs={{0,16},{8,24},{16,0},{24,8},{1,17},{9,25},{17,1},{25,9},{2,18},{10... | collective-permute-start | bytes 3145736 | tf_op jit(solution)/shard_map/ppermute | solution.py:873
  483.4 51.9 %collective-permute-start.11 = (bf16[2,128,2048]{2,1,0:T(8,128)(2,1)}, bf16[2,128,2048]{2,1,0:T(8,128)(2,1)}, u32[]{:S(2)}, u32[]{:S(2)}) collective-permute-start(bf16[2,128,2048]{2,1,0:T(8,128)(2,1)} %slice.171.refs_2_), channel_id=1, source_target_pairs={{0,2},{1,3},{2,0},{3,1},{4,6},{5,7},{6,4},{7,5},{8,10},{9,11},{10,... | collective-permute-start | bytes 3145736 | tf_op jit(solution)/shard_map/ppermute | solution.py:873
  484.9 50.4 %collective-permute-start.12 = (bf16[2,128,2048]{2,1,0:T(8,128)(2,1)}, bf16[2,128,2048]{2,1,0:T(8,128)(2,1)}, u32[]{:S(2)}, u32[]{:S(2)}) collective-permute-start(bf16[2,128,2048]{2,1,0:T(8,128)(2,1)} %slice.211.refs_3_), channel_id=1, source_target_pairs={{0,4},{1,5},{2,6},{3,7},{4,0},{5,1},{6,2},{7,3},{8,12},{9,13},{10,... | collective-permute-start | bytes 3145736 | tf_op jit(solution)/shard_map/ppermute | solution.py:873
  537.1 31.5 %collective-permute-start.18 = (f32[16384]{0:T(1024)S(1)}, f32[16384]{0:T(1024)S(1)}, u32[]{:S(2)}, u32[]{:S(2)}) collective-permute-start(f32[16384]{0:T(1024)S(1)} %add.100.refs_9_), channel_id=1, source_target_pairs={{0,2},{1,3},{2,0},{3,1},{4,6},{5,7},{6,4},{7,5},{8,10},{9,11},{10,... | collective-permute-start | bytes 196616 | tf_op jit(solution)/shard_map/ppermute | solution.py:873
  539.9 28.8 %collective-permute-start.17 = (bf16[512,1024]{1,0:T(8,128)(2,1)S(1)}, bf16[512,1024]{1,0:T(8,128)(2,1)}, u32[]{:S(2)}, u32[]{:S(2)}) collective-permute-start(bf16[512,1024]{1,0:T(8,128)(2,1)S(1)} %add_convert_fusion.3.refs_7_), channel_id=1, source_target_pairs={{0,8},{8,0},{16,24},{24,16},{1,9},{9,1},{17,25},{25,17},{2,10},{10... | collective-permute-start | bytes 3145736 | tf_op jit(solution)/shard_map/ppermute | solution.py:873
  542.5 26.1 %collective-permute-start.16 = (bf16[128,2048]{1,0:T(8,128)(2,1)S(1)}, bf16[128,2048]{1,0:T(8,128)(2,1)}, u32[]{:S(2)}, u32[]{:S(2)}) collective-permute-start(bf16[128,2048]{1,0:T(8,128)(2,1)S(1)} %slice_bitcast_fusion.2.refs_5_), channel_id=1, source_target_pairs={{0,2},{1,3},{2,0},{3,1},{4,6},{5,7},{6,4},{7,5},{8,10},{9,11},{10,... | collective-permute-start | bytes 1572872 | tf_op jit(solution)/shard_map/ppermute | solution.py:873
  546.1 22.5 %collective-permute-start.15 = (bf16[128,2048]{1,0:T(8,128)(2,1)}, bf16[128,2048]{1,0:T(8,128)(2,1)}, u32[]{:S(2)}, u32[]{:S(2)}) collective-permute-start(bf16[128,2048]{1,0:T(8,128)(2,1)} %slice_bitcast_fusion.3.refs_4_), channel_id=1, source_target_pairs={{0,4},{1,5},{2,6},{3,7},{4,0},{5,1},{6,2},{7,3},{8,12},{9,13},{10,... | collective-permute-start | bytes 1572872 | tf_op jit(solution)/shard_map/ppermute | solution.py:873
  568.5 35.9 %collective-permute-start.22 = (f32[5120]{0:T(1024)S(1)}, f32[5120]{0:T(1024)S(1)}, u32[]{:S(2)}, u32[]{:S(2)}) collective-permute-start(f32[5120]{0:T(1024)S(1)} %constant_dynamic-update-slice_fusion.13.refs_9_), channel_id=1, source_target_pairs={{0,1},{1,0},{2,3},{3,2},{4,5},{5,4},{6,7},{7,6},{8,9},{9,8},{10,11... | collective-permute-start | bytes 61448 | tf_op jit(solution)/shard_map/ppermute | solution.py:873
  572.9 37.0 %collective-permute-start.20 = (bf16[64,8192]{1,0:T(8,128)(2,1)}, bf16[64,8192]{1,0:T(8,128)(2,1)}, u32[]{:S(2)}, u32[]{:S(2)}) collective-permute-start(bf16[64,8192]{1,0:T(8,128)(2,1)} %broadcast_select_fusion.2.refs_8_), channel_id=1, source_target_pairs={{0,8},{8,0},{16,24},{24,16},{1,9},{9,1},{17,25},{25,17},{2,10},{10... | collective-permute-start | bytes 3145736 | tf_op jit(solution)/shard_map/ppermute | solution.py:873
  578.0 31.9 %collective-permute-start.19 = (bf16[64,4096]{1,0:T(8,128)(2,1)}, bf16[64,4096]{1,0:T(8,128)(2,1)}, u32[]{:S(2)}, u32[]{:S(2)}) collective-permute-start(bf16[64,4096]{1,0:T(8,128)(2,1)} %broadcast_select_fusion.10.refs_4_), channel_id=1, source_target_pairs={{0,8},{8,0},{16,24},{24,16},{1,9},{9,1},{17,25},{25,17},{2,10},{10... | collective-permute-start | bytes 1572872 | tf_op jit(solution)/shard_map/ppermute | solution.py:873
  578.3 26.1 %collective-permute-start.21 = (f32[16384]{0:T(1024)S(1)}, f32[16384]{0:T(1024)S(1)}, u32[]{:S(2)}, u32[]{:S(2)}) collective-permute-start(f32[16384]{0:T(1024)S(1)} %add.103.refs_7_), channel_id=1, source_target_pairs={{0,4},{1,5},{2,6},{3,7},{4,0},{5,1},{6,2},{7,3},{8,12},{9,13},{10,... | collective-permute-start | bytes 196616 | tf_op jit(solution)/shard_map/ppermute | solution.py:873
  615.5 71.0 %copy-start.9 = (bf16[64,8192]{1,0:T(8,128)(2,1)}, bf16[64,8192]{1,0:T(8,128)(2,1)S(1)}, u32[]{:S(2)}) copy-start(bf16[64,8192]{1,0:T(8,128)(2,1)S(1)} %add_convert_fusion.2.__9_) | copy-start | bytes 3145732
  615.6 70.9 %collective-permute-start.25 = (bf16[64,8192]{1,0:T(8,128)(2,1)S(1)}, bf16[64,8192]{1,0:T(8,128)(2,1)S(1)}, u32[]{:S(2)}, u32[]{:S(2)}) collective-permute-start(bf16[64,8192]{1,0:T(8,128)(2,1)S(1)} %add_convert_fusion.2.__9_), channel_id=1, source_target_pairs={{0,16},{8,24},{16,0},{24,8},{1,17},{9,25},{17,1},{25,9},{2,18},{10... | collective-permute-start | bytes 3145736 | tf_op jit(solution)/shard_map/ppermute | solution.py:873
  618.9 45.5 %collective-permute-start.27 = (bf16[64,4096]{1,0:T(8,128)(2,1)}, bf16[64,4096]{1,0:T(8,128)(2,1)}, u32[]{:S(2)}, u32[]{:S(2)}) collective-permute-start(bf16[64,4096]{1,0:T(8,128)(2,1)} %select_bitcast_fusion.__14_), channel_id=1, source_target_pairs={{0,8},{8,0},{16,24},{24,16},{1,9},{9,1},{17,25},{25,17},{2,10},{10... | collective-permute-start | bytes 1572872 | tf_op jit(solution)/shard_map/ppermute | solution.py:873
  622.4 64.1 %collective-permute-start.23 = (bf16[64,4096]{1,0:T(8,128)(2,1)}, bf16[64,4096]{1,0:T(8,128)(2,1)}, u32[]{:S(2)}, u32[]{:S(2)}) collective-permute-start(bf16[64,4096]{1,0:T(8,128)(2,1)} %add_convert_fusion.9.__7_), channel_id=1, source_target_pairs={{0,16},{8,24},{16,0},{24,8},{1,17},{9,25},{17,1},{25,9},{2,18},{10... | collective-permute-start | bytes 1572872 | tf_op jit(solution)/shard_map/ppermute | solution.py:873
  623.0 63.6 %copy-start.54 = (f32[16384]{0:T(1024)}, f32[16384]{0:T(1024)S(1)}, u32[]{:S(2)}) copy-start(f32[16384]{0:T(1024)S(1)} %add.106.__11_) | copy-start | bytes 196612
  623.0 41.5 %collective-permute-start.24 = (f32[16384]{0:T(1024)S(1)}, f32[16384]{0:T(1024)S(1)}, u32[]{:S(2)}, u32[]{:S(2)}) collective-permute-start(f32[16384]{0:T(1024)S(1)} %add.106.__11_), channel_id=1, source_target_pairs={{0,8},{8,0},{16,24},{24,16},{1,9},{9,1},{17,25},{25,17},{2,10},{10... | collective-permute-start | bytes 196616 | tf_op jit(solution)/shard_map/ppermute | solution.py:873
  623.6 62.9 %copy-start.67 = (f32[5120]{0:T(1024)}, f32[5120]{0:T(1024)S(1)}, u32[]{:S(2)}) copy-start(f32[5120]{0:T(1024)S(1)} %add.104.__13_) | copy-start | bytes 61444
  623.6 3.8 collective-permute-start.26
  625.0 62.5 %copy-start.4 = (bf16[1,128,4096]{2,1,0:T(8,128)(2,1)S(1)}, bf16[1,128,4096]{2,1,0:T(8,128)(2,1)}, u32[]{:S(2)}) copy-start(bf16[1,128,4096]{2,1,0:T(8,128)(2,1)} %get-tuple-element.178.__5_) | copy-start | bytes 3145732
  627.5 59.1 %copy-start.74 = (f32[5120]{0:T(1024)}, f32[5120]{0:T(1024)S(1)}, u32[]{:S(2)}) copy-start(f32[5120]{0:T(1024)S(1)} %collective-permute-done.26.__3_) | copy-start | bytes 61444
  688.9 46.0 %collective-permute-start.32 = (bf16[64,4096]{1,0:T(8,128)(2,1)S(1)}, bf16[64,4096]{1,0:T(8,128)(2,1)S(1)}, u32[]{:S(2)}, u32[]{:S(2)}) collective-permute-start(bf16[64,4096]{1,0:T(8,128)(2,1)S(1)} %fusion.__14_), channel_id=1, source_target_pairs={{0,16},{8,24},{16,0},{24,8},{1,17},{9,25},{17,1},{25,9},{2,18},{10... | collective-permute-start | bytes 1572872 | tf_op jit(solution)/shard_map/ppermute | solution.py:873
  689.5 49.8 %collective-permute-start.30 = (bf16[64,8192]{1,0:T(8,128)(2,1)S(1)}, bf16[64,8192]{1,0:T(8,128)(2,1)S(1)}, u32[]{:S(2)}, u32[]{:S(2)}) collective-permute-start(bf16[64,8192]{1,0:T(8,128)(2,1)S(1)} %add_convert_fusion.1.__10_), channel_id=1, source_target_pairs={{0,8},{8,0},{16,24},{24,16},{1,9},{9,1},{17,25},{25,17},{2,10},{10... | collective-permute-start | bytes 3145736 | tf_op jit(solution)/shard_map/ppermute | solution.py:873
  694.6 43.9 %collective-permute-start.28 = (bf16[64,4096]{1,0:T(8,128)(2,1)S(1)}, bf16[64,4096]{1,0:T(8,128)(2,1)S(1)}, u32[]{:S(2)}, u32[]{:S(2)}) collective-permute-start(bf16[64,4096]{1,0:T(8,128)(2,1)S(1)} %add_convert_fusion.8.__6_), channel_id=1, source_target_pairs={{0,8},{8,0},{16,24},{24,16},{1,9},{9,1},{17,25},{25,17},{2,10},{10... | collective-permute-start | bytes 1572872 | tf_op jit(solution)/shard_map/ppermute | solution.py:873
  696.4 4.9 collective-permute-start.31
  697.9 37.0 %collective-permute-start.29 = (f32[16384]{0:T(1024)S(1)}, f32[16384]{0:T(1024)S(1)}, u32[]{:S(2)}, u32[]{:S(2)}) collective-permute-start(f32[16384]{0:T(1024)S(1)} %add.110.__8_), channel_id=1, source_target_pairs={{0,16},{8,24},{16,0},{24,8},{1,17},{9,25},{17,1},{25,9},{2,18},{10... | collective-permute-start | bytes 196616 | tf_op jit(solution)/shard_map/ppermute | solution.py:873
  744.3 13.9 %collective-permute-start.34 = (bf16[64,4096]{1,0:T(8,128)(2,1)S(1)}, bf16[64,4096]{1,0:T(8,128)(2,1)S(1)}, u32[]{:S(2)}, u32[]{:S(2)}) collective-permute-start(bf16[64,4096]{1,0:T(8,128)(2,1)S(1)} %add_convert_fusion.7.__8_), channel_id=1, source_target_pairs={{0,8},{8,0},{16,24},{24,16},{1,9},{9,1},{17,25},{25,17},{2,10},{10... | collective-permute-start | bytes 1572872 | tf_op jit(solution)/shard_map/ppermute | solution.py:873
  746.2 12.0 %collective-permute-start.33 = (f32[5120]{0:T(1024)S(1)}, f32[5120]{0:T(1024)S(1)}, u32[]{:S(2)}, u32[]{:S(2)}) collective-permute-start(f32[5120]{0:T(1024)S(1)} %add.113.__6_), channel_id=1, source_target_pairs={{0,8},{8,0},{16,24},{24,16},{1,9},{9,1},{17,25},{25,17},{2,10},{10... | collective-permute-start | bytes 61448 | tf_op jit(solution)/shard_map/ppermute | solution.py:873
  760.9 5.6 collective-permute-start.35
  (96 other events, 641.2 us)
Sparse Core Ops, SparseCore 0:
  10.5 68.5 all-gather.6
  80.9 54.3 all-gather.8
  137.3 89.8 all-gather.10
  229.5 54.6 all-gather.12
  287.6 116.9 reduce-scatter.5
  408.0 129.5 reduce-scatter.3
  541.1 72.6 reduce-scatter.7

commit v4 on v3

--- a/solution.py
+++ b/solution.py
@@ -1106,14 +1106,16 @@
     grad_hidden, gain_one, shift_one = project_back(
         scalars, [grads_one], grad_one, hidden, gains[0], held_one, deps=flow.take()
     )
-    (scattered_in,) = flow.meet([gain_one], "cross", "out", "early", more=[scattered_in])
-    flow.start("in", over_copies(scattered_in))
+    flow.meet([gain_one], "cross", "out", "early")
     late = [gain_one[0], shift_one[0], q_one[0], v_one[0], out_one[0]]
     flow.start("late", sum_everywhere(jnp.concatenate(late)))
     output = mlp_out(
         scalars, active, x_two, part(vectors[2], 1), held_out, deps=flow.take()
     )
-    (scattered_one,) = flow.meet([output], "cross", "in", "early", "late", more=[scattered_one])
+    scattered_one, scattered_in = flow.meet(
+        [output], "cross", "early", "late", more=[scattered_one, scattered_in]
+    )
+    summed_in = lax.psum(scattered_in, "rep")
     flow.start("self", over_copies(scattered_one[0]))
     while flow.active:
         flow.meet(flow.take(), *flow.active)
@@ -1135,7 +1137,7 @@
         own(late[D:]),
         *join_heads([done["cross"]], factor),
         own(early[base + D :]),
-        done["in"].astype(F32) * factor,
+        summed_in.astype(F32) * factor,
         done["out"].astype(F32) * factor,
         own(early[D:base]),
     )

time: 782 us -> 775 us (level)
    ppermute x36 -> x33, waiting for transfers between devices: 125 us -> 86.5 us  [swap(): return lax.ppermute(value, axis, [(i, i ^ bit) for i in range(size)])]
    psum x0 -> x1, waiting for transfers between devices: none -> 29.2 us  [ring_device(): summed_in = lax.psum(scattered_in, 'rep')]
    reduce_scatter x3, waiting for transfers between devices: 3.8 us -> 12.9 us  [scattered(): return lax.psum_scatter(value, 'shard', scatter_dimension=0, tiled=True)]
    convert_element_type x12 -> x10, other arithmetic: 22 us -> 18 us  [add(): return (left.astype(F32) + right.astype(F32)).astype(BF16)]
    unnamed x218 -> x198, local copies, waits for them, and re-layouts: 25.5 us -> 24 us
    ppermute x36 -> x33, starting transfers between devices: 38.2 us -> 37.1 us  [swap(): return lax.ppermute(value, axis, [(i, i ^ bit) for i in range(size)])]
  transfers between devices with their start and end apart: 43 -> 41, of which waited for: 14 -> 13; matrix products, arithmetic and copies ran while one was open for 8% -> 7% of each run, Pallas kernels for 53% -> 53%
where the time goes in v4:
time: 775 us; the launch traced here: 770 us
  Pallas kernels  407 us (53%)
  waiting for transfers between devices  186 us (24%)
  other arithmetic  47.5 us (6%)
  blocking collectives  39 us (5%)
  starting transfers between devices  37.6 us (5%)
  local copies, waits for them, and re-layouts  36.4 us (5%)
  between operations  16.2 us (2%)
    pallas_call x2, Pallas kernels, attend_backward(): pl.pallas_call(skipping(functools.partial(attend_backward_body, cross, wi...  110 us
    pallas_call x2, Pallas kernels, attend_forward(): pl.pallas_call(skipping(functools.partial(attend_forward_body, cross, lay...  92.5 us
    ppermute x33, waiting for transfers between devices, swap(): return lax.ppermute(value, axis, [(i, i ^ bit) for i in range(size)])  86.5 us
    pallas_call x1, Pallas kernels, mlp_down(): pl.pallas_call(skipping(functools.partial(mlp_down_body, layout, below[0]...  73.6 us
    all_gather x4, waiting for transfers between devices, gather(): return lax.all_gather(value, 'shard', axis=0, tiled=True)  56.2 us
    pallas_call x1, Pallas kernels, mlp_up(): pl.pallas_call(skipping(mlp_up_body, 0, len(deps)), grid=(ff // TILE,), i...  49.1 us
    pallas_call x2, Pallas kernels, project_back(): pl.pallas_call(skipping(functools.partial(project_back_body, layout, belo...  44.6 us
    all_gather x1, blocking collectives, gather_vectors(): every = lax.all_gather(packed, 'shard').astype(F32)  39 us
  transfers between devices with their start and end apart: 41, of which 13 were waited for; matrix products, arithmetic and copies ran while one was open for 7% of the time, Pallas kernels for 53%

profile of v4, /device:TPU:0, one launch (start us, length us, event | category | flops | bytes accessed | tf_op | source)
XLA Modules:
  0.0 769.7 jit_solution(16102670771446016650)
XLA Ops:
  7.2 2.3 pad_maximum_fusion
  13.9 3.0 collective-permute-start
  18.5 39.0 %all-gather.1 = bf16[8,1,2688]{2,1,0:T(2,128)(2,1)S(1)} all-gather(bf16[1,1,2688]{2,1,0:T(2,128)(2,1)S(1)} %reshape.90), channel_id=2, replica_groups=mesh['rep'=4,'shard'=8] {'shard'}, dimensions={0}, use_global_device_ids=true | all-gather | bytes 48384 | tf_op jit(solution)/shard_map/all_gather | solution.py:836
  58.5 3.9 copy.72
  65.0 6.9 prepare.1
  74.7 1.9 slice.145.refs_3_
  76.5 1.9 slice.146.refs_4_
  79.1 44.8 %self_forward.1 = (f32[1024,1024]{1,0:T(8,128)}, bf16[1024,1024]{1,0:T(8,128)(2,1)}, bf16[1024,1024]{1,0:T(8,128)(2,1)}, bf16[1024,1024]{1,0:T(8,128)(2,1)}, bf1...) custom-call(s32[2]{0:T(128)} %pad_add_fusion.refs_0_, ...), custom_call_target="tpu_custom_call" | custom-call | flops 25769803776 | bytes 30000000 | tf_op jit(solution)/shard_map/self_forward/pallas_call | solution.py:269
  123.8 11.5 %all-gather.9.cloned.1.call-done.refs_9_.refs_18_.refs_8_ = bf16[1024,4096]{1,0:T(8,128)(2,1)} async-done(((bf16[128,4096]{1,0:T(8,128)(2,1)}), bf16[1024,4096]{1,0:T(8,128)(2,1)}) %all-gather.9.cloned.1.call-update) | async-done | bytes 8388624 | tf_op jit(solution)/shard_map/all_gather | solution.py:1001
  135.4 47.8 %cross_forward.1 = (f32[1024,1024]{1,0:T(8,128)}, bf16[1024,1024]{1,0:T(8,128)(2,1)}, bf16[1024,1024]{1,0:T(8,128)(2,1)}, bf16[1024,1024]{1,0:T(8,128)(2,1)}, bf...) custom-call(s32[2]{0:T(128)} %pad_add_fusion.refs_0_, ...), custom_call_target="tpu_custom_call" | custom-call | flops 25769803776 | bytes 30000000 | tf_op jit(solution)/shard_map/cross_forward/pallas_call | solution.py:269
  183.1 44.0 %all-gather.11.cloned.1.call-done.refs_2_.refs_4_ = bf16[1024,8192]{1,0:T(8,128)(2,1)} async-done(((bf16[128,8192]{1,0:T(8,128)(2,1)}), bf16[1024,8192]{1,0:T(8,128)(2,1)}) %all-gather.11.cloned.1.call-update) | async-done | bytes 16777232 | tf_op jit(solution)/shard_map/all_gather | solution.py:1001
  227.2 49.1 %mlp_up.1 = (bf16[1024,8192]{1,0:T(8,128)(2,1)}, bf16[1024,8192]{1,0:T(8,128)(2,1)}, bf16[8192,1024]{1,0:T(8,128)(2,1)}) custom-call(bf16[1024,1024]{1,0:T(8,128)(2,1)} %get-tuple-element.110.refs_0_, bf16[1024,1024]{1,0:T(8,128)(2,1)} %refs_2_.1, bf16[1024,8192]{1,0:T(8,128)(2,1)} %all-gather.11.cloned.1.call-done.refs_2_.refs_4_, f32[1,8192]{1,0:T(1,128)} %slice.199.refs_3_), custom_call_target="tpu_custom_call" | custom-call | flops 34359738368 | bytes 60000000 | tf_op jit(solution)/shard_map/mlp_up/pallas_call | solution.py:626
  280.4 12.7 %collective-permute-done.2.__0_ = bf16[256,1024]{1,0:T(8,128)(2,1)S(1)} collective-permute-done((bf16[256,1024]{1,0:T(8,128)(2,1)}, bf16[256,1024]{1,0:T(8,128)(2,1)S(1)}, u32[]{:S(2)}, u32[]{:S(2)}) %collective-permute-start.2) | collective-permute-done | bytes 524320 | tf_op jit(solution)/shard_map/ppermute | solution.py:873
  295.4 2.0 collective-permute-done.7.__0_
  299.7 73.6 %mlp_down.1 = (bf16[1024,8192]{1,0:T(8,128)(2,1)}, f32[1,8192]{1,0:T(1,128)}, f32[1024,1024]{1,0:T(8,128)}, bf16[1024,1024]{1,0:T(8,128)(2,1)}, bf16[1024,1024]{...) custom-call(s32[2]{0:T(128)} %pad_add_fusion.refs_0_, ...), custom_call_target="tpu_custom_call" | custom-call | flops 51539607552 | bytes 60000000 | tf_op jit(solution)/shard_map/mlp_down/pallas_call | solution.py:720
  373.4 61.2 %cross_backward.1 = (bf16[1024,3072]{1,0:T(8,128)(2,1)}, bf16[4,128,4096]{2,1,0:T(8,128)(2,1)}, bf16[4,128,4096]{2,1,0:T(8,128)(2,1)}, f32[1,1024]{1,0:T(1,128)}, f32[1,1024]{1,0:T(1,128)}) custom-call(s32[2]{0:T(128)} %pad_add_fusion.refs_0_, bf16[1024,1024]{1,0:T(8,128)(2,1)} %get-tuple-element.106.refs_1_, bf16[1024,1024]{1,0:T(8,128)(2,1)} %bitcast.71, ...), custom_call_target="tpu_custom_call" | custom-call | flops 45097156608 | bytes 20000000 | tf_op jit(solution)/shard_map/cross_backward/pallas_call | solution.py:465
  435.0 2.1 convert_reduce_fusion
  437.2 1.7 broadcast_select_fusion.2.refs_2_
  438.9 1.8 collective-permute-start.10
  440.7 24.8 %cross_project.1 = (f32[1024,1024]{1,0:T(8,128)}, f32[1,1024]{1,0:T(1,128)}, f32[1,1024]{1,0:T(1,128)}, bf16[1024,1024]{1,0:T(8,128)(2,1)}, f32[1,1024]{1,0:T(1,...) custom-call(s32[2]{0:T(128)} %pad_add_fusion.refs_0_, bf16[1024,1024]{1,0:T(8,128)(2,1)} %tie.15.refs_1_, ...), custom_call_target="tpu_custom_call" | custom-call | flops 8589934592 | bytes 30000000 | tf_op jit(solution)/shard_map/cross_project/pallas_call | solution.py:585
  467.5 5.3 add_convert_fusion
  472.9 1.9 copy-done.1
  478.0 3.0 add_convert_fusion.4.refs_5_
  481.0 2.4 collective-permute-start.13
  486.1 49.2 %self_backward.1 = (bf16[1024,3072]{1,0:T(8,128)(2,1)}, bf16[8,128,4096]{2,1,0:T(8,128)(2,1)}, f32[1,1024]{1,0:T(1,128)}, f32[1,1024]{1,0:T(1,128)}) custom-call(s32[2]{0:T(128)} %pad_add_fusion.refs_0_, bf16[4,128,4096]{2,1,0:T(8,128)(2,1)} %get-tuple-element.135.refs_1_, bf16[2,128,2048]{2,1,0:T(8,128)(2,1)} %slice.165.refs_2_, ...), custom_call_target="tpu_custom_call" | custom-call | flops 45097156608 | bytes 20000000 | tf_op jit(solution)/shard_map/self_backward/pallas_call | solution.py:465
  538.1 1.6 add_convert_fusion.1.refs_7_
  540.4 2.1 add_convert_fusion.2
  542.6 1.6 collective-permute-start.16
  544.2 1.6 add_convert_fusion.3
  547.4 19.8 %self_project.1 = (bf16[1024,1024]{1,0:T(8,128)(2,1)}, f32[1,1024]{1,0:T(1,128)}, f32[1,1024]{1,0:T(1,128)}) custom-call(s32[2]{0:T(128)} %pad_add_fusion.refs_0_, bf16[8,128,4096]{2,1,0:T(8,128)(2,1)} %get-tuple-element.155.refs_1_, bf16[2,128,2048]{2,1,0:T(8,128)(2,1)} %get-tuple-element.151.refs_2_, bf16[2,128,2048]{2,1,0:T(8,128)(2,1)} %get-tuple-element.152.refs_3_, ...), custom_call_target="tpu_custom_call" | custom-call | flops 6442450944 | bytes 30000000 | tf_op jit(solution)/shard_map/self_project/pallas_call | solution.py:585
  570.3 1.8 fusion.1
  575.6 25.0 %mlp_out.1.__5_ = bf16[1024,1024]{1,0:T(8,128)(2,1)} custom-call(s32[2]{0:T(128)} %pad_add_fusion.refs_0_, bf16[128,2048]{1,0:T(8,128)(2,1)} %get-tuple-element.159.refs_1_, bf16[128,2048]{1,0:T(8,128)(2,1)} %get-tuple-element.160.refs_2_, bf16[64,4096]{1,0:T(8,128)(2,1)} %broadcast_select_fusion.7.refs_3_, bf16[512,1024]{1,0:T(8,128)(2,1)} %get-tuple-element.161.refs_4_, ...), custom_call_target="tpu_custom_call" | custom-call | flops 17179869184 | bytes 40000000 | tf_op jit(solution)/shard_map/mlp_out/pallas_call | solution.py:784
  600.7 12.8 %reduce-scatter.6.cloned.1.call-done.__0_ = bf16[1,128,4096]{2,1,0:T(8,128)(2,1)} async-done(((bf16[8,128,4096]{2,1,0:T(8,128)(2,1)}), bf16[1,128,4096]{2,1,0:T(8,128)(2,1)}) %reduce-scatter.6.cloned.1.call-update) | async-done | bytes 1048592 | tf_op jit(solution)/shard_map/reduce_scatter | solution.py:1005
  613.6 2.1 select_bitcast_fusion.__12_
  618.5 2.5 collective-permute-start.22
  623.0 2.4 collective-permute-done.24.__2_
  625.4 15.9 %collective-permute-done.23.__1_ = f32[16384]{0:T(1024)S(1)} collective-permute-done((f32[16384]{0:T(1024)S(1)}, f32[16384]{0:T(1024)S(1)}, u32[]{:S(2)}, u32[]{:S(2)}) %collective-permute-start.23) | collective-permute-done | bytes 65568 | tf_op jit(solution)/shard_map/ppermute | solution.py:873
  641.3 2.8 collective-permute-done.22.__0_
  648.4 2.2 collective-permute-start.26
  653.7 2.6 convert_multiply_fusion
  656.4 35.9 %collective-permute-done.27.__1_ = f32[16384]{0:T(1024)S(1)} collective-permute-done((f32[16384]{0:T(1024)S(1)}, f32[16384]{0:T(1024)S(1)}, u32[]{:S(2)}, u32[]{:S(2)}) %collective-permute-start.27) | collective-permute-done | bytes 65568 | tf_op jit(solution)/shard_map/ppermute | solution.py:873
  696.2 2.8 collective-permute-start.31
  701.7 2.7 join_heads.3
  704.4 13.3 %collective-permute-done.30.__0_ = f32[5120]{0:T(1024)S(1)} collective-permute-done((f32[5120]{0:T(1024)S(1)}, f32[5120]{0:T(1024)S(1)}, u32[]{:S(2)}, u32[]{:S(2)}) %collective-permute-start.30) | collective-permute-done | bytes 20512 | tf_op jit(solution)/shard_map/ppermute | solution.py:873
  719.8 1.8 collective-permute-start.32
  724.0 2.7 join_heads.2
  729.3 29.2 %all-reduce.2.cloned.1.call-done = bf16[128,8192]{1,0:T(8,128)(2,1)} async-done(((bf16[128,8192]{1,0:T(8,128)(2,1)}), bf16[128,8192]{1,0:T(8,128)(2,1)}) %all-reduce.2.cloned.1.call-update) | async-done | bytes 2097168 | tf_op jit(solution)/shard_map/psum | solution.py:1118
  758.5 4.1 convert_multiply_fusion.1
  (329 shorter events, 66.8 us)
Async XLA Ops:
  7.2 71.9 %all-gather.7.cloned.1.call-start = ((), (), s32[]{:S(2)}) async-start(), calls=%async_computation.3 | async-start | bytes 9437184 | tf_op jit(solution)/shard_map/all_gather | solution.py:1001
  9.6 125.8 %all-gather.9.cloned.1.call-start = ((), (), s32[]{:S(2)}) async-start(), calls=%async_computation.4 | async-start | bytes 9437184 | tf_op jit(solution)/shard_map/all_gather | solution.py:1001
  10.8 216.4 %all-gather.11.cloned.1.call-start = ((), (), s32[]{:S(2)}) async-start(), calls=%async_computation.5 | async-start | bytes 18874368 | tf_op jit(solution)/shard_map/all_gather | solution.py:1001
  11.5 45.9 %copy-start.76 = (s32[1024]{0:T(1024)S(1)}, s32[1024]{0:T(1024)}, u32[]{:S(2)}) copy-start(s32[1024]{0:T(1024)} %param.17) | copy-start | bytes 12292
  11.6 288.2 %all-gather.13.cloned.1.call-start = ((), (), s32[]{:S(2)}) async-start(), calls=%async_computation.6 | async-start | bytes 9437184 | tf_op jit(solution)/shard_map/all_gather | solution.py:1001
  13.8 423.3 %reduce-scatter.4.cloned.1.call-start = ((), (), s32[]{:S(2)}) async-start(), calls=%async_computation.7 | async-start | bytes 18874368 | tf_op jit(solution)/shard_map/reduce_scatter | solution.py:1005
  13.9 59.8 %collective-permute-start = (bf16[512,1024]{1,0:T(8,128)(2,1)}, bf16[512,1024]{1,0:T(8,128)(2,1)S(1)}, u32[]{:S(2)}, u32[]{:S(2)}) collective-permute-start(bf16[512,1024]{1,0:T(8,128)(2,1)} %get-tuple-element.192.refs_5_.refs_8_.refs_12_), channel_id=1, source_target_pairs={{0,2},{1,3},{2,0},{3,1},{4,6},{5,7},{6,4},{7,5},{8,10},{9,11},{10,... | collective-permute-start | bytes 3145736 | tf_op jit(solution)/shard_map/ppermute | solution.py:873
  16.9 56.8 %collective-permute-start.1 = (bf16[512,1024]{1,0:T(8,128)(2,1)}, bf16[512,1024]{1,0:T(8,128)(2,1)}, u32[]{:S(2)}, u32[]{:S(2)}) collective-permute-start(bf16[512,1024]{1,0:T(8,128)(2,1)} %get-tuple-element.192.refs_5_.refs_8_.refs_12_), channel_id=1, source_target_pairs={{0,4},{1,5},{2,6},{3,7},{4,0},{5,1},{6,2},{7,3},{8,12},{9,13},{10,... | collective-permute-start | bytes 3145736 | tf_op jit(solution)/shard_map/ppermute | solution.py:873
  276.3 324.3 %reduce-scatter.8.cloned.1.call-start = ((), (), s32[]{:S(2)}) async-start(), calls=%async_computation.9 | async-start | bytes 18874368 | tf_op jit(solution)/shard_map/reduce_scatter | solution.py:1005
  277.5 2.9 collective-permute-start.4
  277.9 15.2 %collective-permute-start.5 = (bf16[512,1024]{1,0:T(8,128)(2,1)S(1)}, bf16[512,1024]{1,0:T(8,128)(2,1)S(1)}, u32[]{:S(2)}, u32[]{:S(2)}) collective-permute-start(bf16[512,1024]{1,0:T(8,128)(2,1)S(1)} %copy-done.29), channel_id=1, source_target_pairs={{0,1},{1,0},{2,3},{3,2},{4,5},{5,4},{6,7},{7,6},{8,9},{9,8},{10,11... | collective-permute-start | bytes 3145736 | tf_op jit(solution)/shard_map/ppermute | solution.py:873
  278.2 16.7 %collective-permute-start.6 = (bf16[512,1024]{1,0:T(8,128)(2,1)}, bf16[512,1024]{1,0:T(8,128)(2,1)}, u32[]{:S(2)}, u32[]{:S(2)}) collective-permute-start(bf16[512,1024]{1,0:T(8,128)(2,1)} %get-tuple-element.103.refs_2_.refs_7_.refs_10_.refs_14_), channel_id=1, source_target_pairs={{0,1},{1,0},{2,3},{3,2},{4,5},{5,4},{6,7},{7,6},{8,9},{9,8},{10,11... | collective-permute-start | bytes 3145736 | tf_op jit(solution)/shard_map/ppermute | solution.py:873
  278.4 14.7 %collective-permute-start.2 = (bf16[256,1024]{1,0:T(8,128)(2,1)}, bf16[256,1024]{1,0:T(8,128)(2,1)S(1)}, u32[]{:S(2)}, u32[]{:S(2)}) collective-permute-start(bf16[256,1024]{1,0:T(8,128)(2,1)} %slice.145.refs_3_), channel_id=1, source_target_pairs={{0,4},{1,5},{2,6},{3,7},{4,0},{5,1},{6,2},{7,3},{8,12},{9,13},{10,... | collective-permute-start | bytes 1572872 | tf_op jit(solution)/shard_map/ppermute | solution.py:873
  279.2 14.0 %collective-permute-start.3 = (bf16[256,1024]{1,0:T(8,128)(2,1)}, bf16[256,1024]{1,0:T(8,128)(2,1)S(1)}, u32[]{:S(2)}, u32[]{:S(2)}) collective-permute-start(bf16[256,1024]{1,0:T(8,128)(2,1)} %slice.146.refs_4_), channel_id=1, source_target_pairs={{0,2},{1,3},{2,0},{3,1},{4,6},{5,7},{6,4},{7,5},{8,10},{9,11},{10,... | collective-permute-start | bytes 1572872 | tf_op jit(solution)/shard_map/ppermute | solution.py:873
  294.9 2.5 collective-permute-start.7
  294.9 4.0 collective-permute-start.8
  373.4 240.2 %reduce-scatter.6.cloned.1.call-start = ((), (), s32[]{:S(2)}) async-start(), calls=%async_computation.8 | async-start | bytes 9437184 | tf_op jit(solution)/shard_map/reduce_scatter | solution.py:1005
  434.6 32.3 %collective-permute-start.9 = (bf16[4,128,4096]{2,1,0:T(8,128)(2,1)}, bf16[4,128,4096]{2,1,0:T(8,128)(2,1)}, u32[]{:S(2)}, u32[]{:S(2)}) collective-permute-start(bf16[4,128,4096]{2,1,0:T(8,128)(2,1)} %get-tuple-element.129.refs_3_), channel_id=1, source_target_pairs={{0,1},{1,0},{2,3},{3,2},{4,5},{5,4},{6,7},{7,6},{8,9},{9,8},{10,11... | collective-permute-start | bytes 12582920 | tf_op jit(solution)/shard_map/ppermute | solution.py:873
  438.9 28.1 %collective-permute-start.10 = (bf16[512,1024]{1,0:T(8,128)(2,1)S(1)}, bf16[512,1024]{1,0:T(8,128)(2,1)}, u32[]{:S(2)}, u32[]{:S(2)}) collective-permute-start(bf16[512,1024]{1,0:T(8,128)(2,1)S(1)} %broadcast_select_fusion.2.refs_2_), channel_id=1, source_target_pairs={{0,8},{8,0},{16,24},{24,16},{1,9},{9,1},{17,25},{25,17},{2,10},{10... | collective-permute-start | bytes 3145736 | tf_op jit(solution)/shard_map/ppermute | solution.py:873
  440.7 26.2 %copy-start.77 = (f32[1,1024]{1,0:T(1,128)S(1)}, f32[1,1024]{1,0:T(1,128)}, u32[]{:S(2)}) copy-start(f32[1,1024]{1,0:T(1,128)} %get-tuple-element.131.__1_) | copy-start | bytes 12292
  440.7 26.2 %copy-start.81 = (f32[1,1024]{1,0:T(1,128)S(1)}, f32[1,1024]{1,0:T(1,128)}, u32[]{:S(2)}) copy-start(f32[1,1024]{1,0:T(1,128)} %get-tuple-element.142) | copy-start | bytes 12292
  466.9 68.4 %collective-permute-start.14 = (f32[16384]{0:T(1024)S(1)}, f32[16384]{0:T(1024)S(1)}, u32[]{:S(2)}, u32[]{:S(2)}) collective-permute-start(f32[16384]{0:T(1024)S(1)} %constant_dynamic-update-slice_fusion.8.refs_6_), channel_id=1, source_target_pairs={{0,1},{1,0},{2,3},{3,2},{4,5},{5,4},{6,7},{7,6},{8,9},{9,8},{10,11... | collective-permute-start | bytes 196616 | tf_op jit(solution)/shard_map/ppermute | solution.py:873
  481.0 54.4 %collective-permute-start.13 = (bf16[512,1024]{1,0:T(8,128)(2,1)}, bf16[512,1024]{1,0:T(8,128)(2,1)S(1)}, u32[]{:S(2)}, u32[]{:S(2)}) collective-permute-start(bf16[512,1024]{1,0:T(8,128)(2,1)} %add_convert_fusion.4.refs_5_), channel_id=1, source_target_pairs={{0,16},{8,24},{16,0},{24,8},{1,17},{9,25},{17,1},{25,9},{2,18},{10... | collective-permute-start | bytes 3145736 | tf_op jit(solution)/shard_map/ppermute | solution.py:873
  483.4 52.0 %collective-permute-start.11 = (bf16[2,128,2048]{2,1,0:T(8,128)(2,1)}, bf16[2,128,2048]{2,1,0:T(8,128)(2,1)}, u32[]{:S(2)}, u32[]{:S(2)}) collective-permute-start(bf16[2,128,2048]{2,1,0:T(8,128)(2,1)} %slice.165.refs_2_), channel_id=1, source_target_pairs={{0,2},{1,3},{2,0},{3,1},{4,6},{5,7},{6,4},{7,5},{8,10},{9,11},{10,... | collective-permute-start | bytes 3145736 | tf_op jit(solution)/shard_map/ppermute | solution.py:873
  484.8 50.5 %collective-permute-start.12 = (bf16[2,128,2048]{2,1,0:T(8,128)(2,1)}, bf16[2,128,2048]{2,1,0:T(8,128)(2,1)}, u32[]{:S(2)}, u32[]{:S(2)}) collective-permute-start(bf16[2,128,2048]{2,1,0:T(8,128)(2,1)} %slice.203.refs_3_), channel_id=1, source_target_pairs={{0,4},{1,5},{2,6},{3,7},{4,0},{5,1},{6,2},{7,3},{8,12},{9,13},{10,... | collective-permute-start | bytes 3145736 | tf_op jit(solution)/shard_map/ppermute | solution.py:873
  537.2 31.6 %collective-permute-start.18 = (f32[16384]{0:T(1024)S(1)}, f32[16384]{0:T(1024)S(1)}, u32[]{:S(2)}, u32[]{:S(2)}) collective-permute-start(f32[16384]{0:T(1024)S(1)} %add.95.refs_9_), channel_id=1, source_target_pairs={{0,2},{1,3},{2,0},{3,1},{4,6},{5,7},{6,4},{7,5},{8,10},{9,11},{10,... | collective-permute-start | bytes 196616 | tf_op jit(solution)/shard_map/ppermute | solution.py:873
  539.7 29.1 %collective-permute-start.17 = (bf16[512,1024]{1,0:T(8,128)(2,1)S(1)}, bf16[512,1024]{1,0:T(8,128)(2,1)}, u32[]{:S(2)}, u32[]{:S(2)}) collective-permute-start(bf16[512,1024]{1,0:T(8,128)(2,1)S(1)} %add_convert_fusion.1.refs_7_), channel_id=1, source_target_pairs={{0,8},{8,0},{16,24},{24,16},{1,9},{9,1},{17,25},{25,17},{2,10},{10... | collective-permute-start | bytes 3145736 | tf_op jit(solution)/shard_map/ppermute | solution.py:873
  542.6 26.2 %collective-permute-start.16 = (bf16[128,2048]{1,0:T(8,128)(2,1)S(1)}, bf16[128,2048]{1,0:T(8,128)(2,1)}, u32[]{:S(2)}, u32[]{:S(2)}) collective-permute-start(bf16[128,2048]{1,0:T(8,128)(2,1)S(1)} %slice_bitcast_fusion.2.refs_5_), channel_id=1, source_target_pairs={{0,2},{1,3},{2,0},{3,1},{4,6},{5,7},{6,4},{7,5},{8,10},{9,11},{10,... | collective-permute-start | bytes 1572872 | tf_op jit(solution)/shard_map/ppermute | solution.py:873
  547.0 21.9 %collective-permute-start.15 = (bf16[128,2048]{1,0:T(8,128)(2,1)}, bf16[128,2048]{1,0:T(8,128)(2,1)}, u32[]{:S(2)}, u32[]{:S(2)}) collective-permute-start(bf16[128,2048]{1,0:T(8,128)(2,1)} %slice_bitcast_fusion.3.refs_4_), channel_id=1, source_target_pairs={{0,4},{1,5},{2,6},{3,7},{4,0},{5,1},{6,2},{7,3},{8,12},{9,13},{10,... | collective-permute-start | bytes 1572872 | tf_op jit(solution)/shard_map/ppermute | solution.py:873
  568.7 32.0 %collective-permute-start.21 = (f32[5120]{0:T(1024)S(1)}, f32[5120]{0:T(1024)S(1)}, u32[]{:S(2)}, u32[]{:S(2)}) collective-permute-start(f32[5120]{0:T(1024)S(1)} %constant_dynamic-update-slice_fusion.13.refs_7_), channel_id=1, source_target_pairs={{0,1},{1,0},{2,3},{3,2},{4,5},{5,4},{6,7},{7,6},{8,9},{9,8},{10,11... | collective-permute-start | bytes 61448 | tf_op jit(solution)/shard_map/ppermute | solution.py:873
  573.0 27.7 %collective-permute-start.19 = (bf16[64,4096]{1,0:T(8,128)(2,1)}, bf16[64,4096]{1,0:T(8,128)(2,1)S(1)}, u32[]{:S(2)}, u32[]{:S(2)}) collective-permute-start(bf16[64,4096]{1,0:T(8,128)(2,1)} %broadcast_select_fusion.7.refs_3_), channel_id=1, source_target_pairs={{0,8},{8,0},{16,24},{24,16},{1,9},{9,1},{17,25},{25,17},{2,10},{10... | collective-permute-start | bytes 1572872 | tf_op jit(solution)/shard_map/ppermute | solution.py:873
  574.3 26.3 %collective-permute-start.20 = (f32[16384]{0:T(1024)S(1)}, f32[16384]{0:T(1024)S(1)}, u32[]{:S(2)}, u32[]{:S(2)}) collective-permute-start(f32[16384]{0:T(1024)S(1)} %add.98.refs_6_), channel_id=1, source_target_pairs={{0,4},{1,5},{2,6},{3,7},{4,0},{5,1},{6,2},{7,3},{8,12},{9,13},{10,... | collective-permute-start | bytes 196616 | tf_op jit(solution)/shard_map/ppermute | solution.py:873
  615.7 25.6 %collective-permute-start.25 = (bf16[64,4096]{1,0:T(8,128)(2,1)}, bf16[64,4096]{1,0:T(8,128)(2,1)S(1)}, u32[]{:S(2)}, u32[]{:S(2)}) collective-permute-start(bf16[64,4096]{1,0:T(8,128)(2,1)} %select_bitcast_fusion.__12_), channel_id=1, source_target_pairs={{0,8},{8,0},{16,24},{24,16},{1,9},{9,1},{17,25},{25,17},{2,10},{10... | collective-permute-start | bytes 1572872 | tf_op jit(solution)/shard_map/ppermute | solution.py:873
  618.5 25.6 %collective-permute-start.22 = (bf16[64,4096]{1,0:T(8,128)(2,1)S(1)}, bf16[64,4096]{1,0:T(8,128)(2,1)S(1)}, u32[]{:S(2)}, u32[]{:S(2)}) collective-permute-start(bf16[64,4096]{1,0:T(8,128)(2,1)S(1)} %add_convert_fusion.7.__7_), channel_id=1, source_target_pairs={{0,16},{8,24},{16,0},{24,8},{1,17},{9,25},{17,1},{25,9},{2,18},{10... | collective-permute-start | bytes 1572872 | tf_op jit(solution)/shard_map/ppermute | solution.py:873
  621.0 20.3 %collective-permute-start.23 = (f32[16384]{0:T(1024)S(1)}, f32[16384]{0:T(1024)S(1)}, u32[]{:S(2)}, u32[]{:S(2)}) collective-permute-start(f32[16384]{0:T(1024)S(1)} %add.101.__9_), channel_id=1, source_target_pairs={{0,8},{8,0},{16,24},{24,16},{1,9},{9,1},{17,25},{25,17},{2,10},{10... | collective-permute-start | bytes 196616 | tf_op jit(solution)/shard_map/ppermute | solution.py:873
  621.6 3.8 collective-permute-start.24
  644.9 113.6 %all-reduce.2.cloned.1.call-start = ((), (), s32[]{:S(2)}) async-start(), calls=%async_computation.10 | async-start | bytes 4194304 | tf_op jit(solution)/shard_map/psum | solution.py:1118
  647.3 45.0 %collective-permute-start.29 = (bf16[64,4096]{1,0:T(8,128)(2,1)S(1)}, bf16[64,4096]{1,0:T(8,128)(2,1)S(1)}, u32[]{:S(2)}, u32[]{:S(2)}) collective-permute-start(bf16[64,4096]{1,0:T(8,128)(2,1)S(1)} %fusion.__11_), channel_id=1, source_target_pairs={{0,16},{8,24},{16,0},{24,8},{1,17},{9,25},{17,1},{25,9},{2,18},{10... | collective-permute-start | bytes 1572872 | tf_op jit(solution)/shard_map/ppermute | solution.py:873
  648.4 44.0 %collective-permute-start.26 = (bf16[64,4096]{1,0:T(8,128)(2,1)S(1)}, bf16[64,4096]{1,0:T(8,128)(2,1)S(1)}, u32[]{:S(2)}, u32[]{:S(2)}) collective-permute-start(bf16[64,4096]{1,0:T(8,128)(2,1)S(1)} %add_convert_fusion.6.__5_), channel_id=1, source_target_pairs={{0,8},{8,0},{16,24},{24,16},{1,9},{9,1},{17,25},{25,17},{2,10},{10... | collective-permute-start | bytes 1572872 | tf_op jit(solution)/shard_map/ppermute | solution.py:873
  652.0 4.4 collective-permute-start.28
  653.5 38.8 %collective-permute-start.27 = (f32[16384]{0:T(1024)S(1)}, f32[16384]{0:T(1024)S(1)}, u32[]{:S(2)}, u32[]{:S(2)}) collective-permute-start(f32[16384]{0:T(1024)S(1)} %add.104.__7_), channel_id=1, source_target_pairs={{0,16},{8,24},{16,0},{24,8},{1,17},{9,25},{17,1},{25,9},{2,18},{10... | collective-permute-start | bytes 196616 | tf_op jit(solution)/shard_map/ppermute | solution.py:873
  656.4 37.6 %copy-start.47 = (f32[16384]{0:T(1024)S(1)}, f32[16384]{0:T(1024)}, u32[]{:S(2)}) copy-start(f32[16384]{0:T(1024)} %copy-done.46) | copy-start | bytes 196612
  656.4 38.6 %copy-start.18 = (bf16[64,4096]{1,0:T(8,128)(2,1)S(1)}, bf16[64,4096]{1,0:T(8,128)(2,1)}, u32[]{:S(2)}) copy-start(bf16[64,4096]{1,0:T(8,128)(2,1)} %copy-done.17) | copy-start | bytes 1572868
  656.4 39.7 %copy-start.13 = (bf16[64,4096]{1,0:T(8,128)(2,1)S(1)}, bf16[64,4096]{1,0:T(8,128)(2,1)}, u32[]{:S(2)}) copy-start(bf16[64,4096]{1,0:T(8,128)(2,1)} %copy-done.12) | copy-start | bytes 1572868
  656.4 35.9 %copy-start.66 = (f32[5120]{0:T(1024)}, f32[5120]{0:T(1024)S(1)}, u32[]{:S(2)}) copy-start(f32[5120]{0:T(1024)S(1)} %collective-permute-done.28.__2_) | copy-start | bytes 61444
  696.2 21.5 %collective-permute-start.31 = (bf16[64,4096]{1,0:T(8,128)(2,1)S(1)}, bf16[64,4096]{1,0:T(8,128)(2,1)S(1)}, u32[]{:S(2)}, u32[]{:S(2)}) collective-permute-start(bf16[64,4096]{1,0:T(8,128)(2,1)S(1)} %add_convert_fusion.5.__7_), channel_id=1, source_target_pairs={{0,8},{8,0},{16,24},{24,16},{1,9},{9,1},{17,25},{25,17},{2,10},{10... | collective-permute-start | bytes 1572872 | tf_op jit(solution)/shard_map/ppermute | solution.py:873
  699.1 18.6 %collective-permute-start.30 = (f32[5120]{0:T(1024)S(1)}, f32[5120]{0:T(1024)S(1)}, u32[]{:S(2)}, u32[]{:S(2)}) collective-permute-start(f32[5120]{0:T(1024)S(1)} %add.106.__5_), channel_id=1, source_target_pairs={{0,8},{8,0},{16,24},{24,16},{1,9},{9,1},{17,25},{25,17},{2,10},{10... | collective-permute-start | bytes 61448 | tf_op jit(solution)/shard_map/ppermute | solution.py:873
  719.8 6.8 collective-permute-start.32
  (82 other events, 478.9 us)
Sparse Core Ops, SparseCore 0:
  10.5 68.5 all-gather.6
  80.9 54.3 all-gather.8
  137.3 89.8 all-gather.10
  229.5 54.6 all-gather.12
  287.6 116.7 reduce-scatter.3
  407.8 129.5 reduce-scatter.7
  540.9 72.6 reduce-scatter.5
  656.5 102.0 all-reduce.1
